TPU v7x, 32 devices: a whole 2x2x4 slice. The times are simulated.
32 devices in a mesh: runs: 2 (over y), hst: 2 (over core), dom: 8 (over z, x).
Axes of the slice: x: 2, y: 2, z: 4, core: 2. Of those that a mesh axis runs over, the one named last changes fastest.
Arguments:
- features: bfloat16 [49152, 256], P(('runs', 'hst', 'dom')), parts along dimension 0, may hold values from -6 to 6
- aggregated: bfloat16 [49152, 256], P(('runs', 'hst', 'dom')), parts along dimension 0, may hold values from -6 to 6
- cotangent: bfloat16 [49152, 256], P(('runs', 'hst', 'dom')), parts along dimension 0, may hold values from -6 to 6
- w_self: bfloat16 [256, 256], replicated, may hold values from -0.375 to 0.375
- w_neigh: bfloat16 [256, 256], replicated, may hold values from -0.375 to 0.375
- tile_values: bfloat16 [32, 48, 128, 128], P(('runs', 'hst', 'dom')), parts along dimension 0, may hold values from -0.25 to 0.25
- tile_source: int32 [32, 48], P(('runs', 'hst', 'dom')), parts along dimension 0, may hold values from 0 to 11, as said below
- slot_source: int32 [32, 8, 8, 4], P(('runs', 'hst', 'dom')), parts along dimension 0, may hold values from 0 to 1535
- slot_weight: float32 [32, 8, 8, 4], P(('runs', 'hst', 'dom')), parts along dimension 0, may hold values from 0.25 to 1
- send_count: int32 [32, 8], P(('runs', 'hst', 'dom')), parts along dimension 0, may hold values from 0 to 8, as said below
- recv_rows: int32 [32, 8, 8], P(('runs', 'hst', 'dom')), parts along dimension 0, may hold values from 0 to 1535
- stale_grad: bfloat16 [32, 2, 64, 256], P(('runs', 'hst', 'dom')), parts along dimension 0, may hold values from -6 to 6
- version: int32 [32], P(('runs', 'hst', 'dom')), parts along dimension 0, may hold values from 0 to 1
- cross_source: int32 [32, 64, 4], P(('runs', 'hst', 'dom')), parts along dimension 0, may hold values from 0 to 63
- cross_weight: float32 [32, 64, 4], P(('runs', 'hst', 'dom')), parts along dimension 0, may hold values from 0.25 to 1
- cross_count: int32 [32], P(('runs', 'hst', 'dom')), parts along dimension 0, may hold values from 1 to 64, as said below
- cross_rows: int32 [32, 64], P(('runs', 'hst', 'dom')), parts along dimension 0, may hold values from 0 to 1535
Outputs:
- input_grad: bfloat16 [49152, 256], P(('runs', 'hst', 'dom')), parts along dimension 0
- weight_grads: bfloat16 [4, 256, 256], P('runs'), parts along dimension 0
There are 2 independent parts, one for each index of `runs`. A program takes and returns all parts, laid end to end along the dimension named above; an argument that names none is the same for every part. Nothing has to cross between parts.
Inputs may be any that keep to these rules, and one draw needn't show every extreme that they name: `tile_source`: the 4 tiles of one destination block name different source blocks. Slots from index send_count on are padding. A device's own partition gets 0, and every device sends 8 to some other partition. Slots from index cross_count on are padding; some device has 64.
All inputs are finite; a program needn't handle non-finite values.
Results may differ from a plain program's by a relative error of at most 0.0054.
Values may be sent and summed in bfloat16 or wider, within the bound.
No kernel may reach another device: no remote copies, remote signals or barrier semaphores. Data moves between devices by JAX's collectives and lax.ppermute only.
A program may use at most 64 MiB of HBM per device.

v0:
```python
import math

import jax
import jax.numpy as jnp
from jax import lax
from jax.sharding import PartitionSpec as P


def partner(value, axis, distance):
    mask = 2**distance
    pairs = [(source, source ^ mask) for source in range(lax.axis_size(axis))]
    return lax.ppermute(value, axis, pairs)


def silu_slope(preact):
    sigmoid = jax.nn.sigmoid(preact)
    return sigmoid * (1.0 + preact * (1.0 - sigmoid))


def transposed(left, weight):
    return jnp.einsum("rd,ed->re", left, weight, preferred_element_type=jnp.float32)


def stale_path(stale_grad, version, cross_source, cross_weight, cross_count, w_neigh):
    chosen = lax.dynamic_index_in_dim(stale_grad[0], version[0], 0, keepdims=False)
    stale_neigh = transposed(chosen, w_neigh).astype(jnp.bfloat16)
    picked = stale_neigh[cross_source[0]].astype(jnp.float32)
    live_mask = (jnp.arange(cross_source.shape[1]) < cross_count[0]).astype(jnp.float32)
    outgoing = (jnp.sum(picked * cross_weight[0][:, :, None], axis=1) * live_mask[:, None]).astype(
        jnp.bfloat16
    )
    return partner(outgoing, "hst", 0)


def fresh_path(
    pre_grad, w_self, w_neigh, tile_values, tile_source, slot_source, slot_weight, send_count
):
    row_count, feature_dim = pre_grad.shape
    blocks = row_count // 128
    tile_count = tile_values.shape[1]
    per_block = tile_count // blocks
    capacity = slot_source.shape[2]
    neigh_grad = transposed(pre_grad, w_neigh).astype(jnp.bfloat16)
    picked = neigh_grad[slot_source[0]].astype(jnp.float32)
    live_mask = (jnp.arange(capacity)[None, :] < send_count[0][:, None]).astype(jnp.float32)
    outgoing = (
        jnp.sum(picked * slot_weight[0][:, :, :, None], axis=2) * live_mask[:, :, None]
    ).astype(jnp.bfloat16)
    incoming = lax.all_to_all(outgoing, "dom", split_axis=0, concat_axis=0, tiled=True)
    self_term = transposed(pre_grad, w_self)
    tile_block = tile_values[0].reshape(blocks, per_block, 128, 128)
    products = jnp.einsum(
        "btij,bid->btjd",
        tile_block,
        neigh_grad.reshape(blocks, 128, feature_dim),
        preferred_element_type=jnp.float32,
    )
    one_hot = (tile_source[0][:, None] == jnp.arange(blocks)[None, :]).astype(jnp.float32)
    local_term = jnp.einsum(
        "tb,tjd->bjd",
        one_hot,
        products.reshape(tile_count, 128, feature_dim),
        precision=lax.Precision.HIGHEST,
    )
    return (incoming, self_term + local_term.reshape(row_count, feature_dim))


def weight_sums(features, aggregated, pre_grad):
    feature_dim = features.shape[1]
    node_total = features.shape[0] * lax.axis_size("hst") * lax.axis_size("dom")
    grad_scale = 1.0 / math.sqrt(node_total)
    self_part = (
        jnp.einsum("rd,re->de", features, pre_grad, preferred_element_type=jnp.float32) * grad_scale
    )
    neigh_part = (
        jnp.einsum("rd,re->de", aggregated, pre_grad, preferred_element_type=jnp.float32)
        * grad_scale
    )
    stacked = jnp.concatenate([self_part, neigh_part], axis=0)
    shares = lax.psum_scatter(stacked, "dom", scatter_dimension=0, tiled=True)
    shares = lax.psum(shares, "hst")
    summed = lax.all_gather(shares, "dom", axis=0, tiled=True)
    return summed.reshape(2, feature_dim, feature_dim).astype(jnp.bfloat16)


def body(
    features,
    aggregated,
    cotangent,
    w_self,
    w_neigh,
    tile_values,
    tile_source,
    slot_source,
    slot_weight,
    send_count,
    recv_rows,
    stale_grad,
    version,
    cross_source,
    cross_weight,
    cross_count,
    cross_rows,
):
    feature_dim = features.shape[1]
    preact = jnp.dot(features, w_self, preferred_element_type=jnp.float32) + jnp.dot(
        aggregated, w_neigh, preferred_element_type=jnp.float32
    )
    pre_grad = (cotangent.astype(jnp.float32) * silu_slope(preact)).astype(jnp.bfloat16)
    incoming, base_rows = fresh_path(
        pre_grad, w_self, w_neigh, tile_values, tile_source, slot_source, slot_weight, send_count
    )
    stale_in = stale_path(stale_grad, version, cross_source, cross_weight, cross_count, w_neigh)
    accum_rows = base_rows.at[recv_rows[0].reshape(-1)].add(
        incoming.reshape(-1, feature_dim).astype(jnp.float32)
    )
    accum_rows = accum_rows.at[cross_rows[0]].add(stale_in.astype(jnp.float32))
    return (accum_rows.astype(jnp.bfloat16), weight_sums(features, aggregated, pre_grad))


def solution(mesh):
    return jax.shard_map(
        body,
        mesh=mesh,
        in_specs=(
            P(("runs", "hst", "dom"), None),
            P(("runs", "hst", "dom"), None),
            P(("runs", "hst", "dom"), None),
            P(),
            P(),
            P(("runs", "hst", "dom"), None, None, None),
            P(("runs", "hst", "dom"), None),
            P(("runs", "hst", "dom"), None, None, None),
            P(("runs", "hst", "dom"), None, None, None),
            P(("runs", "hst", "dom"), None),
            P(("runs", "hst", "dom"), None, None),
            P(("runs", "hst", "dom"), None, None, None),
            P(("runs", "hst", "dom")),
            P(("runs", "hst", "dom"), None, None),
            P(("runs", "hst", "dom"), None, None),
            P(("runs", "hst", "dom")),
            P(("runs", "hst", "dom"), None),
        ),
        out_specs=(P(("runs", "hst", "dom"), None), P("runs", None, None)),
        check_vma=False,
    )
```

profile of v0, /device:TPU:0, one launch (start us, length us, event | category | flops | bytes accessed | tf_op | source)
XLA Modules:
  0.0 124.1 jit_solution(12371015866241360186)
XLA Ops:
  7.2 0.0 copy-start
  7.2 0.0 copy-start.3
  7.2 0.0 copy-start.1
  7.2 0.0 reduce-scatter.2.cloned.1.call-start
  8.7 0.7 compare_select_fusion.1
  9.4 0.1 copy.29
  9.5 0.1 reshape.179
  9.6 0.8 copy.30
  10.4 1.1 convolution_convert_fusion.1
  11.5 1.2 gather_fusion.1
  12.6 0.1 reshape.204
  12.7 0.0 copy-start.2
  12.7 0.0 copy-start.4
  12.7 0.0 copy-start.10
  12.7 0.2 multiply_reduce_fusion
  13.0 0.7 multiply_convert_fusion.1
  13.7 0.5 collective-permute-start
  14.1 0.0 copy-done.3
  14.1 0.0 copy-done.1
  14.1 0.4 fusion.17
  14.5 0.0 copy-done.2
  14.5 0.0 copy-done.4
  14.5 0.0 copy-done.10
  14.5 0.8 multiply_convert_fusion
  15.3 0.4 fusion.1
  15.8 0.4 fusion
  16.2 0.0 copy-start.9
  16.2 0.0 copy-start.6
  16.2 0.0 copy-start.5
  16.2 0.9 pad_maximum_fusion
  17.1 0.0 reduce-scatter.2.cloned.1.call-update
  17.1 0.4 convolution_convert_fusion
  17.5 0.0 copy-start.7
  17.5 0.0 copy-done.9
  17.5 0.1 fusion.13
  17.6 0.0 copy-done.6
  17.6 0.1 copy.27
  17.8 0.1 reshape.171
  17.9 0.0 copy-done.5
  17.9 0.7 copy.28
  18.6 1.8 %gather_fusion = bf16[256,256]{1,0:T(8,128)(2,1)} fusion(bf16[1536,256]{1,0:T(8,128)(2,1)S(1)} %convolution_convert_fusion, s32[1024]{0:T(1024)S(1)} %pad_clamp_fusion.1), kind=kCustom, calls=%fused_computation | custom fusion | bytes 263168 | tf_op jit(solution)/shard_map/gather | solution.py:44
  20.4 1.0 reshape.203
  21.4 1.0 multiply_reduce_fusion.1
  22.4 0.7 multiply_convert_fusion.2
  23.1 6.9 %all-to-all-start = ((bf16[8,8,256]{2,1,0:T(8,128)(2,1)}), bf16[8,8,256]{2,1,0:T(8,128)(2,1)S(1)}, u32[]{:S(2)}, u32[]{:S(2)}) async-start(bf16[8,8,256]{2,1,0:T(8,128)(2,1)} %multiply_convert_fusion.2), calls=%async_computation | async-start | bytes 65536 | tf_op jit(solution)/shard_map/all_to_all | solution.py:49
  30.0 0.0 copy-done.7
  30.0 0.1 reshape_squeeze.7
  30.0 0.0 copy-done
  30.0 3.7 %fusion.18 = f32[12,256,4,128]{3,1,2,0:T(8,128)} fusion(bf16[12,128,256,1]{2,1,3,0:T(8,128)(2,1)S(1)} %bitcast.71, bf16[12,4,128,128]{3,2,1,0:T(8,128)(2,1)S(1)} %bitcast.69), kind=kOutput, calls=%fused_computation.42 | convolution fusion | flops 402653184 | bytes 8650752 | tf_op jit(solution)/shard_map/btij,bid->btjd/dot_general | solution.py:52
  33.7 6.7 %copy.25 = f32[48,128,256]{2,0,1:T(8,128)} copy(f32[48,128,256]{1,2,0:T(8,128)} %bitcast.70) | data formatting | bytes 12582912 | tf_op jit(solution)/shard_map/reshape | solution.py:62
  40.5 0.0 copy-done.8
  40.5 4.2 %fusion.10 = f32[12,128,256]{2,0,1:T(8,128)S(1)} fusion(f32[48,128,256]{2,0,1:T(8,128)} %copy.25, s32[48]{0:T(128)S(1)} %bitcast.76), kind=kOutput, calls=%fused_computation.28 | convolution fusion | flops 226492992 | bytes 7864512 | tf_op jit(solution)/shard_map/tb,tjd->bjd/dot_general | solution.py:59
  44.7 0.9 copy.26
  45.6 0.0 copy-start.11
  45.7 1.6 %convolution_add_fusion = f32[1536,256]{1,0:T(8,128)} fusion(f32[1536,256]{1,0:T(8,128)S(1)} %bitcast.72, bf16[1536,256]{1,0:T(8,128)(2,1)S(1)} %multiply_convert_fusion, bf16[256,256]{1,0:T(8,128)(2,1)S(1)} %copy-done.3), kind=kOutput, calls=%fused_computation.4 | convolution fusion | flops 201719808 | bytes 4063232 | tf_op jit(solution)/shard_map/rd,ed->re/dot_general | solution.py:21
  47.2 0.0 all-to-all-done
  47.2 3.4 %scatter_custom_fusion = f32[1536,256]{1,0:T(8,128)} fusion(f32[1536,256]{1,0:T(8,128)} %convolution_add_fusion, s32[64]{0:T(128)S(1)} %fusion.14, bf16[8,8,256]{2,1,0:T(8,128)(2,1)S(1)} %all-to-all-done), kind=kCustom, calls=%fused_computation.16 | custom fusion | flops 32768 | bytes 1605632 | tf_op jit(solution)/shard_map/scatter-add | solution.py:114
  50.7 0.0 collective-permute-done
  50.7 3.6 %scatter_custom_fusion.1 = f32[1536,256]{1,0:T(8,128)} fusion(f32[1536,256]{1,0:T(8,128)} %scatter_custom_fusion, s32[64]{0:T(128)S(1)} %fusion.15, bf16[64,256]{1,0:T(8,128)(2,1)} %collective-permute-done), kind=kCustom, calls=%fused_computation.18 | custom fusion | flops 32768 | bytes 1605632 | tf_op jit(solution)/shard_map/scatter-add | solution.py:117
  54.3 2.4 %convert_element_type.70 = bf16[1536,256]{1,0:T(8,128)(2,1)} convert(f32[1536,256]{1,0:T(8,128)} %scatter_custom_fusion.1) | non-fusion elementwise | flops 393216 | bytes 2359296 | tf_op jit(solution)/shard_map/convert_element_type | solution.py:118
  56.7 24.9 %reduce-scatter.2.cloned.1.call-done = f32[64,256]{1,0:T(8,128)} async-done(((f32[512,256]{1,0:T(8,128)}), f32[64,256]{1,0:T(8,128)}) %reduce-scatter.2.cloned.1.call-update) | async-done | bytes 65552 | tf_op jit(solution)/shard_map/reduce_scatter | solution.py:80
  81.6 4.2 %psum.7 = bf16[64,256]{1,0:T(8,128)(2,1)S(1)} all-reduce(f32[64,256]{1,0:T(8,128)} %reduce-scatter.2.cloned.1.call-done), channel_id=1, replica_groups=mesh['runs'=2,'hst'=2,'dom'=8] {'hst'}, use_global_device_ids=true, to_apply=%region_5.6 | all-reduce | flops 16384 | bytes 98304 | tf_op jit(solution)/shard_map/psum | solution.py:81
  85.8 30.7 %all_gather.3 = bf16[512,256]{1,0:T(8,128)(2,1)S(1)} all-gather(bf16[64,256]{1,0:T(8,128)(2,1)S(1)} %psum.7), channel_id=1, replica_groups=mesh['runs'=2,'hst'=2,'dom'=8] {'dom'}, dimensions={0}, use_global_device_ids=true | all-gather | bytes 294912 | tf_op jit(solution)/shard_map/all_gather | solution.py:82
  116.6 0.7 copy.39
  (8 shorter events, 0.0 us)
Async XLA Ops:
  7.2 22.9 %copy-start = (bf16[1,48,128,128]{3,2,1,0:T(8,128)(2,1)S(1)}, bf16[1,48,128,128]{3,2,1,0:T(8,128)(2,1)}, u32[]{:S(2)}) copy-start(bf16[1,48,128,128]{3,2,1,0:T(8,128)(2,1)} %param.22) | copy-start | bytes 4718596
  7.2 6.9 %copy-start.3 = (bf16[256,256]{1,0:T(8,128)(2,1)S(1)}, bf16[256,256]{1,0:T(8,128)(2,1)}, u32[]{:S(2)}) copy-start(bf16[256,256]{1,0:T(8,128)(2,1)} %param.20) | copy-start | bytes 393220
  7.2 6.9 %copy-start.1 = (bf16[1536,256]{1,0:T(8,128)(2,1)S(1)}, bf16[1536,256]{1,0:T(8,128)(2,1)}, u32[]{:S(2)}) copy-start(bf16[1536,256]{1,0:T(8,128)(2,1)} %param.17) | copy-start | bytes 2359300
  7.2 74.4 %reduce-scatter.2.cloned.1.call-start = ((), (), s32[]{:S(2)}) async-start(), calls=%async_computation.2 | async-start | bytes 589824 | tf_op jit(solution)/shard_map/reduce_scatter | solution.py:80
  12.7 1.8 %copy-start.2 = (bf16[1536,256]{1,0:T(8,128)(2,1)S(1)}, bf16[1536,256]{1,0:T(8,128)(2,1)}, u32[]{:S(2)}) copy-start(bf16[1536,256]{1,0:T(8,128)(2,1)} %param.18) | copy-start | bytes 2359300
  12.7 1.8 %copy-start.4 = (bf16[256,256]{1,0:T(8,128)(2,1)S(1)}, bf16[256,256]{1,0:T(8,128)(2,1)}, u32[]{:S(2)}) copy-start(bf16[256,256]{1,0:T(8,128)(2,1)} %param.21) | copy-start | bytes 393220
  12.7 1.8 %copy-start.10 = (bf16[1536,256]{1,0:T(8,128)(2,1)S(1)}, bf16[1536,256]{1,0:T(8,128)(2,1)}, u32[]{:S(2)}) copy-start(bf16[1536,256]{1,0:T(8,128)(2,1)} %param.19) | copy-start | bytes 2359300
  13.7 37.0 %collective-permute-start = (bf16[64,256]{1,0:T(8,128)(2,1)}, bf16[64,256]{1,0:T(8,128)(2,1)}, u32[]{:S(2)}, u32[]{:S(2)}) collective-permute-start(bf16[64,256]{1,0:T(8,128)(2,1)} %multiply_convert_fusion.1), channel_id=1, source_target_pairs={{0,8},{8,0},{1,9},{9,1},{2,10},{10,2},{3,11},{11,3},{4,12},{12,4},... | collective-permute-start | bytes 98312 | tf_op jit(solution)/shard_map/ppermute | solution.py:12
  16.2 1.3 %copy-start.9 = (s32[1,8]{1,0:T(1,128)S(1)}, s32[1,8]{1,0:T(1,128)}, u32[]{:S(2)}) copy-start(s32[1,8]{1,0:T(1,128)} %param.26) | copy-start | bytes 100
  16.2 1.4 %copy-start.6 = (s32[1,8,8,4]{2,3,1,0:T(4,128)S(1)}, s32[1,8,8,4]{2,3,1,0:T(4,128)}, u32[]{:S(2)}) copy-start(s32[1,8,8,4]{2,3,1,0:T(4,128)} %param.24) | copy-start | bytes 3076
  16.2 1.7 %copy-start.5 = (f32[1,8,8,4]{2,3,1,0:T(4,128)S(1)}, f32[1,8,8,4]{2,3,1,0:T(4,128)}, u32[]{:S(2)}) copy-start(f32[1,8,8,4]{2,3,1,0:T(4,128)} %param.25) | copy-start | bytes 3076
  17.5 12.4 %copy-start.7 = (s32[1,8,8]{2,1,0:T(8,128)S(1)}, s32[1,8,8]{2,1,0:T(8,128)}, u32[]{:S(2)}) copy-start(s32[1,8,8]{2,1,0:T(8,128)} %param.27) | copy-start | bytes 772
  23.1 24.2 %all-to-all-start = ((bf16[8,8,256]{2,1,0:T(8,128)(2,1)}), bf16[8,8,256]{2,1,0:T(8,128)(2,1)S(1)}, u32[]{:S(2)}, u32[]{:S(2)}) async-start(bf16[8,8,256]{2,1,0:T(8,128)(2,1)} %multiply_convert_fusion.2), calls=%async_computation | async-start | bytes 65536 | tf_op jit(solution)/shard_map/all_to_all | solution.py:49
  33.7 6.7 %copy-start.8 = (s32[1,48]{1,0:T(1,128)S(1)}, s32[1,48]{1,0:T(1,128)}, u32[]{:S(2)}) copy-start(s32[1,48]{1,0:T(1,128)} %param.23) | copy-start | bytes 580
  45.6 1.6 %copy-start.11 = (s32[1,64]{1,0:T(1,128)S(1)}, s32[1,64]{1,0:T(1,128)}, u32[]{:S(2)}) copy-start(s32[1,64]{1,0:T(1,128)} %param.33) | copy-start | bytes 772
Sparse Core Ops, SparseCore 0:
  17.2 64.3 reduce-scatter.1
where the time goes:
time: 125 us; the launch traced here: 124 us
  blocking collectives  35 us (28%)
  waiting for transfers between devices  24.9 us (20%)
  between operations  15.7 us (13%)
  local copies, waits for them, and re-layouts  14.5 us (12%)
  other arithmetic  13.7 us (11%)
  matrix products  13 us (10%)
  starting transfers between devices  7.36 us (6%)
    all_gather x1, blocking collectives, weight_sums(): summed = lax.all_gather(shares, 'dom', axis=0, tiled=True)  30.7 us
    reduce_scatter x1, waiting for transfers between devices, weight_sums(): shares = lax.psum_scatter(stacked, 'dom', scatter_dimension=0, tiled=True)  24.9 us
    all_to_all x1, starting transfers between devices, fresh_path(): lax.all_to_all(outgoing, 'dom', split_axis=0, concat_axis=0, tiled=True)  6.87 us
    reshape x1, local copies, waits for them, and re-layouts, fresh_path(): products.reshape(tile_count, 128, feature_dim)  6.74 us
    dot_general x1, matrix products, fresh_path(): jnp.einsum('tb,tjd->bjd', one_hot, products.reshape(tile_count, 128, feat...  4.25 us
    psum x1, blocking collectives, weight_sums(): shares = lax.psum(shares, 'hst')  4.22 us
    dot_general x1, matrix products, fresh_path(): jnp.einsum('btij,bid->btjd', tile_block, neigh_grad.reshape(blocks, 128,...  3.68 us
    scatter-add x1, other arithmetic, body(): accum_rows = accum_rows.at[cross_rows[0]].add(stale_in.astype(jnp.float32))  3.64 us
  transfers between devices with their start and end apart: 3, of which 1 were waited for; matrix products, arithmetic and copies ran while one was open for 29% of the time, Pallas kernels for 0%

commit v1 on v0

v1 whole, which is shorter than its diff:
```python
import functools
import math

import jax
import jax.numpy as jnp
from jax import lax
from jax.experimental import pallas as pl
from jax.experimental.pallas import tpu as pltpu
from jax.sharding import PartitionSpec as P

BF16, F32 = jnp.bfloat16, jnp.float32
VMEM = pl.BlockSpec(memory_space=pltpu.VMEM)
SMEM = pl.BlockSpec(memory_space=pltpu.SMEM)
PARAMS = pltpu.CompilerParams(vmem_limit_bytes=40 * 2**20)
NT = (((1,), (1,)), ((), ()))
TN = (((0,), (0,)), ((), ()))


def swap(value, axis, bit):
    pairs = [(source, source ^ (1 << bit)) for source in range(lax.axis_size(axis))]
    return lax.ppermute(value, axis, pairs)


def silu_slope(preact):
    sigmoid = jax.nn.sigmoid(preact)
    return sigmoid * (1.0 + preact * (1.0 - sigmoid))


def bit_reversed(count):
    bits = count.bit_length() - 1
    return [sum(((r >> b) & 1) << (bits - 1 - b) for b in range(bits)) for r in range(count)]


def split_dot(weights, rows):
    high = weights.astype(BF16)
    low = (weights - high.astype(F32)).astype(BF16)
    return jnp.dot(high, rows, preferred_element_type=F32) + jnp.dot(
        low, rows, preferred_element_type=F32
    )


def outgoing_kernel(
    me_ref, count_ref, grad_ref, weight_ref, source_ref, scale_ref, neigh_ref, out_ref
):
    peers, fan, cap = source_ref.shape
    me = me_ref[0]
    neigh = lax.dot_general(grad_ref[...], weight_ref[...], NT, preferred_element_type=F32)
    neigh = neigh.astype(BF16)
    neigh_ref[...] = neigh
    rows = neigh.shape[0]
    order = bit_reversed(peers)
    slot = lax.broadcasted_iota(jnp.int32, (fan, cap), 1)
    group = min(peers, 128 // cap)
    for first in range(0, peers, group):
        sources, scales = [], []
        for r in order[first : first + group]:
            q = jnp.bitwise_xor(me, r)
            live = slot < count_ref[0, q]
            sources.append(source_ref[q])
            scales.append(jnp.where(live, scale_ref[q], 0.0))
        sources = jnp.concatenate(sources, axis=1).T
        scales = jnp.concatenate(scales, axis=1).T
        slots = group * cap
        node = lax.broadcasted_iota(jnp.int32, (slots, rows), 1)
        select = jnp.zeros((slots, rows), F32)
        for k in range(fan):
            select += jnp.where(sources[:, k : k + 1] == node, scales[:, k : k + 1], 0.0)
        out_ref[pl.ds(first * cap, slots), :] = split_dot(select, neigh).astype(BF16)


def stale_kernel(version_ref, count_ref, stale_ref, weight_ref, source_ref, scale_ref, out_ref):
    chosen = stale_ref[version_ref[0]]
    neigh = lax.dot_general(chosen, weight_ref[...], NT, preferred_element_type=F32).astype(BF16)
    fan, slots = source_ref.shape
    slot = lax.broadcasted_iota(jnp.int32, (1, slots), 1)
    live = slot < count_ref[0]
    stored = lax.broadcasted_iota(jnp.int32, (neigh.shape[0], slots), 0)
    select = jnp.zeros(stored.shape, F32)
    for k in range(fan):
        scale = jnp.where(live, scale_ref[pl.ds(k, 1), :], 0.0)
        select += jnp.where(source_ref[pl.ds(k, 1), :] == stored, scale, 0.0)
    out_ref[...] = split_dot(select.T, neigh).astype(BF16)


def local_kernel(source_ref, grad_ref, neigh_ref, weight_ref, tile_ref, base_ref):
    blocks = base_ref.shape[0]
    tiles = tile_ref.shape[0]
    per_block = tiles // blocks
    for b in range(blocks):
        rows = pl.ds(b * 128, 128)
        base_ref[b] = lax.dot_general(
            grad_ref[rows, :], weight_ref[...], NT, preferred_element_type=F32
        )
    for b in range(blocks):
        neigh = neigh_ref[pl.ds(b * 128, 128), :]
        for t in range(b * per_block, (b + 1) * per_block):
            product = lax.dot_general(tile_ref[t], neigh, TN, preferred_element_type=F32)
            base_ref[source_ref[0, t]] += product


def finish_kernel(me_ref, base_ref, fresh_ref, stale_ref, recv_ref, cross_ref, out_ref):
    me = me_ref[0]
    blocks = base_ref.shape[0]
    peers, cap = recv_ref.shape
    targets = [recv_ref[pl.ds(jnp.bitwise_xor(me, o), 1), :] for o in bit_reversed(peers)]
    fresh_rows = jnp.concatenate(targets, axis=1)
    stale_rows = cross_ref[...]
    for b in range(blocks):
        total = base_ref[b]
        for rows, values in ((fresh_rows, fresh_ref), (stale_rows, stale_ref)):
            node = b * 128 + lax.broadcasted_iota(jnp.int32, (128, rows.shape[1]), 0)
            hit = jnp.where(node == rows, 1.0, 0.0).astype(BF16)
            total += jnp.dot(hit, values[...], preferred_element_type=F32)
        out_ref[pl.ds(b * 128, 128), :] = total.astype(BF16)


def body(
    features,
    aggregated,
    cotangent,
    w_self,
    w_neigh,
    tile_values,
    tile_source,
    slot_source,
    slot_weight,
    send_count,
    recv_rows,
    stale_grad,
    version,
    cross_source,
    cross_weight,
    cross_count,
    cross_rows,
):
    row_count, dim = features.shape
    blocks = row_count // 128
    peers = lax.axis_size("dom")
    cap = slot_source.shape[2]
    bits = peers.bit_length() - 1
    host = lax.axis_index("hst")
    me = lax.axis_index("dom")
    me_ref = me.astype(jnp.int32).reshape(1)
    odd = (me & 1) == 1
    struct = jax.ShapeDtypeStruct

    preact = jnp.dot(features, w_self, preferred_element_type=F32) + jnp.dot(
        aggregated, w_neigh, preferred_element_type=F32
    )
    pre_grad = (cotangent.astype(F32) * silu_slope(preact)).astype(BF16)
    self_sum = jnp.einsum("rd,re->de", features, pre_grad, preferred_element_type=F32)
    neigh_sum = jnp.einsum("rd,re->de", aggregated, pre_grad, preferred_element_type=F32)

    first = host == 0
    half = jnp.where(first, self_sum, neigh_sum) + swap(
        jnp.where(first, neigh_sum, self_sum).astype(BF16), "hst", 0
    ).astype(F32)

    neigh_grad, outgoing = pl.pallas_call(
        outgoing_kernel,
        out_shape=(struct((row_count, dim), BF16), struct((peers * cap, dim), BF16)),
        in_specs=[SMEM, SMEM, VMEM, VMEM, VMEM, VMEM],
        out_specs=(VMEM, VMEM),
        compiler_params=PARAMS,
        name="outgoing",
    )(
        me_ref,
        send_count,
        pre_grad,
        w_neigh,
        jnp.swapaxes(slot_source[0], 1, 2),
        jnp.swapaxes(slot_weight[0], 1, 2),
    )
    cross_out = pl.pallas_call(
        stale_kernel,
        out_shape=struct((cross_source.shape[1], dim), BF16),
        in_specs=[SMEM, SMEM, VMEM, VMEM, VMEM, VMEM],
        out_specs=VMEM,
        compiler_params=PARAMS,
        name="stale_rows",
    )(
        version,
        cross_count,
        stale_grad[0],
        w_neigh,
        cross_source[0].T,
        cross_weight[0].T,
    )
    stale_in = swap(cross_out, "hst", 0)
    base = pl.pallas_call(
        local_kernel,
        out_shape=struct((blocks, 128, dim), F32),
        in_specs=[SMEM, VMEM, VMEM, VMEM, VMEM],
        out_specs=VMEM,
        compiler_params=PARAMS,
        name="local_term",
    )(tile_source, pre_grad, neigh_grad, w_self, tile_values[0])

    quarter = dim // 2
    held = outgoing.reshape(1, peers * cap, dim)
    for bit in range(bits):
        if bit == 0:
            low, high = half[:quarter], half[quarter:]
            kept, given = jnp.where(odd, high, low), jnp.where(odd, low, high).astype(BF16)
        else:
            given = kept.astype(BF16)
            kept = given.astype(F32)
        middle = held.shape[1] // 2
        moved = held[:, middle:].reshape(-1, dim)
        arrived = swap(jnp.concatenate([given, moved], axis=0), "dom", bit)
        kept = kept + arrived[:quarter].astype(F32)
        held = jnp.stack(
            [held[:, :middle], arrived[quarter:].reshape(-1, middle, dim)], axis=1
        ).reshape(-1, middle, dim)

    out_rows = pl.pallas_call(
        finish_kernel,
        out_shape=struct((row_count, dim), BF16),
        in_specs=[SMEM, VMEM, VMEM, VMEM, VMEM, VMEM],
        out_specs=VMEM,
        compiler_params=PARAMS,
        name="finish",
    )(me_ref, base, held.reshape(peers * cap, dim), stale_in, recv_rows[0], cross_rows)

    node_total = row_count * lax.axis_size("hst") * peers
    mine = (kept * (1.0 / math.sqrt(node_total))).astype(BF16)
    other = swap(mine, "dom", 0)
    mine = jnp.where(
        odd, jnp.concatenate([other, mine], axis=0), jnp.concatenate([mine, other], axis=0)
    )
    other = swap(mine, "hst", 0)
    sums = jnp.where(first, jnp.stack([mine, other]), jnp.stack([other, mine]))
    return (out_rows, sums)


def solution(mesh):
    rows = ("runs", "hst", "dom")
    specs = [P(rows)] * 17
    specs[3] = specs[4] = P()
    return jax.shard_map(
        body,
        mesh=mesh,
        in_specs=tuple(specs),
        out_specs=(P(rows), P("runs")),
        check_vma=False,
    )
```

time: 125 us -> 31.4 us (0.25)
  blocking collectives: 35 us -> 0 us
  waiting for transfers between devices: 24.9 us -> 8.54 us
  local copies, waits for them, and re-layouts: 14.5 us -> 0.8 us
  between operations: 15.7 us -> 2.35 us
  other arithmetic: 13.7 us -> 1 us
  matrix products: 13 us -> 3.28 us
  Pallas kernels: 0 us -> 5.39 us
  starting transfers between devices: 7.36 us -> 9.74 us
    all_gather x1 -> x0, blocking collectives: 30.7 us -> none  [weight_sums(): summed = lax.all_gather(shares, 'dom', axis=0, tiled=True)]
    reduce_scatter x1 -> x0, waiting for transfers between devices: 24.9 us -> none  [weight_sums(): shares = lax.psum_scatter(stacked, 'dom', scatter_dimension=0, tiled=True)]
    dot_general x9 -> x4, matrix products: 13 us -> 3.28 us  [the longest x1 1.63 us: body(): jnp.dot(features, w_self, preferred_element_type=F32)]
    ppermute x1 -> x7, starting transfers between devices: 0.45 us -> 9.74 us  [swap(): return lax.ppermute(value, axis, pairs)]
    ppermute x1 -> x7, waiting for transfers between devices: 0.01 us -> 8.54 us  [swap(): return lax.ppermute(value, axis, pairs)]
    scatter-add x2 -> x0, other arithmetic: 7.08 us -> none  [the longest x1 3.64 us: body(): accum_rows = accum_rows.at[cross_rows[0]].add(stale_in.astype(jnp.float32))]
    all_to_all x1 -> x0, starting transfers between devices: 6.87 us -> none  [fresh_path(): lax.all_to_all(outgoing, 'dom', split_axis=0, concat_axis=0, tiled=True)]
    reshape x1 -> x0, local copies, waits for them, and re-layouts: 6.74 us -> none  [fresh_path(): products.reshape(tile_count, 128, feature_dim)]
  transfers between devices with their start and end apart: 3 -> 7, of which waited for: 1 -> 3; matrix products, arithmetic and copies ran while one was open for 29% -> 0% of each run, Pallas kernels for 0% -> 17%
where the time goes in v1:
time: 31.4 us; the launch traced here: 31.1 us
  starting transfers between devices  9.74 us (31%)
  waiting for transfers between devices  8.54 us (27%)
  Pallas kernels  5.39 us (17%)
  matrix products  3.28 us (10%)
  between operations  2.35 us (7%)
  other arithmetic  1 us (3%)
  local copies, waits for them, and re-layouts  0.8 us (3%)
    ppermute x7, starting transfers between devices, swap(): return lax.ppermute(value, axis, pairs)  9.74 us
    ppermute x7, waiting for transfers between devices, swap(): return lax.ppermute(value, axis, pairs)  8.54 us
    pallas_call x1, Pallas kernels, body(): pl.pallas_call(local_kernel, out_shape=struct((blocks, 128, dim), F32), i...  2.02 us
    dot_general x1, matrix products, body(): jnp.dot(features, w_self, preferred_element_type=F32)  1.63 us
    pallas_call x1, Pallas kernels, body(): pl.pallas_call(finish_kernel, out_shape=struct((row_count, dim), BF16), i...  1.52 us
    pallas_call x1, Pallas kernels, body(): pl.pallas_call(outgoing_kernel, out_shape=(struct((row_count, dim), BF16)...  1.51 us
    dot_general x1, matrix products, body(): jnp.dot(aggregated, w_neigh, preferred_element_type=F32)  0.8 us
    unnamed x30, local copies, waits for them, and re-layouts  0.77 us
  transfers between devices with their start and end apart: 7, of which 3 were waited for; matrix products, arithmetic and copies ran while one was open for 0% of the time, Pallas kernels for 17%

profile of v1, /device:TPU:0, one launch (start us, length us, event | category | flops | bytes accessed | tf_op | source)
XLA Modules:
  0.0 31.1 jit_solution(17946796563910069955)
XLA Ops:
  0.6 0.0 copy-start
  0.6 0.0 copy-start.3
  0.7 0.0 copy-start.14
  0.7 1.6 %fusion.1 = f32[1536,256]{1,0:T(8,128)S(1)} fusion(bf16[1536,256]{1,0:T(8,128)(2,1)} %param.17, bf16[256,256]{1,0:T(8,128)(2,1)} %weight_ref.4), kind=kOutput, calls=%fused_computation.25 | convolution fusion | flops 201326592 | bytes 2490368 | tf_op jit(solution)/shard_map/dot_general | solution.py:147
  2.3 0.0 copy-done
  2.3 0.0 copy-done.3
  2.3 0.0 copy-done.14
  2.3 0.8 %multiply_convert_fusion.grad_ref = bf16[1536,256]{1,0:T(8,128)(2,1)S(1)} fusion(f32[1536,256]{1,0:T(8,128)S(1)} %fusion.1, bf16[1536,256]{1,0:T(8,128)(2,1)S(1)} %copy-done, bf16[256,256]{1,0:T(8,128)(2,1)S(1)} %copy-done.3, bf16[1536,256]{1,0:T(8,128)(2,1)S(1)} %copy-done.14), kind=kOutput, calls=%fused_computation.1 | convolution fusion | flops 205651968 | bytes 4063232 | tf_op jit(solution)/shard_map/dot_general | solution.py:147
  3.1 0.0 copy-start.13
  3.2 0.4 %fusion.3 = f32[256,256]{0,1:T(8,128)S(1)} fusion(bf16[1536,256]{1,0:T(8,128)(2,1)S(1)} %multiply_convert_fusion.grad_ref, bf16[1536,256]{1,0:T(8,128)(2,1)S(1)} %copy-done), kind=kOutput, calls=%fused_computation.27 | convolution fusion | flops 201326592 | bytes 1835008 | tf_op jit(solution)/shard_map/rd,re->de/dot_general | solution.py:152
  3.6 0.7 %copy-done.13 = bf16[1536,256]{1,0:T(8,128)(2,1)S(1)} copy-done((bf16[1536,256]{1,0:T(8,128)(2,1)S(1)}, bf16[1536,256]{1,0:T(8,128)(2,1)}, u32[]{:S(2)}) %copy-start.13) | copy-done | bytes 786456
  4.3 0.0 copy-start.5
  4.3 0.0 copy-start.6
  4.3 0.0 copy-start.10
  4.3 0.4 %fusion.2 = f32[256,256]{0,1:T(8,128)S(1)} fusion(bf16[1536,256]{1,0:T(8,128)(2,1)S(1)} %multiply_convert_fusion.grad_ref, bf16[1536,256]{1,0:T(8,128)(2,1)S(1)} %copy-done.13), kind=kOutput, calls=%fused_computation.26 | convolution fusion | flops 201326592 | bytes 1835008 | tf_op jit(solution)/shard_map/rd,re->de/dot_general | solution.py:151
  4.8 0.5 %collective-permute-start = (bf16[256,256]{1,0:T(8,128)(2,1)S(1)}, bf16[256,256]{1,0:T(8,128)(2,1)S(1)}, u32[]{:S(2)}, u32[]{:S(2)}) collective-permute-start(bf16[256,256]{1,0:T(8,128)(2,1)S(1)} %fusion), channel_id=1, source_target_pairs={{0,8},{8,0},{1,9},{9,1},{2,10},{10,2},{3,11},{11,3},{4,12},{12,4},... | collective-permute-start | bytes 393224 | tf_op jit(solution)/shard_map/ppermute | solution.py:21
  5.3 0.0 copy-done.5
  5.3 0.0 copy-done.6
  5.3 0.0 copy-done.10
  5.3 1.5 %outgoing.1 = (bf16[1536,256]{1,0:T(8,128)(2,1)S(1)}, bf16[64,256]{1,0:T(8,128)(2,1)S(1)}) custom-call(s32[1]{0:T(128)} %bitcast.me_ref, s32[1,8]{1,0:T(1,128)S(1)} %copy-done.10, bf16[1536,256]{1,0:T(8,128)(2,1)S(1)} %multiply_convert_fusion.grad_ref, bf16[256,256]{1,0:T(8,128)(2,1)S(1)} %copy-done.3, s32[8,4,8]{2,1,0:T(4,128)S(1)} %bitcast.56, ...), custom_call_target="tpu_custom_call" | custom-call | tf_op jit(solution)/shard_map/outgoing/pallas_call | solution.py:159
  6.8 0.0 copy-start.4
  6.8 0.0 copy-start.8
  6.8 0.0 copy-start.9
  6.8 0.0 copy-start.1
  6.8 0.0 copy-start.2
  6.9 0.0 copy-start.11
  6.9 0.0 collective-permute-done
  7.0 2.7 %collective-permute-start.1 = (bf16[160,256]{1,0:T(8,128)(2,1)S(1)}, bf16[160,256]{1,0:T(8,128)(2,1)S(1)}, u32[]{:S(2)}, u32[]{:S(2)}) collective-permute-start(bf16[160,256]{1,0:T(8,128)(2,1)S(1)} %pad_maximum_fusion), channel_id=1, source_target_pairs={{0,1},{1,0},{2,3},{3,2},{4,5},{5,4},{6,7},{7,6},{8,9},{9,8},{10,11... | collective-permute-start | bytes 245768 | tf_op jit(solution)/shard_map/ppermute | solution.py:21
  9.7 2.9 %collective-permute-done.1 = bf16[160,256]{1,0:T(8,128)(2,1)S(1)} collective-permute-done((bf16[160,256]{1,0:T(8,128)(2,1)S(1)}, bf16[160,256]{1,0:T(8,128)(2,1)S(1)}, u32[]{:S(2)}, u32[]{:S(2)}) %collective-permute-start.1) | collective-permute-done | bytes 81952 | tf_op jit(solution)/shard_map/ppermute | solution.py:21
  12.7 1.9 %collective-permute-start.2 = (bf16[160,256]{1,0:T(8,128)(2,1)S(1)}, bf16[160,256]{1,0:T(8,128)(2,1)S(1)}, u32[]{:S(2)}, u32[]{:S(2)}) collective-permute-start(bf16[160,256]{1,0:T(8,128)(2,1)S(1)} %pad_maximum_fusion.1), channel_id=1, source_target_pairs={{0,2},{1,3},{2,0},{3,1},{4,6},{5,7},{6,4},{7,5},{8,10},{9,11},{10,... | collective-permute-start | bytes 245768 | tf_op jit(solution)/shard_map/ppermute | solution.py:21
  14.6 2.6 %collective-permute-done.2 = bf16[160,256]{1,0:T(8,128)(2,1)S(1)} collective-permute-done((bf16[160,256]{1,0:T(8,128)(2,1)S(1)}, bf16[160,256]{1,0:T(8,128)(2,1)S(1)}, u32[]{:S(2)}, u32[]{:S(2)}) %collective-permute-start.2) | collective-permute-done | bytes 81952 | tf_op jit(solution)/shard_map/ppermute | solution.py:21
  17.3 2.9 %collective-permute-start.3 = (bf16[160,256]{1,0:T(8,128)(2,1)S(1)}, bf16[160,256]{1,0:T(8,128)(2,1)S(1)}, u32[]{:S(2)}, u32[]{:S(2)}) collective-permute-start(bf16[160,256]{1,0:T(8,128)(2,1)S(1)} %pad_maximum_fusion.2), channel_id=1, source_target_pairs={{0,4},{1,5},{2,6},{3,7},{4,0},{5,1},{6,2},{7,3},{8,12},{9,13},{10,... | collective-permute-start | bytes 245768 | tf_op jit(solution)/shard_map/ppermute | solution.py:21
  21.5 0.0 copy-done.4
  21.5 0.0 copy-done.8
  21.5 0.0 copy-done.9
  21.5 0.3 %stale_rows.1 = bf16[64,256]{1,0:T(8,128)(2,1)S(1)} custom-call(s32[1]{0:T(128)S(6)} %copy.22.version_ref, s32[1]{0:T(128)S(6)} %copy.23.count_ref, bf16[2,64,256]{2,1,0:T(8,128)(2,1)S(1)} %bitcast.54, bf16[256,256]{1,0:T(8,128)(2,1)S(1)} %copy-done.3, s32[4,64]{1,0:T(4,128)S(1)} %bitcast.59, f32[4,64]{1,0:T(4,128)S(1)} %bitcast.60), custom_call_target="tpu_custom_call" | custom-call | tf_op jit(solution)/shard_map/stale_rows/pallas_call | solution.py:174
  21.9 0.1 collective-permute-start.4
  22.0 0.0 copy-done.1
  22.0 0.0 copy-done.2
  22.0 0.0 copy-done.11
  22.0 0.0 copy-start.7
  22.0 0.0 copy-start.12
  22.0 2.0 %local_term.1.base_ref = f32[12,128,256]{2,1,0:T(8,128)S(1)} custom-call(s32[1,48]{1,0:T(1,128)S(1)} %copy-done.11, bf16[1536,256]{1,0:T(8,128)(2,1)S(1)} %multiply_convert_fusion.grad_ref, bf16[1536,256]{1,0:T(8,128)(2,1)S(1)} %get-tuple-element.4.neigh_ref, bf16[256,256]{1,0:T(8,128)(2,1)S(1)} %copy-done.2, bf16[48,128,128]{2,1,0:T(8,128)(2,1)S(1)} %bitcast.52), custom_call_target="tpu_custom_call" | custom-call | tf_op jit(solution)/shard_map/local_term/pallas_call | solution.py:190
  24.0 0.0 collective-permute-done.3
  24.1 1.6 %collective-permute-start.5 = (bf16[128,256]{1,0:T(8,128)(2,1)S(1)}, bf16[128,256]{1,0:T(8,128)(2,1)S(1)}, u32[]{:S(2)}, u32[]{:S(2)}) collective-permute-start(bf16[128,256]{1,0:T(8,128)(2,1)S(1)} %multiply_convert_fusion.1), channel_id=1, source_target_pairs={{0,1},{1,0},{2,3},{3,2},{4,5},{5,4},{6,7},{7,6},{8,9},{9,8},{10,11... | collective-permute-start | bytes 196616 | tf_op jit(solution)/shard_map/ppermute | solution.py:21
  25.7 3.0 %collective-permute-done.5 = bf16[128,256]{1,0:T(8,128)(2,1)S(1)} collective-permute-done((bf16[128,256]{1,0:T(8,128)(2,1)S(1)}, bf16[128,256]{1,0:T(8,128)(2,1)S(1)}, u32[]{:S(2)}, u32[]{:S(2)}) %collective-permute-start.5) | collective-permute-done | bytes 65568 | tf_op jit(solution)/shard_map/ppermute | solution.py:21
  28.7 0.1 collective-permute-start.6
  28.8 0.0 collective-permute-done.4.stale_ref
  28.8 0.0 copy-done.7
  28.8 0.0 copy-done.12
  28.8 1.5 %finish.1 = bf16[1536,256]{1,0:T(8,128)(2,1)} custom-call(s32[1]{0:T(128)} %bitcast.me_ref, f32[12,128,256]{2,1,0:T(8,128)S(1)} %local_term.1.base_ref, bf16[64,256]{1,0:T(8,128)(2,1)S(1)} %bitcast.53, bf16[64,256]{1,0:T(8,128)(2,1)S(1)} %collective-permute-done.4.stale_ref, s32[8,8]{1,0:T(8,128)S(1)} %bitcast.58, s32[1,64]{1,0:T(1,128)S(1)} %copy-done.12), custom_call_target="tpu_custom_call" | custom-call | tf_op jit(solution)/shard_map/finish/pallas_call | solution.py:216
  30.4 0.0 collective-permute-done.6
  30.4 0.7 %maximum_select_fusion = bf16[2,256,256]{2,1,0:T(8,128)(2,1)} fusion(bf16[1,256,256]{2,1,0:T(8,128)(2,1)S(1)} %bitcast.63, bf16[1,256,256]{2,1,0:T(8,128)(2,1)S(1)} %maximum_select_fusion.1, pred[]{:T(512)S(6)} %eq.7), kind=kLoop, calls=%fused_computation.2 | loop fusion | flops 393216 | bytes 524289 | tf_op jit(solution)/shard_map/jit(_where)/select_n | solution.py:232
  (22 shorter events, 0.3 us)
Async XLA Ops:
  0.6 1.7 %copy-start = (bf16[1536,256]{1,0:T(8,128)(2,1)S(1)}, bf16[1536,256]{1,0:T(8,128)(2,1)}, u32[]{:S(2)}) copy-start(bf16[1536,256]{1,0:T(8,128)(2,1)} %param.18) | copy-start | bytes 2359300
  0.6 1.7 %copy-start.3 = (bf16[256,256]{1,0:T(8,128)(2,1)S(1)}, bf16[256,256]{1,0:T(8,128)(2,1)}, u32[]{:S(2)}) copy-start(bf16[256,256]{1,0:T(8,128)(2,1)} %weight_ref.5) | copy-start | bytes 393220
  0.7 1.7 %copy-start.14 = (bf16[1536,256]{1,0:T(8,128)(2,1)S(1)}, bf16[1536,256]{1,0:T(8,128)(2,1)}, u32[]{:S(2)}) copy-start(bf16[1536,256]{1,0:T(8,128)(2,1)} %param.19) | copy-start | bytes 2359300
  3.1 1.1 %copy-start.13 = (bf16[1536,256]{1,0:T(8,128)(2,1)S(1)}, bf16[1536,256]{1,0:T(8,128)(2,1)}, u32[]{:S(2)}) copy-start(bf16[1536,256]{1,0:T(8,128)(2,1)} %param.17) | copy-start | bytes 2359300
  4.3 1.0 %copy-start.5 = (s32[1,8,8,4]{2,3,1,0:T(4,128)S(1)}, s32[1,8,8,4]{2,3,1,0:T(4,128)}, u32[]{:S(2)}) copy-start(s32[1,8,8,4]{2,3,1,0:T(4,128)} %param.24) | copy-start | bytes 3076
  4.3 1.0 %copy-start.6 = (f32[1,8,8,4]{2,3,1,0:T(4,128)S(1)}, f32[1,8,8,4]{2,3,1,0:T(4,128)}, u32[]{:S(2)}) copy-start(f32[1,8,8,4]{2,3,1,0:T(4,128)} %param.25) | copy-start | bytes 3076
  4.3 1.0 %copy-start.10 = (s32[1,8]{1,0:T(1,128)S(1)}, s32[1,8]{1,0:T(1,128)}, u32[]{:S(2)}) copy-start(s32[1,8]{1,0:T(1,128)} %count_ref.2) | copy-start | bytes 100
  4.8 2.1 %collective-permute-start = (bf16[256,256]{1,0:T(8,128)(2,1)S(1)}, bf16[256,256]{1,0:T(8,128)(2,1)S(1)}, u32[]{:S(2)}, u32[]{:S(2)}) collective-permute-start(bf16[256,256]{1,0:T(8,128)(2,1)S(1)} %fusion), channel_id=1, source_target_pairs={{0,8},{8,0},{1,9},{9,1},{2,10},{10,2},{3,11},{11,3},{4,12},{12,4},... | collective-permute-start | bytes 393224 | tf_op jit(solution)/shard_map/ppermute | solution.py:21
  6.8 14.7 %copy-start.4 = (bf16[1,2,64,256]{3,2,1,0:T(8,128)(2,1)S(1)}, bf16[1,2,64,256]{3,2,1,0:T(8,128)(2,1)}, u32[]{:S(2)}) copy-start(bf16[1,2,64,256]{3,2,1,0:T(8,128)(2,1)} %param.28) | copy-start | bytes 196612
  6.8 14.7 %copy-start.8 = (s32[1,64,4]{1,2,0:T(4,128)S(1)}, s32[1,64,4]{1,2,0:T(4,128)}, u32[]{:S(2)}) copy-start(s32[1,64,4]{1,2,0:T(4,128)} %param.30) | copy-start | bytes 3076
  6.8 14.7 %copy-start.9 = (f32[1,64,4]{1,2,0:T(4,128)S(1)}, f32[1,64,4]{1,2,0:T(4,128)}, u32[]{:S(2)}) copy-start(f32[1,64,4]{1,2,0:T(4,128)} %param.31) | copy-start | bytes 3076
  6.8 15.1 %copy-start.1 = (bf16[1,48,128,128]{3,2,1,0:T(8,128)(2,1)S(1)}, bf16[1,48,128,128]{3,2,1,0:T(8,128)(2,1)}, u32[]{:S(2)}) copy-start(bf16[1,48,128,128]{3,2,1,0:T(8,128)(2,1)} %param.22) | copy-start | bytes 4718596
  6.8 15.1 %copy-start.2 = (bf16[256,256]{1,0:T(8,128)(2,1)S(1)}, bf16[256,256]{1,0:T(8,128)(2,1)}, u32[]{:S(2)}) copy-start(bf16[256,256]{1,0:T(8,128)(2,1)} %weight_ref.4) | copy-start | bytes 393220
  6.9 15.1 %copy-start.11 = (s32[1,48]{1,0:T(1,128)S(1)}, s32[1,48]{1,0:T(1,128)}, u32[]{:S(2)}) copy-start(s32[1,48]{1,0:T(1,128)} %source_ref.1) | copy-start | bytes 580
  7.0 5.7 %collective-permute-start.1 = (bf16[160,256]{1,0:T(8,128)(2,1)S(1)}, bf16[160,256]{1,0:T(8,128)(2,1)S(1)}, u32[]{:S(2)}, u32[]{:S(2)}) collective-permute-start(bf16[160,256]{1,0:T(8,128)(2,1)S(1)} %pad_maximum_fusion), channel_id=1, source_target_pairs={{0,1},{1,0},{2,3},{3,2},{4,5},{5,4},{6,7},{7,6},{8,9},{9,8},{10,11... | collective-permute-start | bytes 245768 | tf_op jit(solution)/shard_map/ppermute | solution.py:21
  12.7 4.5 %collective-permute-start.2 = (bf16[160,256]{1,0:T(8,128)(2,1)S(1)}, bf16[160,256]{1,0:T(8,128)(2,1)S(1)}, u32[]{:S(2)}, u32[]{:S(2)}) collective-permute-start(bf16[160,256]{1,0:T(8,128)(2,1)S(1)} %pad_maximum_fusion.1), channel_id=1, source_target_pairs={{0,2},{1,3},{2,0},{3,1},{4,6},{5,7},{6,4},{7,5},{8,10},{9,11},{10,... | collective-permute-start | bytes 245768 | tf_op jit(solution)/shard_map/ppermute | solution.py:21
  17.3 6.7 %collective-permute-start.3 = (bf16[160,256]{1,0:T(8,128)(2,1)S(1)}, bf16[160,256]{1,0:T(8,128)(2,1)S(1)}, u32[]{:S(2)}, u32[]{:S(2)}) collective-permute-start(bf16[160,256]{1,0:T(8,128)(2,1)S(1)} %pad_maximum_fusion.2), channel_id=1, source_target_pairs={{0,4},{1,5},{2,6},{3,7},{4,0},{5,1},{6,2},{7,3},{8,12},{9,13},{10,... | collective-permute-start | bytes 245768 | tf_op jit(solution)/shard_map/ppermute | solution.py:21
  21.9 6.9 %collective-permute-start.4 = (bf16[64,256]{1,0:T(8,128)(2,1)S(1)}, bf16[64,256]{1,0:T(8,128)(2,1)S(1)}, u32[]{:S(2)}, u32[]{:S(2)}) collective-permute-start(bf16[64,256]{1,0:T(8,128)(2,1)S(1)} %stale_rows.1), channel_id=1, source_target_pairs={{0,8},{8,0},{1,9},{9,1},{2,10},{10,2},{3,11},{11,3},{4,12},{12,4},... | collective-permute-start | bytes 98312 | tf_op jit(solution)/shard_map/ppermute | solution.py:21
  22.0 6.8 %copy-start.7 = (s32[1,8,8]{2,1,0:T(8,128)S(1)}, s32[1,8,8]{2,1,0:T(8,128)}, u32[]{:S(2)}) copy-start(s32[1,8,8]{2,1,0:T(8,128)} %param.27) | copy-start | bytes 772
  22.0 6.8 %copy-start.12 = (s32[1,64]{1,0:T(1,128)S(1)}, s32[1,64]{1,0:T(1,128)}, u32[]{:S(2)}) copy-start(s32[1,64]{1,0:T(1,128)} %cross_ref.1) | copy-start | bytes 772
  24.1 4.5 %collective-permute-start.5 = (bf16[128,256]{1,0:T(8,128)(2,1)S(1)}, bf16[128,256]{1,0:T(8,128)(2,1)S(1)}, u32[]{:S(2)}, u32[]{:S(2)}) collective-permute-start(bf16[128,256]{1,0:T(8,128)(2,1)S(1)} %multiply_convert_fusion.1), channel_id=1, source_target_pairs={{0,1},{1,0},{2,3},{3,2},{4,5},{5,4},{6,7},{7,6},{8,9},{9,8},{10,11... | collective-permute-start | bytes 196616 | tf_op jit(solution)/shard_map/ppermute | solution.py:21
  28.7 1.7 %collective-permute-start.6 = (bf16[256,256]{1,0:T(8,128)(2,1)S(1)}, bf16[256,256]{1,0:T(8,128)(2,1)S(1)}, u32[]{:S(2)}, u32[]{:S(2)}) collective-permute-start(bf16[256,256]{1,0:T(8,128)(2,1)S(1)} %maximum_select_fusion.2), channel_id=1, source_target_pairs={{0,8},{8,0},{1,9},{9,1},{2,10},{10,2},{3,11},{11,3},{4,12},{12,4},... | collective-permute-start | bytes 393224 | tf_op jit(solution)/shard_map/ppermute | solution.py:21

commit v2 on v1

v2 whole, which is shorter than its diff:
```python
import functools
import math

import jax
import jax.numpy as jnp
from jax import lax
from jax.experimental import pallas as pl
from jax.experimental.pallas import tpu as pltpu
from jax.sharding import PartitionSpec as P

BF16, F32 = jnp.bfloat16, jnp.float32
VMEM = pl.BlockSpec(memory_space=pltpu.VMEM)
ANY = pl.BlockSpec(memory_space=pl.ANY)
SMEM = pl.BlockSpec(memory_space=pltpu.SMEM)
PARAMS = pltpu.CompilerParams(vmem_limit_bytes=16 * 2**20)
NT = (((1,), (1,)), ((), ()))
TN = (((0,), (0,)), ((), ()))
PARTS = 2
CHUNKS = 3
OUT_BLOCKS = 4


def in_hbm(*values):
    return [pltpu.with_memory_space_constraint(value, pltpu.HBM) for value in values]


def swap(value, axis, bit):
    pairs = [(source, source ^ (1 << bit)) for source in range(lax.axis_size(axis))]
    return lax.ppermute(value, axis, pairs)


def silu_slope(preact):
    sigmoid = jax.nn.sigmoid(preact)
    return sigmoid * (1.0 + preact * (1.0 - sigmoid))


def hop_bits(count):
    bits = count.bit_length() - 1
    return [*range(1, bits), 0]


def hop_order(count):
    hops = hop_bits(count)[::-1]
    return [sum(((i >> j) & 1) << bit for j, bit in enumerate(hops)) for i in range(count)]


def split_dot(weights, rows):
    high = weights.astype(BF16)
    low = (weights - high.astype(F32)).astype(BF16)
    return jnp.dot(high, rows, preferred_element_type=F32) + jnp.dot(
        low, rows, preferred_element_type=F32
    )


def gradient_kernel(
    host_ref,
    features_hbm,
    aggregated_hbm,
    cotangent_hbm,
    self_hbm,
    neigh_hbm,
    grad_ref,
    kept_ref,
    given_ref,
    features,
    aggregated,
    cotangent,
    self_weight,
    neigh_weight,
    sums,
    sems,
):
    part_rows = features.shape[0] // PARTS
    rows = part_rows // CHUNKS
    copies = []

    def fetch(source, target):
        copy = pltpu.make_async_copy(source, target, sems.at[len(copies)])
        copy.start()
        copies.append(copy)

    fetch(self_hbm, self_weight)
    fetch(neigh_hbm, neigh_weight)
    for p in range(PARTS):
        part = pl.ds(p * part_rows, part_rows)
        fetch(features_hbm.at[part], features.at[part])
        fetch(aggregated_hbm.at[part], aggregated.at[part])
        fetch(cotangent_hbm.at[part], cotangent.at[part])
    copies[0].wait()
    copies[1].wait()
    for p in range(PARTS):
        for copy in copies[3 * p + 2 : 3 * p + 5]:
            copy.wait()
        for c in range(CHUNKS):
            part = pl.ds(p * part_rows + c * rows, rows)
            left, right = features[part, :], aggregated[part, :]
            preact = jnp.dot(left, self_weight[...], preferred_element_type=F32) + jnp.dot(
                right, neigh_weight[...], preferred_element_type=F32
            )
            grad = (cotangent[part, :].astype(F32) * silu_slope(preact)).astype(BF16)
            grad_ref[part, :] = grad
            for i, values in enumerate((left, right)):
                term = lax.dot_general(values, grad, TN, preferred_element_type=F32)
                if p == 0 and c == 0:
                    sums[i] = term
                else:
                    sums[i] += term
    host = host_ref[0]
    kept_ref[...] = sums[host]
    given_ref[...] = sums[1 - host].astype(BF16)


def outgoing_kernel(
    me_ref,
    count_ref,
    grad_ref,
    weight_ref,
    source_ref,
    scale_ref,
    after_ref,
    neigh_ref,
    out_ref,
):
    peers, fan, cap = source_ref.shape
    me = me_ref[0]
    neigh = lax.dot_general(grad_ref[...], weight_ref[...], NT, preferred_element_type=F32)
    neigh = neigh.astype(BF16)
    neigh_ref[...] = neigh
    rows = neigh.shape[0]
    order = hop_order(peers)
    slot = lax.broadcasted_iota(jnp.int32, (fan, cap), 1)
    group = min(peers, 128 // cap)
    for first in range(0, peers, group):
        sources, scales = [], []
        for r in order[first : first + group]:
            q = jnp.bitwise_xor(me, r)
            live = slot < count_ref[0, q]
            sources.append(source_ref[q])
            scales.append(jnp.where(live, scale_ref[q], 0.0))
        sources = jnp.concatenate(sources, axis=1).T
        scales = jnp.concatenate(scales, axis=1).T
        slots = group * cap
        node = lax.broadcasted_iota(jnp.int32, (slots, rows), 1)
        select = jnp.zeros((slots, rows), F32)
        for k in range(fan):
            select += jnp.where(sources[:, k : k + 1] == node, scales[:, k : k + 1], 0.0)
        out_ref[pl.ds(first * cap, slots), :] = split_dot(select, neigh).astype(BF16)


def stale_kernel(
    version_ref, count_ref, stale_ref, weight_ref, source_ref, scale_ref, stay_ref, out_ref, same_ref
):
    chosen = stale_ref[version_ref[0]]
    neigh = lax.dot_general(chosen, weight_ref[...], NT, preferred_element_type=F32).astype(BF16)
    fan, slots = source_ref.shape
    live = lax.broadcasted_iota(jnp.int32, (1, slots), 1) < count_ref[0]
    stored = lax.broadcasted_iota(jnp.int32, (neigh.shape[0], slots), 0)
    select = jnp.zeros(stored.shape, F32)
    for k in range(fan):
        scale = jnp.where(live, scale_ref[pl.ds(k, 1), :], 0.0)
        select += jnp.where(source_ref[pl.ds(k, 1), :] == stored, scale, 0.0)
    out_ref[...] = split_dot(select.T, neigh).astype(BF16)


def local_kernel(
    source_ref,
    grad_ref,
    neigh_ref,
    weight_ref,
    tile_ref,
    stay_ref,
    base_ref,
    same_ref,
):
    blocks = base_ref.shape[0]
    tiles = tile_ref.shape[0]
    per_block = tiles // blocks
    for b in range(blocks):
        rows = pl.ds(b * 128, 128)
        base_ref[b] = lax.dot_general(
            grad_ref[rows, :], weight_ref[...], NT, preferred_element_type=F32
        )
    for b in range(blocks):
        neigh = neigh_ref[pl.ds(b * 128, 128), :]
        for t in range(b * per_block, (b + 1) * per_block):
            product = lax.dot_general(tile_ref[t], neigh, TN, preferred_element_type=F32)
            base_ref[source_ref[0, t]] += product


def finish_kernel(
    me_ref, base_ref, fresh_ref, stale_ref, recv_ref, cross_ref, out_hbm, out, sems
):
    me = me_ref[0]
    blocks = base_ref.shape[0]
    peers, cap = recv_ref.shape
    targets = [recv_ref[pl.ds(jnp.bitwise_xor(me, o), 1), :] for o in hop_order(peers)]
    targets = jnp.concatenate(targets + [cross_ref[...]], axis=1)
    values = jnp.concatenate([fresh_ref[...], stale_ref[...]], axis=0)
    copies = []
    for b in range(blocks):
        node = b * 128 + lax.broadcasted_iota(jnp.int32, (128, targets.shape[1]), 0)
        hit = jnp.where(node == targets, 1.0, 0.0).astype(BF16)
        total = base_ref[b] + jnp.dot(hit, values, preferred_element_type=F32)
        out[pl.ds(b * 128, 128), :] = total.astype(BF16)
        if (b + 1) % OUT_BLOCKS == 0 or b + 1 == blocks:
            first = b // OUT_BLOCKS * OUT_BLOCKS
            part = pl.ds(first * 128, (b + 1 - first) * 128)
            copy = pltpu.make_async_copy(out.at[part], out_hbm.at[part], sems.at[len(copies)])
            copy.start()
            copies.append(copy)
    for copy in copies:
        copy.wait()


def body(
    features,
    aggregated,
    cotangent,
    w_self,
    w_neigh,
    tile_values,
    tile_source,
    slot_source,
    slot_weight,
    send_count,
    recv_rows,
    stale_grad,
    version,
    cross_source,
    cross_weight,
    cross_count,
    cross_rows,
):
    row_count, dim = features.shape
    blocks = row_count // 128
    peers = lax.axis_size("dom")
    cap = slot_source.shape[2]
    bits = peers.bit_length() - 1
    host = lax.axis_index("hst")
    me = lax.axis_index("dom")
    me_ref = me.astype(jnp.int32).reshape(1)
    host_ref = host.astype(jnp.int32).reshape(1)
    odd = (me & 1) == 1
    struct = jax.ShapeDtypeStruct

    pre_grad, own, given = pl.pallas_call(
        gradient_kernel,
        out_shape=(
            pltpu.VMEM((row_count, dim), BF16),
            pltpu.VMEM((dim, dim), F32),
            pltpu.VMEM((dim, dim), BF16),
        ),
        in_specs=[SMEM, ANY, ANY, ANY, ANY, ANY],
        out_specs=(VMEM, VMEM, VMEM),
        scratch_shapes=[
            pltpu.VMEM((row_count, dim), BF16),
            pltpu.VMEM((row_count, dim), BF16),
            pltpu.VMEM((row_count, dim), BF16),
            pltpu.VMEM((dim, dim), BF16),
            pltpu.VMEM((dim, dim), BF16),
            pltpu.VMEM((2, dim, dim), F32),
            pltpu.SemaphoreType.DMA((2 + 3 * PARTS,)),
        ],
        compiler_params=PARAMS,
        name="gradients",
    )(host_ref, *in_hbm(features, aggregated, cotangent, w_self, w_neigh))
    first = host == 0
    half = own + swap(given, "hst", 0).astype(F32)
    quarter = dim // 2
    low, high = half[:quarter], half[quarter:]
    kept, given = jnp.where(odd, high, low), jnp.where(odd, low, high).astype(BF16)
    kept = kept + swap(given, "dom", 0).astype(F32)

    neigh_grad, outgoing = pl.pallas_call(
        outgoing_kernel,
        out_shape=(struct((row_count, dim), BF16), struct((peers * cap, dim), BF16)),
        in_specs=[SMEM, SMEM, VMEM, VMEM, VMEM, VMEM, ANY],
        out_specs=(VMEM, VMEM),
        compiler_params=PARAMS,
        name="outgoing",
    )(
        me_ref,
        send_count,
        pre_grad,
        w_neigh,
        jnp.swapaxes(slot_source[0], 1, 2),
        jnp.swapaxes(slot_weight[0], 1, 2),
        given,
    )
    held = outgoing.reshape(1, peers * cap, dim)
    scale = 1.0 / math.sqrt(row_count * lax.axis_size("hst") * peers)
    for step, bit in enumerate(hop_bits(peers)):
        given = (kept if bit else kept * scale).astype(BF16)
        middle = held.shape[1] // 2
        stay, moved = held[:, :middle], held[:, middle:].reshape(-1, dim)
        arrived = swap(jnp.concatenate([given, moved], axis=0), "dom", bit)
        if step == 0:
            cross_out, stay = pl.pallas_call(
                stale_kernel,
                out_shape=(
                    struct((cross_source.shape[1], dim), BF16),
                    struct(stay.shape, stay.dtype),
                ),
                in_specs=[SMEM, SMEM, VMEM, VMEM, VMEM, VMEM, ANY],
                out_specs=(VMEM, ANY),
                input_output_aliases={6: 1},
                compiler_params=PARAMS,
                name="stale_rows",
            )(
                version,
                cross_count,
                stale_grad[0],
                w_neigh,
                cross_source[0].T,
                cross_weight[0].T,
                stay,
            )
            stale_in = swap(cross_out, "hst", 0)
        if step == 1:
            base, stay = pl.pallas_call(
                local_kernel,
                out_shape=(
                    struct((blocks, 128, dim), F32),
                    struct(stay.shape, stay.dtype),
                ),
                in_specs=[SMEM, VMEM, VMEM, VMEM, VMEM, ANY],
                out_specs=(VMEM, ANY),
                input_output_aliases={5: 1},
                compiler_params=PARAMS,
                name="local_term",
            )(tile_source, pre_grad, neigh_grad, w_self, tile_values[0], stay)
        other = arrived[:quarter]
        kept = given.astype(F32) + other.astype(F32)
        held = jnp.stack([stay, arrived[quarter:].reshape(stay.shape)], axis=1)
        held = held.reshape(-1, middle, dim)
    mine = jnp.where(
        odd, jnp.concatenate([other, given], axis=0), jnp.concatenate([given, other], axis=0)
    )
    other = swap(mine, "hst", 0)
    sums = jnp.where(first, jnp.stack([mine, other]), jnp.stack([other, mine]))

    out_rows = pl.pallas_call(
        finish_kernel,
        out_shape=struct((row_count, dim), BF16),
        in_specs=[SMEM, VMEM, VMEM, VMEM, VMEM, VMEM],
        out_specs=ANY,
        scratch_shapes=[
            pltpu.VMEM((row_count, dim), BF16),
            pltpu.SemaphoreType.DMA((pl.cdiv(blocks, OUT_BLOCKS),)),
        ],
        compiler_params=PARAMS,
        name="finish",
    )(me_ref, base, held.reshape(peers * cap, dim), stale_in, recv_rows[0], cross_rows)
    return (out_rows, sums)


def solution(mesh):
    rows = ("runs", "hst", "dom")
    specs = [P(rows)] * 17
    specs[3] = specs[4] = P()
    return jax.shard_map(
        body,
        mesh=mesh,
        in_specs=tuple(specs),
        out_specs=(P(rows), P("runs")),
        check_vma=False,
    )
```

time: 31.4 us -> 27.9 us (0.89)
  matrix products: 3.28 us -> 0 us
  waiting for transfers between devices: 8.54 us -> 5.63 us
  Pallas kernels: 5.39 us -> 8.17 us
  local copies, waits for them, and re-layouts: 0.8 us -> 0.1 us
  starting transfers between devices: 9.74 us -> 10.4 us
    dot_general x4 -> x0, matrix products: 3.28 us -> none  [the longest x1 1.63 us: body(): jnp.dot(features, w_self, preferred_element_type=F32)]
    pallas_call x2 -> x3, Pallas kernels: 2.36 us -> 5.47 us  [the longest x1 3.06 us: body(): pl.pallas_call(gradient_kernel, out_shape=(pltpu.VMEM((row_count, dim), B...]
    ppermute x7, waiting for transfers between devices: 8.54 us -> 5.63 us  [swap(): return lax.ppermute(value, axis, pairs)]
    unnamed x30 -> x24, local copies, waits for them, and re-layouts: 0.77 us -> 0.06 us
    ppermute x7, starting transfers between devices: 9.74 us -> 10.4 us  [swap(): return lax.ppermute(value, axis, pairs)]
    pallas_call x1, Pallas kernels: 1.52 us -> 1.19 us  [body(): pl.pallas_call(finish_kernel, out_shape=struct((row_count, dim), BF16), i...]
  transfers between devices with their start and end apart: 7 -> 7, of which waited for: 3 -> 5; matrix products, arithmetic and copies ran while one was open for 0% -> 0% of each run, Pallas kernels for 17% -> 19%
where the time goes in v2:
time: 27.9 us; the launch traced here: 27.5 us
  starting transfers between devices  10.4 us (37%)
  Pallas kernels  8.17 us (29%)
  waiting for transfers between devices  5.63 us (20%)
  between operations  2.24 us (8%)
  other arithmetic  0.95 us (3%)
    ppermute x7, starting transfers between devices, swap(): return lax.ppermute(value, axis, pairs)  10.4 us
    ppermute x7, waiting for transfers between devices, swap(): return lax.ppermute(value, axis, pairs)  5.63 us
    pallas_call x1, Pallas kernels, body(): pl.pallas_call(gradient_kernel, out_shape=(pltpu.VMEM((row_count, dim), B...  3.06 us
    pallas_call x1, Pallas kernels, body(): pl.pallas_call(local_kernel, out_shape=(struct((blocks, 128, dim), F32),...  2.07 us
    pallas_call x1, Pallas kernels, body(): pl.pallas_call(outgoing_kernel, out_shape=(struct((row_count, dim), BF16)...  1.51 us
    pallas_call x1, Pallas kernels, body(): pl.pallas_call(finish_kernel, out_shape=struct((row_count, dim), BF16), i...  1.19 us
    select_n x1, other arithmetic, body(): sums = jnp.where(first, jnp.stack([mine, other]), jnp.stack([other, mine]))  0.73 us
  transfers between devices with their start and end apart: 7, of which 5 were waited for; matrix products, arithmetic and copies ran while one was open for 0% of the time, Pallas kernels for 19%

profile of v2, /device:TPU:0, one launch (start us, length us, event | category | flops | bytes accessed | tf_op | source)
XLA Modules:
  0.0 27.5 jit_solution(13072366003010153283)
XLA Ops:
  0.6 0.0 copy-start.1
  0.6 0.0 copy-start.4
  0.7 0.0 copy-start.5
  0.7 0.0 copy-start.9
  0.7 3.1 %gradients.1 = (bf16[1536,256]{1,0:T(8,128)(2,1)S(1)}, f32[256,256]{1,0:T(8,128)S(1)}, bf16[256,256]{1,0:T(8,128)(2,1)S(1)}) custom-call(s32[1]{0:T(128)} %bitcast.1.host_ref, bf16[1536,256]{1,0:T(8,128)(2,1)} %features_hbm.1, bf16[1536,256]{1,0:T(8,128)(2,1)} %aggregated_hbm.1, bf16[1536,256]{1,0:T(8,128)(2,1)} %cotangent_hbm.1, ...), custom_call_target="tpu_custom_call" | custom-call | tf_op jit(solution)/shard_map/gradients/pallas_call | solution.py:246
  3.7 0.0 copy-start.3
  3.8 0.0 copy-start.7
  3.8 0.0 copy-start.8
  3.8 0.5 %collective-permute-start = (bf16[256,256]{1,0:T(8,128)(2,1)S(1)}, bf16[256,256]{1,0:T(8,128)(2,1)S(1)}, u32[]{:S(2)}, u32[]{:S(2)}) collective-permute-start(bf16[256,256]{1,0:T(8,128)(2,1)S(1)} %get-tuple-element.13), channel_id=1, source_target_pairs={{0,8},{8,0},{1,9},{9,1},{2,10},{10,2},{3,11},{11,3},{4,12},{12,4},... | collective-permute-start | bytes 393224 | tf_op jit(solution)/shard_map/ppermute | solution.py:29
  4.3 1.0 %collective-permute-done = bf16[256,256]{1,0:T(8,128)(2,1)S(1)} collective-permute-done((bf16[256,256]{1,0:T(8,128)(2,1)S(1)}, bf16[256,256]{1,0:T(8,128)(2,1)S(1)}, u32[]{:S(2)}, u32[]{:S(2)}) %collective-permute-start) | collective-permute-done | bytes 131104 | tf_op jit(solution)/shard_map/ppermute | solution.py:29
  5.3 0.0 copy-start
  5.3 0.0 copy-start.2
  5.3 0.0 copy-start.11
  5.3 2.9 %collective-permute-start.1 = (bf16[128,256]{1,0:T(8,128)(2,1)S(1)}, bf16[128,256]{1,0:T(8,128)(2,1)S(1)}, u32[]{:S(2)}, u32[]{:S(2)}) collective-permute-start(bf16[128,256]{1,0:T(8,128)(2,1)S(1)} %select_convert_fusion.after_ref), channel_id=1, source_target_pairs={{0,1},{1,0},{2,3},{3,2},{4,5},{5,4},{6,7},{7,6},{8,9},{9,8},{10,11... | collective-permute-start | bytes 196616 | tf_op jit(solution)/shard_map/ppermute | solution.py:29
  8.3 0.0 copy-done.1
  8.3 0.0 copy-done.4
  8.3 0.0 copy-done.5
  8.3 0.0 copy-done.9
  8.3 1.5 %outgoing.1 = (bf16[1536,256]{1,0:T(8,128)(2,1)S(1)}, bf16[64,256]{1,0:T(8,128)(2,1)S(1)}) custom-call(s32[1]{0:T(128)} %bitcast.me_ref, s32[1,8]{1,0:T(1,128)S(1)} %copy-done.9, bf16[1536,256]{1,0:T(8,128)(2,1)S(1)} %get-tuple-element.11.grad_ref, bf16[256,256]{1,0:T(8,128)(2,1)S(1)} %copy-done.1, s32[8,4,8]{2,1,0:T(4,128)S(1)} %bitcast.46, ...), custom_call_target="tpu_custom_call" | custom-call | tf_op jit(solution)/shard_map/outgoing/pallas_call | solution.py:274
  9.8 0.9 %collective-permute-done.1 = bf16[128,256]{1,0:T(8,128)(2,1)S(1)} collective-permute-done((bf16[128,256]{1,0:T(8,128)(2,1)S(1)}, bf16[128,256]{1,0:T(8,128)(2,1)S(1)}, u32[]{:S(2)}, u32[]{:S(2)}) %collective-permute-start.1) | collective-permute-done | bytes 65568 | tf_op jit(solution)/shard_map/ppermute | solution.py:29
  10.7 2.0 %collective-permute-start.2 = (bf16[160,256]{1,0:T(8,128)(2,1)S(1)}, bf16[160,256]{1,0:T(8,128)(2,1)S(1)}, u32[]{:S(2)}, u32[]{:S(2)}) collective-permute-start(bf16[160,256]{1,0:T(8,128)(2,1)S(1)} %pad_maximum_fusion), channel_id=1, source_target_pairs={{0,2},{1,3},{2,0},{3,1},{4,6},{5,7},{6,4},{7,5},{8,10},{9,11},{10,... | collective-permute-start | bytes 245768 | tf_op jit(solution)/shard_map/ppermute | solution.py:29
  14.0 0.0 copy-done.3
  14.0 0.0 copy-done.7
  14.0 0.0 copy-done.8
  14.0 0.3 %stale_rows.1 = (bf16[64,256]{1,0:T(8,128)(2,1)S(1)}, bf16[1,32,256]{2,1,0:T(8,128)(2,1)S(1)}) custom-call(s32[1]{0:T(128)S(6)} %copy.26.version_ref, s32[1]{0:T(128)S(6)} %copy.27.count_ref, bf16[2,64,256]{2,1,0:T(8,128)(2,1)S(1)} %bitcast.44, bf16[256,256]{1,0:T(8,128)(2,1)S(1)} %copy-done.1, ...), custom_call_target="tpu_custom_call", output_to_operand_aliasing={{1}: (6, {})} | custom-call | tf_op jit(solution)/shard_map/stale_rows/pallas_call | solution.py:298
  14.4 0.8 %collective-permute-done.2 = bf16[160,256]{1,0:T(8,128)(2,1)S(1)} collective-permute-done((bf16[160,256]{1,0:T(8,128)(2,1)S(1)}, bf16[160,256]{1,0:T(8,128)(2,1)S(1)}, u32[]{:S(2)}, u32[]{:S(2)}) %collective-permute-start.2) | collective-permute-done | bytes 81952 | tf_op jit(solution)/shard_map/ppermute | solution.py:29
  15.3 3.0 %collective-permute-start.3 = (bf16[160,256]{1,0:T(8,128)(2,1)S(1)}, bf16[160,256]{1,0:T(8,128)(2,1)S(1)}, u32[]{:S(2)}, u32[]{:S(2)}) collective-permute-start(bf16[160,256]{1,0:T(8,128)(2,1)S(1)} %pad_maximum_fusion.1), channel_id=1, source_target_pairs={{0,4},{1,5},{2,6},{3,7},{4,0},{5,1},{6,2},{7,3},{8,12},{9,13},{10,... | collective-permute-start | bytes 245768 | tf_op jit(solution)/shard_map/ppermute | solution.py:29
  18.3 0.0 copy-done
  18.3 0.0 copy-done.2
  18.3 0.0 copy-done.11
  18.3 0.0 copy-start.6
  18.3 0.0 copy-start.10
  18.3 2.1 %local_term.1 = (f32[12,128,256]{2,1,0:T(8,128)S(1)}, bf16[2,16,256]{2,1,0:T(8,128)(2,1)S(1)}) custom-call(s32[1,48]{1,0:T(1,128)S(1)} %copy-done.11, bf16[1536,256]{1,0:T(8,128)(2,1)S(1)} %get-tuple-element.11.grad_ref, bf16[1536,256]{1,0:T(8,128)(2,1)S(1)} %get-tuple-element.14.neigh_ref, ...), custom_call_target="tpu_custom_call", output_to_operand_aliasing={{1}: (5, {})} | custom-call | tf_op jit(solution)/shard_map/local_term/pallas_call | solution.py:320
  20.4 0.3 %collective-permute-done.3 = bf16[160,256]{1,0:T(8,128)(2,1)S(1)} collective-permute-done((bf16[160,256]{1,0:T(8,128)(2,1)S(1)}, bf16[160,256]{1,0:T(8,128)(2,1)S(1)}, u32[]{:S(2)}, u32[]{:S(2)}) %collective-permute-start.3) | collective-permute-done | bytes 81952 | tf_op jit(solution)/shard_map/ppermute | solution.py:29
  20.8 1.9 %collective-permute-start.4 = (bf16[160,256]{1,0:T(8,128)(2,1)S(1)}, bf16[160,256]{1,0:T(8,128)(2,1)S(1)}, u32[]{:S(2)}, u32[]{:S(2)}) collective-permute-start(bf16[160,256]{1,0:T(8,128)(2,1)S(1)} %pad_maximum_fusion.2), channel_id=1, source_target_pairs={{0,1},{1,0},{2,3},{3,2},{4,5},{5,4},{6,7},{7,6},{8,9},{9,8},{10,11... | collective-permute-start | bytes 245768 | tf_op jit(solution)/shard_map/ppermute | solution.py:29
  22.7 0.0 collective-permute-start.5
  22.7 2.6 %collective-permute-done.4 = bf16[160,256]{1,0:T(8,128)(2,1)S(1)} collective-permute-done((bf16[160,256]{1,0:T(8,128)(2,1)S(1)}, bf16[160,256]{1,0:T(8,128)(2,1)S(1)}, u32[]{:S(2)}, u32[]{:S(2)}) %collective-permute-start.4) | collective-permute-done | bytes 81952 | tf_op jit(solution)/shard_map/ppermute | solution.py:29
  25.4 0.1 collective-permute-start.6
  25.5 0.0 collective-permute-done.5.stale_ref
  25.5 0.0 copy-done.6
  25.5 0.0 copy-done.10
  25.5 1.2 %finish.1 = bf16[1536,256]{1,0:T(8,128)(2,1)} custom-call(s32[1]{0:T(128)} %bitcast.me_ref, f32[12,128,256]{2,1,0:T(8,128)S(1)} %get-tuple-element.17.base_ref, bf16[64,256]{1,0:T(8,128)(2,1)S(1)} %bitcast.43, bf16[64,256]{1,0:T(8,128)(2,1)S(1)} %collective-permute-done.5.stale_ref, s32[8,8]{1,0:T(8,128)S(1)} %bitcast.48, s32[1,64]{1,0:T(1,128)S(1)} %copy-done.10), custom_call_target="tpu_custom_call" | custom-call | tf_op jit(solution)/shard_map/finish/pallas_call | solution.py:342
  26.7 0.0 collective-permute-done.6
  26.8 0.7 %maximum_select_fusion = bf16[2,256,256]{2,1,0:T(8,128)(2,1)} fusion(bf16[1,256,256]{2,1,0:T(8,128)(2,1)S(1)} %bitcast.52, bf16[1,256,256]{2,1,0:T(8,128)(2,1)S(1)} %maximum_select_fusion.1, pred[]{:T(512)S(6)} %eq.7), kind=kLoop, calls=%fused_computation | loop fusion | flops 393216 | bytes 524289 | tf_op jit(solution)/shard_map/jit(_where)/select_n | solution.py:340
  (22 shorter events, 0.3 us)
Async XLA Ops:
  0.6 7.6 %copy-start.1 = (bf16[256,256]{1,0:T(8,128)(2,1)S(1)}, bf16[256,256]{1,0:T(8,128)(2,1)}, u32[]{:S(2)}) copy-start(bf16[256,256]{1,0:T(8,128)(2,1)} %weight_ref.4) | copy-start | bytes 393220
  0.6 7.6 %copy-start.4 = (s32[1,8,8,4]{2,3,1,0:T(4,128)S(1)}, s32[1,8,8,4]{2,3,1,0:T(4,128)}, u32[]{:S(2)}) copy-start(s32[1,8,8,4]{2,3,1,0:T(4,128)} %param.24) | copy-start | bytes 3076
  0.7 7.6 %copy-start.5 = (f32[1,8,8,4]{2,3,1,0:T(4,128)S(1)}, f32[1,8,8,4]{2,3,1,0:T(4,128)}, u32[]{:S(2)}) copy-start(f32[1,8,8,4]{2,3,1,0:T(4,128)} %param.25) | copy-start | bytes 3076
  0.7 7.6 %copy-start.9 = (s32[1,8]{1,0:T(1,128)S(1)}, s32[1,8]{1,0:T(1,128)}, u32[]{:S(2)}) copy-start(s32[1,8]{1,0:T(1,128)} %count_ref.2) | copy-start | bytes 100
  3.7 10.3 %copy-start.3 = (bf16[1,2,64,256]{3,2,1,0:T(8,128)(2,1)S(1)}, bf16[1,2,64,256]{3,2,1,0:T(8,128)(2,1)}, u32[]{:S(2)}) copy-start(bf16[1,2,64,256]{3,2,1,0:T(8,128)(2,1)} %param.28) | copy-start | bytes 196612
  3.8 10.3 %copy-start.7 = (s32[1,64,4]{1,2,0:T(4,128)S(1)}, s32[1,64,4]{1,2,0:T(4,128)}, u32[]{:S(2)}) copy-start(s32[1,64,4]{1,2,0:T(4,128)} %param.30) | copy-start | bytes 3076
  3.8 10.3 %copy-start.8 = (f32[1,64,4]{1,2,0:T(4,128)S(1)}, f32[1,64,4]{1,2,0:T(4,128)}, u32[]{:S(2)}) copy-start(f32[1,64,4]{1,2,0:T(4,128)} %param.31) | copy-start | bytes 3076
  3.8 1.5 %collective-permute-start = (bf16[256,256]{1,0:T(8,128)(2,1)S(1)}, bf16[256,256]{1,0:T(8,128)(2,1)S(1)}, u32[]{:S(2)}, u32[]{:S(2)}) collective-permute-start(bf16[256,256]{1,0:T(8,128)(2,1)S(1)} %get-tuple-element.13), channel_id=1, source_target_pairs={{0,8},{8,0},{1,9},{9,1},{2,10},{10,2},{3,11},{11,3},{4,12},{12,4},... | collective-permute-start | bytes 393224 | tf_op jit(solution)/shard_map/ppermute | solution.py:29
  5.3 13.0 %copy-start = (bf16[1,48,128,128]{3,2,1,0:T(8,128)(2,1)S(1)}, bf16[1,48,128,128]{3,2,1,0:T(8,128)(2,1)}, u32[]{:S(2)}) copy-start(bf16[1,48,128,128]{3,2,1,0:T(8,128)(2,1)} %param.22) | copy-start | bytes 4718596
  5.3 13.0 %copy-start.2 = (bf16[256,256]{1,0:T(8,128)(2,1)S(1)}, bf16[256,256]{1,0:T(8,128)(2,1)}, u32[]{:S(2)}) copy-start(bf16[256,256]{1,0:T(8,128)(2,1)} %weight_ref.5) | copy-start | bytes 393220
  5.3 13.0 %copy-start.11 = (s32[1,48]{1,0:T(1,128)S(1)}, s32[1,48]{1,0:T(1,128)}, u32[]{:S(2)}) copy-start(s32[1,48]{1,0:T(1,128)} %source_ref.1) | copy-start | bytes 580
  5.3 5.3 %collective-permute-start.1 = (bf16[128,256]{1,0:T(8,128)(2,1)S(1)}, bf16[128,256]{1,0:T(8,128)(2,1)S(1)}, u32[]{:S(2)}, u32[]{:S(2)}) collective-permute-start(bf16[128,256]{1,0:T(8,128)(2,1)S(1)} %select_convert_fusion.after_ref), channel_id=1, source_target_pairs={{0,1},{1,0},{2,3},{3,2},{4,5},{5,4},{6,7},{7,6},{8,9},{9,8},{10,11... | collective-permute-start | bytes 196616 | tf_op jit(solution)/shard_map/ppermute | solution.py:29
  10.7 4.5 %collective-permute-start.2 = (bf16[160,256]{1,0:T(8,128)(2,1)S(1)}, bf16[160,256]{1,0:T(8,128)(2,1)S(1)}, u32[]{:S(2)}, u32[]{:S(2)}) collective-permute-start(bf16[160,256]{1,0:T(8,128)(2,1)S(1)} %pad_maximum_fusion), channel_id=1, source_target_pairs={{0,2},{1,3},{2,0},{3,1},{4,6},{5,7},{6,4},{7,5},{8,10},{9,11},{10,... | collective-permute-start | bytes 245768 | tf_op jit(solution)/shard_map/ppermute | solution.py:29
  15.3 5.4 %collective-permute-start.3 = (bf16[160,256]{1,0:T(8,128)(2,1)S(1)}, bf16[160,256]{1,0:T(8,128)(2,1)S(1)}, u32[]{:S(2)}, u32[]{:S(2)}) collective-permute-start(bf16[160,256]{1,0:T(8,128)(2,1)S(1)} %pad_maximum_fusion.1), channel_id=1, source_target_pairs={{0,4},{1,5},{2,6},{3,7},{4,0},{5,1},{6,2},{7,3},{8,12},{9,13},{10,... | collective-permute-start | bytes 245768 | tf_op jit(solution)/shard_map/ppermute | solution.py:29
  18.3 7.2 %copy-start.6 = (s32[1,8,8]{2,1,0:T(8,128)S(1)}, s32[1,8,8]{2,1,0:T(8,128)}, u32[]{:S(2)}) copy-start(s32[1,8,8]{2,1,0:T(8,128)} %param.27) | copy-start | bytes 772
  18.3 7.2 %copy-start.10 = (s32[1,64]{1,0:T(1,128)S(1)}, s32[1,64]{1,0:T(1,128)}, u32[]{:S(2)}) copy-start(s32[1,64]{1,0:T(1,128)} %cross_ref.1) | copy-start | bytes 772
  20.8 4.5 %collective-permute-start.4 = (bf16[160,256]{1,0:T(8,128)(2,1)S(1)}, bf16[160,256]{1,0:T(8,128)(2,1)S(1)}, u32[]{:S(2)}, u32[]{:S(2)}) collective-permute-start(bf16[160,256]{1,0:T(8,128)(2,1)S(1)} %pad_maximum_fusion.2), channel_id=1, source_target_pairs={{0,1},{1,0},{2,3},{3,2},{4,5},{5,4},{6,7},{7,6},{8,9},{9,8},{10,11... | collective-permute-start | bytes 245768 | tf_op jit(solution)/shard_map/ppermute | solution.py:29
  22.7 2.8 %collective-permute-start.5 = (bf16[64,256]{1,0:T(8,128)(2,1)S(1)}, bf16[64,256]{1,0:T(8,128)(2,1)S(1)}, u32[]{:S(2)}, u32[]{:S(2)}) collective-permute-start(bf16[64,256]{1,0:T(8,128)(2,1)S(1)} %get-tuple-element.19), channel_id=1, source_target_pairs={{0,8},{8,0},{1,9},{9,1},{2,10},{10,2},{3,11},{11,3},{4,12},{12,4},... | collective-permute-start | bytes 98312 | tf_op jit(solution)/shard_map/ppermute | solution.py:29
  25.4 1.4 %collective-permute-start.6 = (bf16[256,256]{1,0:T(8,128)(2,1)S(1)}, bf16[256,256]{1,0:T(8,128)(2,1)S(1)}, u32[]{:S(2)}, u32[]{:S(2)}) collective-permute-start(bf16[256,256]{1,0:T(8,128)(2,1)S(1)} %maximum_select_fusion.2), channel_id=1, source_target_pairs={{0,8},{8,0},{1,9},{9,1},{2,10},{10,2},{3,11},{11,3},{4,12},{12,4},... | collective-permute-start | bytes 393224 | tf_op jit(solution)/shard_map/ppermute | solution.py:29

commit v3 on v2

--- a/solution.py
+++ b/solution.py
@@ -17,7 +17,7 @@
 TN = (((0,), (0,)), ((), ()))
 PARTS = 2
 CHUNKS = 3
-OUT_BLOCKS = 4
+OUT_BLOCKS = 2
 
 
 def in_hbm(*values):
@@ -53,24 +53,21 @@
 
 
 def gradient_kernel(
-    host_ref,
     features_hbm,
     aggregated_hbm,
     cotangent_hbm,
     self_hbm,
     neigh_hbm,
+    inputs_ref,
     grad_ref,
-    kept_ref,
     given_ref,
-    features,
-    aggregated,
     cotangent,
     self_weight,
     neigh_weight,
-    sums,
+    turned,
     sems,
 ):
-    part_rows = features.shape[0] // PARTS
+    part_rows = cotangent.shape[0] // PARTS
     rows = part_rows // CHUNKS
     copies = []
 
@@ -83,35 +80,37 @@
     fetch(neigh_hbm, neigh_weight)
     for p in range(PARTS):
         part = pl.ds(p * part_rows, part_rows)
-        fetch(features_hbm.at[part], features.at[part])
-        fetch(aggregated_hbm.at[part], aggregated.at[part])
+        fetch(features_hbm.at[part], inputs_ref.at[0, part])
+        fetch(aggregated_hbm.at[part], inputs_ref.at[1, part])
         fetch(cotangent_hbm.at[part], cotangent.at[part])
     copies[0].wait()
     copies[1].wait()
+    other = 1 - lax.axis_index("hst")
     for p in range(PARTS):
         for copy in copies[3 * p + 2 : 3 * p + 5]:
             copy.wait()
         for c in range(CHUNKS):
             part = pl.ds(p * part_rows + c * rows, rows)
-            left, right = features[part, :], aggregated[part, :]
+            left, right = inputs_ref[0, part, :], inputs_ref[1, part, :]
             preact = jnp.dot(left, self_weight[...], preferred_element_type=F32) + jnp.dot(
                 right, neigh_weight[...], preferred_element_type=F32
             )
             grad = (cotangent[part, :].astype(F32) * silu_slope(preact)).astype(BF16)
             grad_ref[part, :] = grad
-            for i, values in enumerate((left, right)):
-                term = lax.dot_general(values, grad, TN, preferred_element_type=F32)
-                if p == 0 and c == 0:
-                    sums[i] = term
-                else:
-                    sums[i] += term
-    host = host_ref[0]
-    kept_ref[...] = sums[host]
-    given_ref[...] = sums[1 - host].astype(BF16)
+            turned[:, part] = jnp.where(other == 0, left, right).T
+    given_ref[...] = jnp.dot(
+        turned[...], grad_ref[...], preferred_element_type=F32
+    ).astype(BF16)
+
+
+def kept_kernel(inputs_ref, grad_ref, after_ref, kept_ref):
+    host = lax.axis_index("hst")
+    kept_ref[...] = lax.dot_general(
+        inputs_ref[host], grad_ref[...], TN, preferred_element_type=F32
+    )
 
 
 def outgoing_kernel(
-    me_ref,
     count_ref,
     grad_ref,
     weight_ref,
@@ -122,7 +121,7 @@
     out_ref,
 ):
     peers, fan, cap = source_ref.shape
-    me = me_ref[0]
+    me = lax.axis_index("dom")
     neigh = lax.dot_general(grad_ref[...], weight_ref[...], NT, preferred_element_type=F32)
     neigh = neigh.astype(BF16)
     neigh_ref[...] = neigh
@@ -188,9 +187,9 @@
 
 
 def finish_kernel(
-    me_ref, base_ref, fresh_ref, stale_ref, recv_ref, cross_ref, out_hbm, out, sems
-):
-    me = me_ref[0]
+    base_ref, fresh_ref, stale_ref, recv_ref, cross_ref, out_hbm, out, sems
+):
+    me = lax.axis_index("dom")
     blocks = base_ref.shape[0]
     peers, cap = recv_ref.shape
     targets = [recv_ref[pl.ds(jnp.bitwise_xor(me, o), 1), :] for o in hop_order(peers)]
@@ -212,6 +211,18 @@
         copy.wait()
 
 
+def sums_kernel(mine_ref, other_ref, out_hbm, sems):
+    host = lax.axis_index("hst")
+    copies = [
+        pltpu.make_async_copy(mine_ref, out_hbm.at[host], sems.at[0]),
+        pltpu.make_async_copy(other_ref, out_hbm.at[1 - host], sems.at[1]),
+    ]
+    for copy in copies:
+        copy.start()
+    for copy in copies:
+        copy.wait()
+
+
 def body(
     features,
     aggregated,
@@ -238,32 +249,37 @@
     bits = peers.bit_length() - 1
     host = lax.axis_index("hst")
     me = lax.axis_index("dom")
-    me_ref = me.astype(jnp.int32).reshape(1)
-    host_ref = host.astype(jnp.int32).reshape(1)
     odd = (me & 1) == 1
     struct = jax.ShapeDtypeStruct
 
-    pre_grad, own, given = pl.pallas_call(
+    inputs, pre_grad, given = pl.pallas_call(
         gradient_kernel,
         out_shape=(
+            pltpu.VMEM((2, row_count, dim), BF16),
             pltpu.VMEM((row_count, dim), BF16),
-            pltpu.VMEM((dim, dim), F32),
             pltpu.VMEM((dim, dim), BF16),
         ),
-        in_specs=[SMEM, ANY, ANY, ANY, ANY, ANY],
+        in_specs=[ANY] * 5,
         out_specs=(VMEM, VMEM, VMEM),
         scratch_shapes=[
             pltpu.VMEM((row_count, dim), BF16),
-            pltpu.VMEM((row_count, dim), BF16),
-            pltpu.VMEM((row_count, dim), BF16),
             pltpu.VMEM((dim, dim), BF16),
             pltpu.VMEM((dim, dim), BF16),
-            pltpu.VMEM((2, dim, dim), F32),
+            pltpu.VMEM((dim, row_count), BF16),
             pltpu.SemaphoreType.DMA((2 + 3 * PARTS,)),
         ],
         compiler_params=PARAMS,
         name="gradients",
-    )(host_ref, *in_hbm(features, aggregated, cotangent, w_self, w_neigh))
+    )(*in_hbm(features, aggregated, cotangent, w_self, w_neigh))
+    own = pl.pallas_call(
+        kept_kernel,
+        out_shape=pltpu.VMEM((dim, dim), F32),
+        in_specs=[VMEM, VMEM, ANY],
+        out_specs=VMEM,
+        compiler_params=PARAMS,
+        name="kept_sum",
+    )(inputs, pre_grad, given)
+
     first = host == 0
     half = own + swap(given, "hst", 0).astype(F32)
     quarter = dim // 2
@@ -274,12 +290,11 @@
     neigh_grad, outgoing = pl.pallas_call(
         outgoing_kernel,
         out_shape=(struct((row_count, dim), BF16), struct((peers * cap, dim), BF16)),
-        in_specs=[SMEM, SMEM, VMEM, VMEM, VMEM, VMEM, ANY],
+        in_specs=[SMEM, VMEM, VMEM, VMEM, VMEM, ANY],
         out_specs=(VMEM, VMEM),
         compiler_params=PARAMS,
         name="outgoing",
     )(
-        me_ref,
         send_count,
         pre_grad,
         w_neigh,
@@ -337,12 +352,20 @@
         odd, jnp.concatenate([other, given], axis=0), jnp.concatenate([given, other], axis=0)
     )
     other = swap(mine, "hst", 0)
-    sums = jnp.where(first, jnp.stack([mine, other]), jnp.stack([other, mine]))
+    sums = pl.pallas_call(
+        sums_kernel,
+        out_shape=struct((2, dim, dim), BF16),
+        in_specs=[VMEM, VMEM],
+        out_specs=ANY,
+        scratch_shapes=[pltpu.SemaphoreType.DMA((2,))],
+        compiler_params=PARAMS,
+        name="weight_grads",
+    )(mine, other)
 
     out_rows = pl.pallas_call(
         finish_kernel,
         out_shape=struct((row_count, dim), BF16),
-        in_specs=[SMEM, VMEM, VMEM, VMEM, VMEM, VMEM],
+        in_specs=[VMEM] * 5,
         out_specs=ANY,
         scratch_shapes=[
             pltpu.VMEM((row_count, dim), BF16),
@@ -350,7 +373,7 @@
         ],
         compiler_params=PARAMS,
         name="finish",
-    )(me_ref, base, held.reshape(peers * cap, dim), stale_in, recv_rows[0], cross_rows)
+    )(base, held.reshape(peers * cap, dim), stale_in, recv_rows[0], cross_rows)
     return (out_rows, sums)
 
 

time: 27.9 us -> 27.5 us (0.986)
  Pallas kernels: 8.17 us -> 8.94 us
  other arithmetic: 0.95 us -> 0.19 us
  waiting for transfers between devices: 5.63 us -> 5.21 us
    pallas_call x1 -> x3, Pallas kernels: 3.06 us -> 3.89 us  [the longest x1 2.75 us: body(): pl.pallas_call(gradient_kernel, out_shape=(pltpu.VMEM((2, row_count, dim)...]
    select_n x1 -> x0, other arithmetic: 0.73 us -> none  [body(): sums = jnp.where(first, jnp.stack([mine, other]), jnp.stack([other, mine]))]
    ppermute x7, waiting for transfers between devices: 5.63 us -> 5.21 us  [swap(): return lax.ppermute(value, axis, pairs)]
  transfers between devices with their start and end apart: 7 -> 7, of which waited for: 5 -> 6; matrix products, arithmetic and copies ran while one was open for 0% -> 0% of each run, Pallas kernels for 19% -> 20%
where the time goes in v3:
time: 27.5 us; the launch traced here: 27.1 us
  starting transfers between devices  10.4 us (38%)
  Pallas kernels  8.94 us (33%)
  waiting for transfers between devices  5.21 us (19%)
  between operations  2.22 us (8%)
    ppermute x7, starting transfers between devices, swap(): return lax.ppermute(value, axis, pairs)  10.4 us
    ppermute x7, waiting for transfers between devices, swap(): return lax.ppermute(value, axis, pairs)  5.21 us
    pallas_call x1, Pallas kernels, body(): pl.pallas_call(gradient_kernel, out_shape=(pltpu.VMEM((2, row_count, dim)...  2.75 us
    pallas_call x1, Pallas kernels, body(): pl.pallas_call(local_kernel, out_shape=(struct((blocks, 128, dim), F32),...  2.02 us
    pallas_call x1, Pallas kernels, body(): pl.pallas_call(outgoing_kernel, out_shape=(struct((row_count, dim), BF16)...  1.52 us
    pallas_call x1, Pallas kernels, body(): pl.pallas_call(finish_kernel, out_shape=struct((row_count, dim), BF16), i...  1.18 us
    pallas_call x1, Pallas kernels, body(): pl.pallas_call(sums_kernel, out_shape=struct((2, dim, dim), BF16), in_spe...  0.71 us
  transfers between devices with their start and end apart: 7, of which 6 were waited for; matrix products, arithmetic and copies ran while one was open for 0% of the time, Pallas kernels for 20%

profile of v3, /device:TPU:0, one launch (start us, length us, event | category | flops | bytes accessed | tf_op | source)
XLA Modules:
  0.0 27.1 jit_solution(14828359326845098488)
XLA Ops:
  0.6 2.7 %gradients.1 = (bf16[2,1536,256]{2,1,0:T(8,128)(2,1)S(1)}, bf16[1536,256]{1,0:T(8,128)(2,1)S(1)}, bf16[256,256]{1,0:T(8,128)(2,1)S(1)}) custom-call(bf16[1536,256]{1,0:T(8,128)(2,1)} %features_hbm.1, bf16[1536,256]{1,0:T(8,128)(2,1)} %aggregated_hbm.1, bf16[1536,256]{1,0:T(8,128)(2,1)} %cotangent_hbm.1, bf16[256,256]{1,0:T(8,128)(2,1)} %weight_ref.5, ...), custom_call_target="tpu_custom_call" | custom-call | tf_op jit(solution)/shard_map/gradients/pallas_call | solution.py:255
  3.4 0.5 %collective-permute-start = (bf16[256,256]{1,0:T(8,128)(2,1)S(1)}, bf16[256,256]{1,0:T(8,128)(2,1)S(1)}, u32[]{:S(2)}, u32[]{:S(2)}) collective-permute-start(bf16[256,256]{1,0:T(8,128)(2,1)S(1)} %get-tuple-element.13.after_ref), channel_id=1, source_target_pairs={{0,8},{8,0},{1,9},{9,1},{2,10},{10,2},{3,11},{11,3},{4,12},{12,4},... | collective-permute-start | bytes 393224 | tf_op jit(solution)/shard_map/ppermute | solution.py:29
  3.9 0.0 copy-start.1
  3.9 0.0 copy-start.4
  3.9 0.0 copy-start.5
  3.9 0.0 copy-start.9
  3.9 0.4 %kept_sum.1 = f32[256,256]{1,0:T(8,128)S(1)} custom-call(bf16[2,1536,256]{2,1,0:T(8,128)(2,1)S(1)} %get-tuple-element.12.inputs_ref, bf16[1536,256]{1,0:T(8,128)(2,1)S(1)} %get-tuple-element.11.grad_ref, bf16[256,256]{1,0:T(8,128)(2,1)S(1)} %get-tuple-element.13.after_ref), custom_call_target="tpu_custom_call" | custom-call | tf_op jit(solution)/shard_map/kept_sum/pallas_call | solution.py:274
  4.3 0.0 copy-start.3
  4.4 0.0 copy-start.7
  4.4 0.0 copy-start.8
  4.4 0.0 copy-start
  4.4 0.0 copy-start.2
  4.4 0.0 copy-start.10
  4.4 0.5 %collective-permute-done = bf16[256,256]{1,0:T(8,128)(2,1)S(1)} collective-permute-done((bf16[256,256]{1,0:T(8,128)(2,1)S(1)}, bf16[256,256]{1,0:T(8,128)(2,1)S(1)}, u32[]{:S(2)}, u32[]{:S(2)}) %collective-permute-start) | collective-permute-done | bytes 131104 | tf_op jit(solution)/shard_map/ppermute | solution.py:29
  4.9 2.9 %collective-permute-start.1 = (bf16[128,256]{1,0:T(8,128)(2,1)S(1)}, bf16[128,256]{1,0:T(8,128)(2,1)S(1)}, u32[]{:S(2)}, u32[]{:S(2)}) collective-permute-start(bf16[128,256]{1,0:T(8,128)(2,1)S(1)} %select_convert_fusion.after_ref), channel_id=1, source_target_pairs={{0,1},{1,0},{2,3},{3,2},{4,5},{5,4},{6,7},{7,6},{8,9},{9,8},{10,11... | collective-permute-start | bytes 196616 | tf_op jit(solution)/shard_map/ppermute | solution.py:29
  7.9 0.0 copy-done.1
  7.9 0.0 copy-done.4
  7.9 0.0 copy-done.5
  7.9 0.0 copy-done.9
  7.9 1.5 %outgoing.1 = (bf16[1536,256]{1,0:T(8,128)(2,1)S(1)}, bf16[64,256]{1,0:T(8,128)(2,1)S(1)}) custom-call(s32[1,8]{1,0:T(1,128)S(1)} %copy-done.9, bf16[1536,256]{1,0:T(8,128)(2,1)S(1)} %get-tuple-element.11.grad_ref, bf16[256,256]{1,0:T(8,128)(2,1)S(1)} %copy-done.1, s32[8,4,8]{2,1,0:T(4,128)S(1)} %bitcast.40, f32[8,4,8]{2,1,0:T(4,128)S(1)} %bitcast.41, ...), custom_call_target="tpu_custom_call" | custom-call | tf_op jit(solution)/shard_map/outgoing/pallas_call | solution.py:290
  9.4 0.9 %collective-permute-done.1 = bf16[128,256]{1,0:T(8,128)(2,1)S(1)} collective-permute-done((bf16[128,256]{1,0:T(8,128)(2,1)S(1)}, bf16[128,256]{1,0:T(8,128)(2,1)S(1)}, u32[]{:S(2)}, u32[]{:S(2)}) %collective-permute-start.1) | collective-permute-done | bytes 65568 | tf_op jit(solution)/shard_map/ppermute | solution.py:29
  10.3 2.0 %collective-permute-start.2 = (bf16[160,256]{1,0:T(8,128)(2,1)S(1)}, bf16[160,256]{1,0:T(8,128)(2,1)S(1)}, u32[]{:S(2)}, u32[]{:S(2)}) collective-permute-start(bf16[160,256]{1,0:T(8,128)(2,1)S(1)} %pad_maximum_fusion), channel_id=1, source_target_pairs={{0,2},{1,3},{2,0},{3,1},{4,6},{5,7},{6,4},{7,5},{8,10},{9,11},{10,... | collective-permute-start | bytes 245768 | tf_op jit(solution)/shard_map/ppermute | solution.py:29
  13.6 0.0 copy-done.3
  13.6 0.0 copy-done.7
  13.6 0.0 copy-done.8
  13.6 0.3 %stale_rows.1 = (bf16[64,256]{1,0:T(8,128)(2,1)S(1)}, bf16[1,32,256]{2,1,0:T(8,128)(2,1)S(1)}) custom-call(s32[1]{0:T(128)S(6)} %copy.26.version_ref, s32[1]{0:T(128)S(6)} %copy.27.count_ref, bf16[2,64,256]{2,1,0:T(8,128)(2,1)S(1)} %bitcast.38, bf16[256,256]{1,0:T(8,128)(2,1)S(1)} %copy-done.1, ...), custom_call_target="tpu_custom_call", output_to_operand_aliasing={{1}: (6, {})} | custom-call | tf_op jit(solution)/shard_map/stale_rows/pallas_call | solution.py:313
  14.0 0.8 %collective-permute-done.2 = bf16[160,256]{1,0:T(8,128)(2,1)S(1)} collective-permute-done((bf16[160,256]{1,0:T(8,128)(2,1)S(1)}, bf16[160,256]{1,0:T(8,128)(2,1)S(1)}, u32[]{:S(2)}, u32[]{:S(2)}) %collective-permute-start.2) | collective-permute-done | bytes 81952 | tf_op jit(solution)/shard_map/ppermute | solution.py:29
  14.9 3.0 %collective-permute-start.3 = (bf16[160,256]{1,0:T(8,128)(2,1)S(1)}, bf16[160,256]{1,0:T(8,128)(2,1)S(1)}, u32[]{:S(2)}, u32[]{:S(2)}) collective-permute-start(bf16[160,256]{1,0:T(8,128)(2,1)S(1)} %pad_maximum_fusion.1), channel_id=1, source_target_pairs={{0,4},{1,5},{2,6},{3,7},{4,0},{5,1},{6,2},{7,3},{8,12},{9,13},{10,... | collective-permute-start | bytes 245768 | tf_op jit(solution)/shard_map/ppermute | solution.py:29
  17.9 0.0 copy-done
  17.9 0.0 copy-done.2
  17.9 0.0 copy-done.10
  17.9 0.0 copy-start.6
  17.9 0.0 copy-start.11
  17.9 2.0 %local_term.1 = (f32[12,128,256]{2,1,0:T(8,128)S(1)}, bf16[2,16,256]{2,1,0:T(8,128)(2,1)S(1)}) custom-call(s32[1,48]{1,0:T(1,128)S(1)} %copy-done.10, bf16[1536,256]{1,0:T(8,128)(2,1)S(1)} %get-tuple-element.11.grad_ref, bf16[1536,256]{1,0:T(8,128)(2,1)S(1)} %get-tuple-element.14.neigh_ref, ...), custom_call_target="tpu_custom_call", output_to_operand_aliasing={{1}: (5, {})} | custom-call | tf_op jit(solution)/shard_map/local_term/pallas_call | solution.py:335
  20.0 0.4 %collective-permute-done.3 = bf16[160,256]{1,0:T(8,128)(2,1)S(1)} collective-permute-done((bf16[160,256]{1,0:T(8,128)(2,1)S(1)}, bf16[160,256]{1,0:T(8,128)(2,1)S(1)}, u32[]{:S(2)}, u32[]{:S(2)}) %collective-permute-start.3) | collective-permute-done | bytes 81952 | tf_op jit(solution)/shard_map/ppermute | solution.py:29
  20.4 1.9 %collective-permute-start.4 = (bf16[160,256]{1,0:T(8,128)(2,1)S(1)}, bf16[160,256]{1,0:T(8,128)(2,1)S(1)}, u32[]{:S(2)}, u32[]{:S(2)}) collective-permute-start(bf16[160,256]{1,0:T(8,128)(2,1)S(1)} %pad_maximum_fusion.2), channel_id=1, source_target_pairs={{0,1},{1,0},{2,3},{3,2},{4,5},{5,4},{6,7},{7,6},{8,9},{9,8},{10,11... | collective-permute-start | bytes 245768 | tf_op jit(solution)/shard_map/ppermute | solution.py:29
  22.3 0.0 collective-permute-start.5
  22.3 2.6 %collective-permute-done.4 = bf16[160,256]{1,0:T(8,128)(2,1)S(1)} collective-permute-done((bf16[160,256]{1,0:T(8,128)(2,1)S(1)}, bf16[160,256]{1,0:T(8,128)(2,1)S(1)}, u32[]{:S(2)}, u32[]{:S(2)}) %collective-permute-start.4) | collective-permute-done | bytes 81952 | tf_op jit(solution)/shard_map/ppermute | solution.py:29
  25.0 0.1 collective-permute-start.6
  25.1 0.0 collective-permute-done.5.stale_ref
  25.1 0.0 copy-done.6
  25.1 0.0 copy-done.11
  25.1 1.2 %finish.1 = bf16[1536,256]{1,0:T(8,128)(2,1)} custom-call(f32[12,128,256]{2,1,0:T(8,128)S(1)} %get-tuple-element.17.base_ref, bf16[64,256]{1,0:T(8,128)(2,1)S(1)} %bitcast.37, bf16[64,256]{1,0:T(8,128)(2,1)S(1)} %collective-permute-done.5.stale_ref, s32[8,8]{1,0:T(8,128)S(1)} %bitcast.42, s32[1,64]{1,0:T(1,128)S(1)} %copy-done.11), custom_call_target="tpu_custom_call" | custom-call | tf_op jit(solution)/shard_map/finish/pallas_call | solution.py:365
  26.3 0.1 collective-permute-done.6.other_ref
  26.4 0.7 %weight_grads.1 = bf16[2,256,256]{2,1,0:T(8,128)(2,1)} custom-call(bf16[256,256]{1,0:T(8,128)(2,1)S(1)} %maximum_select_fusion.mine_ref, bf16[256,256]{1,0:T(8,128)(2,1)S(1)} %collective-permute-done.6.other_ref), custom_call_target="tpu_custom_call" | custom-call | tf_op jit(solution)/shard_map/weight_grads/pallas_call | solution.py:355
  (21 shorter events, 0.2 us)
Async XLA Ops:
  3.4 1.5 %collective-permute-start = (bf16[256,256]{1,0:T(8,128)(2,1)S(1)}, bf16[256,256]{1,0:T(8,128)(2,1)S(1)}, u32[]{:S(2)}, u32[]{:S(2)}) collective-permute-start(bf16[256,256]{1,0:T(8,128)(2,1)S(1)} %get-tuple-element.13.after_ref), channel_id=1, source_target_pairs={{0,8},{8,0},{1,9},{9,1},{2,10},{10,2},{3,11},{11,3},{4,12},{12,4},... | collective-permute-start | bytes 393224 | tf_op jit(solution)/shard_map/ppermute | solution.py:29
  3.9 4.0 %copy-start.1 = (bf16[256,256]{1,0:T(8,128)(2,1)S(1)}, bf16[256,256]{1,0:T(8,128)(2,1)}, u32[]{:S(2)}) copy-start(bf16[256,256]{1,0:T(8,128)(2,1)} %weight_ref.4) | copy-start | bytes 393220
  3.9 4.0 %copy-start.4 = (s32[1,8,8,4]{2,3,1,0:T(4,128)S(1)}, s32[1,8,8,4]{2,3,1,0:T(4,128)}, u32[]{:S(2)}) copy-start(s32[1,8,8,4]{2,3,1,0:T(4,128)} %param.24) | copy-start | bytes 3076
  3.9 4.0 %copy-start.5 = (f32[1,8,8,4]{2,3,1,0:T(4,128)S(1)}, f32[1,8,8,4]{2,3,1,0:T(4,128)}, u32[]{:S(2)}) copy-start(f32[1,8,8,4]{2,3,1,0:T(4,128)} %param.25) | copy-start | bytes 3076
  3.9 4.0 %copy-start.9 = (s32[1,8]{1,0:T(1,128)S(1)}, s32[1,8]{1,0:T(1,128)}, u32[]{:S(2)}) copy-start(s32[1,8]{1,0:T(1,128)} %count_ref.2) | copy-start | bytes 100
  4.3 9.3 %copy-start.3 = (bf16[1,2,64,256]{3,2,1,0:T(8,128)(2,1)S(1)}, bf16[1,2,64,256]{3,2,1,0:T(8,128)(2,1)}, u32[]{:S(2)}) copy-start(bf16[1,2,64,256]{3,2,1,0:T(8,128)(2,1)} %param.28) | copy-start | bytes 196612
  4.4 9.3 %copy-start.7 = (s32[1,64,4]{1,2,0:T(4,128)S(1)}, s32[1,64,4]{1,2,0:T(4,128)}, u32[]{:S(2)}) copy-start(s32[1,64,4]{1,2,0:T(4,128)} %param.30) | copy-start | bytes 3076
  4.4 9.3 %copy-start.8 = (f32[1,64,4]{1,2,0:T(4,128)S(1)}, f32[1,64,4]{1,2,0:T(4,128)}, u32[]{:S(2)}) copy-start(f32[1,64,4]{1,2,0:T(4,128)} %param.31) | copy-start | bytes 3076
  4.4 13.5 %copy-start = (bf16[1,48,128,128]{3,2,1,0:T(8,128)(2,1)S(1)}, bf16[1,48,128,128]{3,2,1,0:T(8,128)(2,1)}, u32[]{:S(2)}) copy-start(bf16[1,48,128,128]{3,2,1,0:T(8,128)(2,1)} %param.22) | copy-start | bytes 4718596
  4.4 13.5 %copy-start.2 = (bf16[256,256]{1,0:T(8,128)(2,1)S(1)}, bf16[256,256]{1,0:T(8,128)(2,1)}, u32[]{:S(2)}) copy-start(bf16[256,256]{1,0:T(8,128)(2,1)} %weight_ref.5) | copy-start | bytes 393220
  4.4 13.5 %copy-start.10 = (s32[1,48]{1,0:T(1,128)S(1)}, s32[1,48]{1,0:T(1,128)}, u32[]{:S(2)}) copy-start(s32[1,48]{1,0:T(1,128)} %source_ref.1) | copy-start | bytes 580
  4.9 5.3 %collective-permute-start.1 = (bf16[128,256]{1,0:T(8,128)(2,1)S(1)}, bf16[128,256]{1,0:T(8,128)(2,1)S(1)}, u32[]{:S(2)}, u32[]{:S(2)}) collective-permute-start(bf16[128,256]{1,0:T(8,128)(2,1)S(1)} %select_convert_fusion.after_ref), channel_id=1, source_target_pairs={{0,1},{1,0},{2,3},{3,2},{4,5},{5,4},{6,7},{7,6},{8,9},{9,8},{10,11... | collective-permute-start | bytes 196616 | tf_op jit(solution)/shard_map/ppermute | solution.py:29
  10.3 4.5 %collective-permute-start.2 = (bf16[160,256]{1,0:T(8,128)(2,1)S(1)}, bf16[160,256]{1,0:T(8,128)(2,1)S(1)}, u32[]{:S(2)}, u32[]{:S(2)}) collective-permute-start(bf16[160,256]{1,0:T(8,128)(2,1)S(1)} %pad_maximum_fusion), channel_id=1, source_target_pairs={{0,2},{1,3},{2,0},{3,1},{4,6},{5,7},{6,4},{7,5},{8,10},{9,11},{10,... | collective-permute-start | bytes 245768 | tf_op jit(solution)/shard_map/ppermute | solution.py:29
  14.9 5.4 %collective-permute-start.3 = (bf16[160,256]{1,0:T(8,128)(2,1)S(1)}, bf16[160,256]{1,0:T(8,128)(2,1)S(1)}, u32[]{:S(2)}, u32[]{:S(2)}) collective-permute-start(bf16[160,256]{1,0:T(8,128)(2,1)S(1)} %pad_maximum_fusion.1), channel_id=1, source_target_pairs={{0,4},{1,5},{2,6},{3,7},{4,0},{5,1},{6,2},{7,3},{8,12},{9,13},{10,... | collective-permute-start | bytes 245768 | tf_op jit(solution)/shard_map/ppermute | solution.py:29
  17.9 7.2 %copy-start.6 = (s32[1,8,8]{2,1,0:T(8,128)S(1)}, s32[1,8,8]{2,1,0:T(8,128)}, u32[]{:S(2)}) copy-start(s32[1,8,8]{2,1,0:T(8,128)} %param.27) | copy-start | bytes 772
  17.9 7.2 %copy-start.11 = (s32[1,64]{1,0:T(1,128)S(1)}, s32[1,64]{1,0:T(1,128)}, u32[]{:S(2)}) copy-start(s32[1,64]{1,0:T(1,128)} %cross_ref.1) | copy-start | bytes 772
  20.4 4.5 %collective-permute-start.4 = (bf16[160,256]{1,0:T(8,128)(2,1)S(1)}, bf16[160,256]{1,0:T(8,128)(2,1)S(1)}, u32[]{:S(2)}, u32[]{:S(2)}) collective-permute-start(bf16[160,256]{1,0:T(8,128)(2,1)S(1)} %pad_maximum_fusion.2), channel_id=1, source_target_pairs={{0,1},{1,0},{2,3},{3,2},{4,5},{5,4},{6,7},{7,6},{8,9},{9,8},{10,11... | collective-permute-start | bytes 245768 | tf_op jit(solution)/shard_map/ppermute | solution.py:29
  22.3 2.8 %collective-permute-start.5 = (bf16[64,256]{1,0:T(8,128)(2,1)S(1)}, bf16[64,256]{1,0:T(8,128)(2,1)S(1)}, u32[]{:S(2)}, u32[]{:S(2)}) collective-permute-start(bf16[64,256]{1,0:T(8,128)(2,1)S(1)} %get-tuple-element.19), channel_id=1, source_target_pairs={{0,8},{8,0},{1,9},{9,1},{2,10},{10,2},{3,11},{11,3},{4,12},{12,4},... | collective-permute-start | bytes 98312 | tf_op jit(solution)/shard_map/ppermute | solution.py:29
  25.0 1.4 %collective-permute-start.6 = (bf16[256,256]{1,0:T(8,128)(2,1)S(1)}, bf16[256,256]{1,0:T(8,128)(2,1)S(1)}, u32[]{:S(2)}, u32[]{:S(2)}) collective-permute-start(bf16[256,256]{1,0:T(8,128)(2,1)S(1)} %maximum_select_fusion.mine_ref), channel_id=1, source_target_pairs={{0,8},{8,0},{1,9},{9,1},{2,10},{10,2},{3,11},{11,3},{4,12},{12,4},... | collective-permute-start | bytes 393224 | tf_op jit(solution)/shard_map/ppermute | solution.py:29

commit v4 on v3

--- a/solution.py
+++ b/solution.py
@@ -76,18 +76,17 @@
         copy.start()
         copies.append(copy)
 
-    fetch(self_hbm, self_weight)
-    fetch(neigh_hbm, neigh_weight)
     for p in range(PARTS):
         part = pl.ds(p * part_rows, part_rows)
         fetch(features_hbm.at[part], inputs_ref.at[0, part])
+        if p == 0:
+            fetch(self_hbm, self_weight)
+            fetch(neigh_hbm, neigh_weight)
         fetch(aggregated_hbm.at[part], inputs_ref.at[1, part])
         fetch(cotangent_hbm.at[part], cotangent.at[part])
-    copies[0].wait()
-    copies[1].wait()
     other = 1 - lax.axis_index("hst")
     for p in range(PARTS):
-        for copy in copies[3 * p + 2 : 3 * p + 5]:
+        for copy in copies[:5] if p == 0 else copies[3 * p + 2 : 3 * p + 5]:
             copy.wait()
         for c in range(CHUNKS):
             part = pl.ds(p * part_rows + c * rows, rows)
@@ -211,11 +210,17 @@
         copy.wait()
 
 
-def sums_kernel(mine_ref, other_ref, out_hbm, sems):
+def sums_kernel(own_ref, across_ref, host_ref, last_ref, out_hbm, sems):
+    quarter = own_ref.shape[0]
     host = lax.axis_index("hst")
+    odd = jnp.bitwise_and(lax.axis_index("dom"), 1)
+    here = pl.ds(pl.multiple_of(odd * quarter, quarter), quarter)
+    there = pl.ds(pl.multiple_of((1 - odd) * quarter, quarter), quarter)
     copies = [
-        pltpu.make_async_copy(mine_ref, out_hbm.at[host], sems.at[0]),
-        pltpu.make_async_copy(other_ref, out_hbm.at[1 - host], sems.at[1]),
+        pltpu.make_async_copy(own_ref, out_hbm.at[host, here], sems.at[0]),
+        pltpu.make_async_copy(across_ref, out_hbm.at[host, there], sems.at[1]),
+        pltpu.make_async_copy(host_ref, out_hbm.at[1 - host, here], sems.at[2]),
+        pltpu.make_async_copy(last_ref, out_hbm.at[1 - host, there], sems.at[3]),
     ]
     for copy in copies:
         copy.start()
@@ -247,7 +252,6 @@
     peers = lax.axis_size("dom")
     cap = slot_source.shape[2]
     bits = peers.bit_length() - 1
-    host = lax.axis_index("hst")
     me = lax.axis_index("dom")
     odd = (me & 1) == 1
     struct = jax.ShapeDtypeStruct
@@ -280,7 +284,6 @@
         name="kept_sum",
     )(inputs, pre_grad, given)
 
-    first = host == 0
     half = own + swap(given, "hst", 0).astype(F32)
     quarter = dim // 2
     low, high = half[:quarter], half[quarter:]
@@ -330,7 +333,6 @@
                 cross_weight[0].T,
                 stay,
             )
-            stale_in = swap(cross_out, "hst", 0)
         if step == 1:
             base, stay = pl.pallas_call(
                 local_kernel,
@@ -348,19 +350,18 @@
         kept = given.astype(F32) + other.astype(F32)
         held = jnp.stack([stay, arrived[quarter:].reshape(stay.shape)], axis=1)
         held = held.reshape(-1, middle, dim)
-    mine = jnp.where(
-        odd, jnp.concatenate([other, given], axis=0), jnp.concatenate([given, other], axis=0)
-    )
-    other = swap(mine, "hst", 0)
+    early = swap(jnp.concatenate([given, cross_out], axis=0), "hst", 0)
+    stale_in = early[quarter:]
+    last = swap(other, "hst", 0)
     sums = pl.pallas_call(
         sums_kernel,
         out_shape=struct((2, dim, dim), BF16),
-        in_specs=[VMEM, VMEM],
+        in_specs=[VMEM] * 4,
         out_specs=ANY,
-        scratch_shapes=[pltpu.SemaphoreType.DMA((2,))],
+        scratch_shapes=[pltpu.SemaphoreType.DMA((4,))],
         compiler_params=PARAMS,
         name="weight_grads",
-    )(mine, other)
+    )(given, other, early[:quarter], last)
 
     out_rows = pl.pallas_call(
         finish_kernel,

time: 27.5 us -> 27.4 us (level)
  transfers between devices with their start and end apart: 7 -> 7, of which waited for: 6 -> 5; matrix products, arithmetic and copies ran while one was open for 0% -> 0% of each run, Pallas kernels for 20% -> 20%
where the time goes in v4:
time: 27.4 us; the launch traced here: 26.9 us
  starting transfers between devices  10.4 us (38%)
  Pallas kernels  8.93 us (33%)
  waiting for transfers between devices  5.05 us (18%)
  between operations  2.25 us (8%)
    ppermute x7, starting transfers between devices, swap(): return lax.ppermute(value, axis, pairs)  10.4 us
    ppermute x7, waiting for transfers between devices, swap(): return lax.ppermute(value, axis, pairs)  5.05 us
    pallas_call x1, Pallas kernels, body(): pl.pallas_call(gradient_kernel, out_shape=(pltpu.VMEM((2, row_count, dim)...  2.71 us
    pallas_call x1, Pallas kernels, body(): pl.pallas_call(local_kernel, out_shape=(struct((blocks, 128, dim), F32),...  2.02 us
    pallas_call x1, Pallas kernels, body(): pl.pallas_call(outgoing_kernel, out_shape=(struct((row_count, dim), BF16)...  1.52 us
    pallas_call x1, Pallas kernels, body(): pl.pallas_call(finish_kernel, out_shape=struct((row_count, dim), BF16), i...  1.18 us
    pallas_call x1, Pallas kernels, body(): pl.pallas_call(sums_kernel, out_shape=struct((2, dim, dim), BF16), in_spe...  0.74 us
  transfers between devices with their start and end apart: 7, of which 5 were waited for; matrix products, arithmetic and copies ran while one was open for 0% of the time, Pallas kernels for 20%

profile of v4, /device:TPU:0, one launch (start us, length us, event | category | flops | bytes accessed | tf_op | source)
XLA Modules:
  0.0 26.9 jit_solution(15481804591587274754)
XLA Ops:
  0.6 2.7 %gradients.1 = (bf16[2,1536,256]{2,1,0:T(8,128)(2,1)S(1)}, bf16[1536,256]{1,0:T(8,128)(2,1)S(1)}, bf16[256,256]{1,0:T(8,128)(2,1)S(1)}) custom-call(bf16[1536,256]{1,0:T(8,128)(2,1)} %features_hbm.1, bf16[1536,256]{1,0:T(8,128)(2,1)} %aggregated_hbm.1, bf16[1536,256]{1,0:T(8,128)(2,1)} %cotangent_hbm.1, bf16[256,256]{1,0:T(8,128)(2,1)} %weight_ref.5, ...), custom_call_target="tpu_custom_call" | custom-call | tf_op jit(solution)/shard_map/gradients/pallas_call | solution.py:259
  3.4 0.5 %collective-permute-start = (bf16[256,256]{1,0:T(8,128)(2,1)S(1)}, bf16[256,256]{1,0:T(8,128)(2,1)S(1)}, u32[]{:S(2)}, u32[]{:S(2)}) collective-permute-start(bf16[256,256]{1,0:T(8,128)(2,1)S(1)} %get-tuple-element.13.after_ref), channel_id=1, source_target_pairs={{0,8},{8,0},{1,9},{9,1},{2,10},{10,2},{3,11},{11,3},{4,12},{12,4},... | collective-permute-start | bytes 393224 | tf_op jit(solution)/shard_map/ppermute | solution.py:29
  3.9 0.0 copy-start.1
  3.9 0.0 copy-start.4
  3.9 0.0 copy-start.5
  3.9 0.0 copy-start.9
  3.9 0.4 %kept_sum.1 = f32[256,256]{1,0:T(8,128)S(1)} custom-call(bf16[2,1536,256]{2,1,0:T(8,128)(2,1)S(1)} %get-tuple-element.12.inputs_ref, bf16[1536,256]{1,0:T(8,128)(2,1)S(1)} %get-tuple-element.11.grad_ref, bf16[256,256]{1,0:T(8,128)(2,1)S(1)} %get-tuple-element.13.after_ref), custom_call_target="tpu_custom_call" | custom-call | tf_op jit(solution)/shard_map/kept_sum/pallas_call | solution.py:278
  4.3 0.0 copy-start.3
  4.3 0.0 copy-start.7
  4.3 0.0 copy-start.8
  4.3 0.0 copy-start
  4.4 0.0 copy-start.2
  4.4 0.0 copy-start.10
  4.4 0.5 %collective-permute-done = bf16[256,256]{1,0:T(8,128)(2,1)S(1)} collective-permute-done((bf16[256,256]{1,0:T(8,128)(2,1)S(1)}, bf16[256,256]{1,0:T(8,128)(2,1)S(1)}, u32[]{:S(2)}, u32[]{:S(2)}) %collective-permute-start) | collective-permute-done | bytes 131104 | tf_op jit(solution)/shard_map/ppermute | solution.py:29
  4.9 2.9 %collective-permute-start.1 = (bf16[128,256]{1,0:T(8,128)(2,1)S(1)}, bf16[128,256]{1,0:T(8,128)(2,1)S(1)}, u32[]{:S(2)}, u32[]{:S(2)}) collective-permute-start(bf16[128,256]{1,0:T(8,128)(2,1)S(1)} %select_convert_fusion.after_ref), channel_id=1, source_target_pairs={{0,1},{1,0},{2,3},{3,2},{4,5},{5,4},{6,7},{7,6},{8,9},{9,8},{10,11... | collective-permute-start | bytes 196616 | tf_op jit(solution)/shard_map/ppermute | solution.py:29
  7.8 0.0 copy-done.1
  7.8 0.0 copy-done.4
  7.8 0.0 copy-done.5
  7.8 0.0 copy-done.9
  7.8 1.5 %outgoing.1 = (bf16[1536,256]{1,0:T(8,128)(2,1)S(1)}, bf16[64,256]{1,0:T(8,128)(2,1)S(1)}) custom-call(s32[1,8]{1,0:T(1,128)S(1)} %copy-done.9, bf16[1536,256]{1,0:T(8,128)(2,1)S(1)} %get-tuple-element.11.grad_ref, bf16[256,256]{1,0:T(8,128)(2,1)S(1)} %copy-done.1, s32[8,4,8]{2,1,0:T(4,128)S(1)} %bitcast.40, f32[8,4,8]{2,1,0:T(4,128)S(1)} %bitcast.41, ...), custom_call_target="tpu_custom_call" | custom-call | tf_op jit(solution)/shard_map/outgoing/pallas_call | solution.py:293
  9.4 0.9 %collective-permute-done.1 = bf16[128,256]{1,0:T(8,128)(2,1)S(1)} collective-permute-done((bf16[128,256]{1,0:T(8,128)(2,1)S(1)}, bf16[128,256]{1,0:T(8,128)(2,1)S(1)}, u32[]{:S(2)}, u32[]{:S(2)}) %collective-permute-start.1) | collective-permute-done | bytes 65568 | tf_op jit(solution)/shard_map/ppermute | solution.py:29
  10.3 2.0 %collective-permute-start.2 = (bf16[160,256]{1,0:T(8,128)(2,1)S(1)}, bf16[160,256]{1,0:T(8,128)(2,1)S(1)}, u32[]{:S(2)}, u32[]{:S(2)}) collective-permute-start(bf16[160,256]{1,0:T(8,128)(2,1)S(1)} %pad_maximum_fusion.1), channel_id=1, source_target_pairs={{0,2},{1,3},{2,0},{3,1},{4,6},{5,7},{6,4},{7,5},{8,10},{9,11},{10,... | collective-permute-start | bytes 245768 | tf_op jit(solution)/shard_map/ppermute | solution.py:29
  13.6 0.0 copy-done.3
  13.6 0.0 copy-done.7
  13.6 0.0 copy-done.8
  13.6 0.3 %stale_rows.1 = (bf16[64,256]{1,0:T(8,128)(2,1)S(1)}, bf16[1,32,256]{2,1,0:T(8,128)(2,1)S(1)}) custom-call(s32[1]{0:T(128)S(6)} %copy.26.version_ref, s32[1]{0:T(128)S(6)} %copy.27.count_ref, bf16[2,64,256]{2,1,0:T(8,128)(2,1)S(1)} %bitcast.38, bf16[256,256]{1,0:T(8,128)(2,1)S(1)} %copy-done.1, ...), custom_call_target="tpu_custom_call", output_to_operand_aliasing={{1}: (6, {})} | custom-call | tf_op jit(solution)/shard_map/stale_rows/pallas_call | solution.py:316
  14.0 0.8 %collective-permute-done.2 = bf16[160,256]{1,0:T(8,128)(2,1)S(1)} collective-permute-done((bf16[160,256]{1,0:T(8,128)(2,1)S(1)}, bf16[160,256]{1,0:T(8,128)(2,1)S(1)}, u32[]{:S(2)}, u32[]{:S(2)}) %collective-permute-start.2) | collective-permute-done | bytes 81952 | tf_op jit(solution)/shard_map/ppermute | solution.py:29
  14.8 3.0 %collective-permute-start.3 = (bf16[160,256]{1,0:T(8,128)(2,1)S(1)}, bf16[160,256]{1,0:T(8,128)(2,1)S(1)}, u32[]{:S(2)}, u32[]{:S(2)}) collective-permute-start(bf16[160,256]{1,0:T(8,128)(2,1)S(1)} %pad_maximum_fusion.2), channel_id=1, source_target_pairs={{0,4},{1,5},{2,6},{3,7},{4,0},{5,1},{6,2},{7,3},{8,12},{9,13},{10,... | collective-permute-start | bytes 245768 | tf_op jit(solution)/shard_map/ppermute | solution.py:29
  17.9 0.0 copy-done
  17.9 0.0 copy-done.2
  17.9 0.0 copy-done.10
  17.9 0.0 copy-start.6
  17.9 0.0 copy-start.11
  17.9 2.0 %local_term.1 = (f32[12,128,256]{2,1,0:T(8,128)S(1)}, bf16[2,16,256]{2,1,0:T(8,128)(2,1)S(1)}) custom-call(s32[1,48]{1,0:T(1,128)S(1)} %copy-done.10, bf16[1536,256]{1,0:T(8,128)(2,1)S(1)} %get-tuple-element.11.grad_ref, bf16[1536,256]{1,0:T(8,128)(2,1)S(1)} %get-tuple-element.14.neigh_ref, ...), custom_call_target="tpu_custom_call", output_to_operand_aliasing={{1}: (5, {})} | custom-call | tf_op jit(solution)/shard_map/local_term/pallas_call | solution.py:337
  19.9 0.4 %collective-permute-done.3 = bf16[160,256]{1,0:T(8,128)(2,1)S(1)} collective-permute-done((bf16[160,256]{1,0:T(8,128)(2,1)S(1)}, bf16[160,256]{1,0:T(8,128)(2,1)S(1)}, u32[]{:S(2)}, u32[]{:S(2)}) %collective-permute-start.3) | collective-permute-done | bytes 81952 | tf_op jit(solution)/shard_map/ppermute | solution.py:29
  20.4 1.9 %collective-permute-start.4 = (bf16[160,256]{1,0:T(8,128)(2,1)S(1)}, bf16[160,256]{1,0:T(8,128)(2,1)S(1)}, u32[]{:S(2)}, u32[]{:S(2)}) collective-permute-start(bf16[160,256]{1,0:T(8,128)(2,1)S(1)} %pad_maximum_fusion.3), channel_id=1, source_target_pairs={{0,1},{1,0},{2,3},{3,2},{4,5},{5,4},{6,7},{7,6},{8,9},{9,8},{10,11... | collective-permute-start | bytes 245768 | tf_op jit(solution)/shard_map/ppermute | solution.py:29
  22.3 0.1 collective-permute-start.5
  22.3 2.5 %collective-permute-done.4 = bf16[160,256]{1,0:T(8,128)(2,1)S(1)} collective-permute-done((bf16[160,256]{1,0:T(8,128)(2,1)S(1)}, bf16[160,256]{1,0:T(8,128)(2,1)S(1)}, u32[]{:S(2)}, u32[]{:S(2)}) %collective-permute-start.4) | collective-permute-done | bytes 81952 | tf_op jit(solution)/shard_map/ppermute | solution.py:29
  24.9 0.0 collective-permute-start.6
  24.9 0.0 collective-permute-done.5
  25.0 0.0 copy-done.6
  25.0 0.0 copy-done.11
  25.0 1.2 %finish.1 = bf16[1536,256]{1,0:T(8,128)(2,1)} custom-call(f32[12,128,256]{2,1,0:T(8,128)S(1)} %get-tuple-element.17.base_ref, bf16[64,256]{1,0:T(8,128)(2,1)S(1)} %bitcast.37, bf16[64,256]{1,0:T(8,128)(2,1)S(1)} %slice.77.stale_ref, s32[8,8]{1,0:T(8,128)S(1)} %bitcast.42, s32[1,64]{1,0:T(1,128)S(1)} %copy-done.11), custom_call_target="tpu_custom_call" | custom-call | tf_op jit(solution)/shard_map/finish/pallas_call | solution.py:366
  26.2 0.0 collective-permute-done.6.last_ref
  26.2 0.7 %weight_grads.1 = bf16[2,256,256]{2,1,0:T(8,128)(2,1)} custom-call(bf16[128,256]{1,0:T(8,128)(2,1)S(1)} %multiply_convert_fusion.own_ref, bf16[128,256]{1,0:T(8,128)(2,1)S(1)} %slice.78.across_ref, bf16[128,256]{1,0:T(8,128)(2,1)S(1)} %slice.79.host_ref, bf16[128,256]{1,0:T(8,128)(2,1)S(1)} %collective-permute-done.6.last_ref), custom_call_target="tpu_custom_call" | custom-call | tf_op jit(solution)/shard_map/weight_grads/pallas_call | solution.py:356
  (23 shorter events, 0.2 us)
Async XLA Ops:
  3.4 1.5 %collective-permute-start = (bf16[256,256]{1,0:T(8,128)(2,1)S(1)}, bf16[256,256]{1,0:T(8,128)(2,1)S(1)}, u32[]{:S(2)}, u32[]{:S(2)}) collective-permute-start(bf16[256,256]{1,0:T(8,128)(2,1)S(1)} %get-tuple-element.13.after_ref), channel_id=1, source_target_pairs={{0,8},{8,0},{1,9},{9,1},{2,10},{10,2},{3,11},{11,3},{4,12},{12,4},... | collective-permute-start | bytes 393224 | tf_op jit(solution)/shard_map/ppermute | solution.py:29
  3.9 4.0 %copy-start.1 = (bf16[256,256]{1,0:T(8,128)(2,1)S(1)}, bf16[256,256]{1,0:T(8,128)(2,1)}, u32[]{:S(2)}) copy-start(bf16[256,256]{1,0:T(8,128)(2,1)} %weight_ref.4) | copy-start | bytes 393220
  3.9 4.0 %copy-start.4 = (s32[1,8,8,4]{2,3,1,0:T(4,128)S(1)}, s32[1,8,8,4]{2,3,1,0:T(4,128)}, u32[]{:S(2)}) copy-start(s32[1,8,8,4]{2,3,1,0:T(4,128)} %param.24) | copy-start | bytes 3076
  3.9 4.0 %copy-start.5 = (f32[1,8,8,4]{2,3,1,0:T(4,128)S(1)}, f32[1,8,8,4]{2,3,1,0:T(4,128)}, u32[]{:S(2)}) copy-start(f32[1,8,8,4]{2,3,1,0:T(4,128)} %param.25) | copy-start | bytes 3076
  3.9 4.0 %copy-start.9 = (s32[1,8]{1,0:T(1,128)S(1)}, s32[1,8]{1,0:T(1,128)}, u32[]{:S(2)}) copy-start(s32[1,8]{1,0:T(1,128)} %count_ref.2) | copy-start | bytes 100
  4.3 9.3 %copy-start.3 = (bf16[1,2,64,256]{3,2,1,0:T(8,128)(2,1)S(1)}, bf16[1,2,64,256]{3,2,1,0:T(8,128)(2,1)}, u32[]{:S(2)}) copy-start(bf16[1,2,64,256]{3,2,1,0:T(8,128)(2,1)} %param.28) | copy-start | bytes 196612
  4.3 9.3 %copy-start.7 = (s32[1,64,4]{1,2,0:T(4,128)S(1)}, s32[1,64,4]{1,2,0:T(4,128)}, u32[]{:S(2)}) copy-start(s32[1,64,4]{1,2,0:T(4,128)} %param.30) | copy-start | bytes 3076
  4.3 9.3 %copy-start.8 = (f32[1,64,4]{1,2,0:T(4,128)S(1)}, f32[1,64,4]{1,2,0:T(4,128)}, u32[]{:S(2)}) copy-start(f32[1,64,4]{1,2,0:T(4,128)} %param.31) | copy-start | bytes 3076
  4.3 13.5 %copy-start = (bf16[1,48,128,128]{3,2,1,0:T(8,128)(2,1)S(1)}, bf16[1,48,128,128]{3,2,1,0:T(8,128)(2,1)}, u32[]{:S(2)}) copy-start(bf16[1,48,128,128]{3,2,1,0:T(8,128)(2,1)} %param.22) | copy-start | bytes 4718596
  4.4 13.5 %copy-start.2 = (bf16[256,256]{1,0:T(8,128)(2,1)S(1)}, bf16[256,256]{1,0:T(8,128)(2,1)}, u32[]{:S(2)}) copy-start(bf16[256,256]{1,0:T(8,128)(2,1)} %weight_ref.5) | copy-start | bytes 393220
  4.4 13.5 %copy-start.10 = (s32[1,48]{1,0:T(1,128)S(1)}, s32[1,48]{1,0:T(1,128)}, u32[]{:S(2)}) copy-start(s32[1,48]{1,0:T(1,128)} %source_ref.1) | copy-start | bytes 580
  4.9 5.3 %collective-permute-start.1 = (bf16[128,256]{1,0:T(8,128)(2,1)S(1)}, bf16[128,256]{1,0:T(8,128)(2,1)S(1)}, u32[]{:S(2)}, u32[]{:S(2)}) collective-permute-start(bf16[128,256]{1,0:T(8,128)(2,1)S(1)} %select_convert_fusion.after_ref), channel_id=1, source_target_pairs={{0,1},{1,0},{2,3},{3,2},{4,5},{5,4},{6,7},{7,6},{8,9},{9,8},{10,11... | collective-permute-start | bytes 196616 | tf_op jit(solution)/shard_map/ppermute | solution.py:29
  10.3 4.5 %collective-permute-start.2 = (bf16[160,256]{1,0:T(8,128)(2,1)S(1)}, bf16[160,256]{1,0:T(8,128)(2,1)S(1)}, u32[]{:S(2)}, u32[]{:S(2)}) collective-permute-start(bf16[160,256]{1,0:T(8,128)(2,1)S(1)} %pad_maximum_fusion.1), channel_id=1, source_target_pairs={{0,2},{1,3},{2,0},{3,1},{4,6},{5,7},{6,4},{7,5},{8,10},{9,11},{10,... | collective-permute-start | bytes 245768 | tf_op jit(solution)/shard_map/ppermute | solution.py:29
  14.8 5.4 %collective-permute-start.3 = (bf16[160,256]{1,0:T(8,128)(2,1)S(1)}, bf16[160,256]{1,0:T(8,128)(2,1)S(1)}, u32[]{:S(2)}, u32[]{:S(2)}) collective-permute-start(bf16[160,256]{1,0:T(8,128)(2,1)S(1)} %pad_maximum_fusion.2), channel_id=1, source_target_pairs={{0,4},{1,5},{2,6},{3,7},{4,0},{5,1},{6,2},{7,3},{8,12},{9,13},{10,... | collective-permute-start | bytes 245768 | tf_op jit(solution)/shard_map/ppermute | solution.py:29
  17.9 7.1 %copy-start.6 = (s32[1,8,8]{2,1,0:T(8,128)S(1)}, s32[1,8,8]{2,1,0:T(8,128)}, u32[]{:S(2)}) copy-start(s32[1,8,8]{2,1,0:T(8,128)} %param.27) | copy-start | bytes 772
  17.9 7.1 %copy-start.11 = (s32[1,64]{1,0:T(1,128)S(1)}, s32[1,64]{1,0:T(1,128)}, u32[]{:S(2)}) copy-start(s32[1,64]{1,0:T(1,128)} %cross_ref.1) | copy-start | bytes 772
  20.4 4.5 %collective-permute-start.4 = (bf16[160,256]{1,0:T(8,128)(2,1)S(1)}, bf16[160,256]{1,0:T(8,128)(2,1)S(1)}, u32[]{:S(2)}, u32[]{:S(2)}) collective-permute-start(bf16[160,256]{1,0:T(8,128)(2,1)S(1)} %pad_maximum_fusion.3), channel_id=1, source_target_pairs={{0,1},{1,0},{2,3},{3,2},{4,5},{5,4},{6,7},{7,6},{8,9},{9,8},{10,11... | collective-permute-start | bytes 245768 | tf_op jit(solution)/shard_map/ppermute | solution.py:29
  22.3 2.7 %collective-permute-start.5 = (bf16[192,256]{1,0:T(8,128)(2,1)S(1)}, bf16[192,256]{1,0:T(8,128)(2,1)S(1)}, u32[]{:S(2)}, u32[]{:S(2)}) collective-permute-start(bf16[192,256]{1,0:T(8,128)(2,1)S(1)} %pad_maximum_fusion), channel_id=1, source_target_pairs={{0,8},{8,0},{1,9},{9,1},{2,10},{10,2},{3,11},{11,3},{4,12},{12,4},... | collective-permute-start | bytes 294920 | tf_op jit(solution)/shard_map/ppermute | solution.py:29
  24.9 1.3 %collective-permute-start.6 = (bf16[128,256]{1,0:T(8,128)(2,1)S(1)}, bf16[128,256]{1,0:T(8,128)(2,1)S(1)}, u32[]{:S(2)}, u32[]{:S(2)}) collective-permute-start(bf16[128,256]{1,0:T(8,128)(2,1)S(1)} %slice.78.across_ref), channel_id=1, source_target_pairs={{0,8},{8,0},{1,9},{9,1},{2,10},{10,2},{3,11},{11,3},{4,12},{12,4},... | collective-permute-start | bytes 196616 | tf_op jit(solution)/shard_map/ppermute | solution.py:29

commit v5 on v4

--- a/solution.py
+++ b/solution.py
@@ -185,8 +185,24 @@
             base_ref[source_ref[0, t]] += product
 
 
+def quarters(size):
+    odd = jnp.bitwise_and(lax.axis_index("dom"), 1)
+    return [pl.ds(pl.multiple_of(i * size, size), size) for i in (odd, 1 - odd)]
+
+
 def finish_kernel(
-    base_ref, fresh_ref, stale_ref, recv_ref, cross_ref, out_hbm, out, sems
+    base_ref,
+    fresh_ref,
+    stale_ref,
+    recv_ref,
+    cross_ref,
+    own_ref,
+    across_ref,
+    host_ref,
+    out_hbm,
+    sums_hbm,
+    out,
+    sems,
 ):
     me = lax.axis_index("dom")
     blocks = base_ref.shape[0]
@@ -194,7 +210,15 @@
     targets = [recv_ref[pl.ds(jnp.bitwise_xor(me, o), 1), :] for o in hop_order(peers)]
     targets = jnp.concatenate(targets + [cross_ref[...]], axis=1)
     values = jnp.concatenate([fresh_ref[...], stale_ref[...]], axis=0)
-    copies = []
+    host = lax.axis_index("hst")
+    here, there = quarters(own_ref.shape[0])
+    copies = [
+        pltpu.make_async_copy(own_ref, sums_hbm.at[host, here], sems.at[0]),
+        pltpu.make_async_copy(across_ref, sums_hbm.at[host, there], sems.at[1]),
+        pltpu.make_async_copy(host_ref, sums_hbm.at[1 - host, here], sems.at[2]),
+    ]
+    for copy in copies:
+        copy.start()
     for b in range(blocks):
         node = b * 128 + lax.broadcasted_iota(jnp.int32, (128, targets.shape[1]), 0)
         hit = jnp.where(node == targets, 1.0, 0.0).astype(BF16)
@@ -210,22 +234,12 @@
         copy.wait()
 
 
-def sums_kernel(own_ref, across_ref, host_ref, last_ref, out_hbm, sems):
-    quarter = own_ref.shape[0]
+def last_kernel(last_ref, sums_in, sums_hbm, sem):
+    here, there = quarters(last_ref.shape[0])
     host = lax.axis_index("hst")
-    odd = jnp.bitwise_and(lax.axis_index("dom"), 1)
-    here = pl.ds(pl.multiple_of(odd * quarter, quarter), quarter)
-    there = pl.ds(pl.multiple_of((1 - odd) * quarter, quarter), quarter)
-    copies = [
-        pltpu.make_async_copy(own_ref, out_hbm.at[host, here], sems.at[0]),
-        pltpu.make_async_copy(across_ref, out_hbm.at[host, there], sems.at[1]),
-        pltpu.make_async_copy(host_ref, out_hbm.at[1 - host, here], sems.at[2]),
-        pltpu.make_async_copy(last_ref, out_hbm.at[1 - host, there], sems.at[3]),
-    ]
-    for copy in copies:
-        copy.start()
-    for copy in copies:
-        copy.wait()
+    copy = pltpu.make_async_copy(last_ref, sums_hbm.at[1 - host, there], sem)
+    copy.start()
+    copy.wait()
 
 
 def body(
@@ -353,28 +367,37 @@
     early = swap(jnp.concatenate([given, cross_out], axis=0), "hst", 0)
     stale_in = early[quarter:]
     last = swap(other, "hst", 0)
-    sums = pl.pallas_call(
-        sums_kernel,
-        out_shape=struct((2, dim, dim), BF16),
-        in_specs=[VMEM] * 4,
-        out_specs=ANY,
-        scratch_shapes=[pltpu.SemaphoreType.DMA((4,))],
-        compiler_params=PARAMS,
-        name="weight_grads",
-    )(given, other, early[:quarter], last)
-
-    out_rows = pl.pallas_call(
+    out_rows, sums = pl.pallas_call(
         finish_kernel,
-        out_shape=struct((row_count, dim), BF16),
-        in_specs=[VMEM] * 5,
-        out_specs=ANY,
+        out_shape=(struct((row_count, dim), BF16), struct((2, dim, dim), BF16)),
+        in_specs=[VMEM] * 8,
+        out_specs=(ANY, ANY),
         scratch_shapes=[
             pltpu.VMEM((row_count, dim), BF16),
-            pltpu.SemaphoreType.DMA((pl.cdiv(blocks, OUT_BLOCKS),)),
+            pltpu.SemaphoreType.DMA((3 + pl.cdiv(blocks, OUT_BLOCKS),)),
         ],
         compiler_params=PARAMS,
         name="finish",
-    )(base, held.reshape(peers * cap, dim), stale_in, recv_rows[0], cross_rows)
+    )(
+        base,
+        held.reshape(peers * cap, dim),
+        stale_in,
+        recv_rows[0],
+        cross_rows,
+        given,
+        other,
+        early[:quarter],
+    )
+    sums = pl.pallas_call(
+        last_kernel,
+        out_shape=struct((2, dim, dim), BF16),
+        in_specs=[VMEM, ANY],
+        out_specs=ANY,
+        input_output_aliases={1: 0},
+        scratch_shapes=[pltpu.SemaphoreType.DMA],
+        compiler_params=PARAMS,
+        name="weight_grads",
+    )(last, sums)
     return (out_rows, sums)
 
 

time: 27.4 us -> 27.3 us (level)
  no operation moved by 1% of the time
where the time goes in v5:
time: 27.3 us; the launch traced here: 26.9 us
  starting transfers between devices  10.4 us (38%)
  Pallas kernels  8.87 us (32%)
  waiting for transfers between devices  5.05 us (18%)
  between operations  2.25 us (8%)
    ppermute x7, starting transfers between devices, swap(): return lax.ppermute(value, axis, pairs)  10.4 us
    ppermute x7, waiting for transfers between devices, swap(): return lax.ppermute(value, axis, pairs)  5.05 us
    pallas_call x1, Pallas kernels, body(): pl.pallas_call(gradient_kernel, out_shape=(pltpu.VMEM((2, row_count, dim)...  2.71 us
    pallas_call x1, Pallas kernels, body(): pl.pallas_call(local_kernel, out_shape=(struct((blocks, 128, dim), F32),...  2.02 us
    pallas_call x1, Pallas kernels, body(): pl.pallas_call(outgoing_kernel, out_shape=(struct((row_count, dim), BF16)...  1.52 us
    pallas_call x1, Pallas kernels, body(): pl.pallas_call(finish_kernel, out_shape=(struct((row_count, dim), BF16),...  1.2 us
    pallas_call x1, Pallas kernels, body(): pl.pallas_call(last_kernel, out_shape=struct((2, dim, dim), BF16), in_spe...  0.65 us
  transfers between devices with their start and end apart: 7, of which 5 were waited for; matrix products, arithmetic and copies ran while one was open for 0% of the time, Pallas kernels for 20%

profile of v5, /device:TPU:0, one launch (start us, length us, event | category | flops | bytes accessed | tf_op | source)
XLA Modules:
  0.0 26.9 jit_solution(10988620703585570090)
XLA Ops:
  0.6 2.7 %gradients.1 = (bf16[2,1536,256]{2,1,0:T(8,128)(2,1)S(1)}, bf16[1536,256]{1,0:T(8,128)(2,1)S(1)}, bf16[256,256]{1,0:T(8,128)(2,1)S(1)}) custom-call(bf16[1536,256]{1,0:T(8,128)(2,1)} %features_hbm.1, bf16[1536,256]{1,0:T(8,128)(2,1)} %aggregated_hbm.1, bf16[1536,256]{1,0:T(8,128)(2,1)} %cotangent_hbm.1, bf16[256,256]{1,0:T(8,128)(2,1)} %weight_ref.5, ...), custom_call_target="tpu_custom_call" | custom-call | tf_op jit(solution)/shard_map/gradients/pallas_call | solution.py:273
  3.4 0.5 %collective-permute-start = (bf16[256,256]{1,0:T(8,128)(2,1)S(1)}, bf16[256,256]{1,0:T(8,128)(2,1)S(1)}, u32[]{:S(2)}, u32[]{:S(2)}) collective-permute-start(bf16[256,256]{1,0:T(8,128)(2,1)S(1)} %get-tuple-element.15.after_ref), channel_id=1, source_target_pairs={{0,8},{8,0},{1,9},{9,1},{2,10},{10,2},{3,11},{11,3},{4,12},{12,4},... | collective-permute-start | bytes 393224 | tf_op jit(solution)/shard_map/ppermute | solution.py:29
  3.9 0.0 copy-start.1
  3.9 0.0 copy-start.4
  3.9 0.0 copy-start.5
  3.9 0.0 copy-start.9
  3.9 0.4 %kept_sum.1 = f32[256,256]{1,0:T(8,128)S(1)} custom-call(bf16[2,1536,256]{2,1,0:T(8,128)(2,1)S(1)} %get-tuple-element.14.inputs_ref, bf16[1536,256]{1,0:T(8,128)(2,1)S(1)} %get-tuple-element.13.grad_ref, bf16[256,256]{1,0:T(8,128)(2,1)S(1)} %get-tuple-element.15.after_ref), custom_call_target="tpu_custom_call" | custom-call | tf_op jit(solution)/shard_map/kept_sum/pallas_call | solution.py:292
  4.3 0.0 copy-start.3
  4.3 0.0 copy-start.7
  4.3 0.0 copy-start.8
  4.3 0.0 copy-start
  4.4 0.0 copy-start.2
  4.4 0.0 copy-start.10
  4.4 0.5 %collective-permute-done = bf16[256,256]{1,0:T(8,128)(2,1)S(1)} collective-permute-done((bf16[256,256]{1,0:T(8,128)(2,1)S(1)}, bf16[256,256]{1,0:T(8,128)(2,1)S(1)}, u32[]{:S(2)}, u32[]{:S(2)}) %collective-permute-start) | collective-permute-done | bytes 131104 | tf_op jit(solution)/shard_map/ppermute | solution.py:29
  4.9 2.9 %collective-permute-start.1 = (bf16[128,256]{1,0:T(8,128)(2,1)S(1)}, bf16[128,256]{1,0:T(8,128)(2,1)S(1)}, u32[]{:S(2)}, u32[]{:S(2)}) collective-permute-start(bf16[128,256]{1,0:T(8,128)(2,1)S(1)} %select_convert_fusion.after_ref), channel_id=1, source_target_pairs={{0,1},{1,0},{2,3},{3,2},{4,5},{5,4},{6,7},{7,6},{8,9},{9,8},{10,11... | collective-permute-start | bytes 196616 | tf_op jit(solution)/shard_map/ppermute | solution.py:29
  7.8 0.0 copy-done.1
  7.8 0.0 copy-done.4
  7.8 0.0 copy-done.5
  7.8 0.0 copy-done.9
  7.8 1.5 %outgoing.1 = (bf16[1536,256]{1,0:T(8,128)(2,1)S(1)}, bf16[64,256]{1,0:T(8,128)(2,1)S(1)}) custom-call(s32[1,8]{1,0:T(1,128)S(1)} %copy-done.9, bf16[1536,256]{1,0:T(8,128)(2,1)S(1)} %get-tuple-element.13.grad_ref, bf16[256,256]{1,0:T(8,128)(2,1)S(1)} %copy-done.1, s32[8,4,8]{2,1,0:T(4,128)S(1)} %bitcast.40, f32[8,4,8]{2,1,0:T(4,128)S(1)} %bitcast.41, ...), custom_call_target="tpu_custom_call" | custom-call | tf_op jit(solution)/shard_map/outgoing/pallas_call | solution.py:307
  9.4 0.9 %collective-permute-done.1 = bf16[128,256]{1,0:T(8,128)(2,1)S(1)} collective-permute-done((bf16[128,256]{1,0:T(8,128)(2,1)S(1)}, bf16[128,256]{1,0:T(8,128)(2,1)S(1)}, u32[]{:S(2)}, u32[]{:S(2)}) %collective-permute-start.1) | collective-permute-done | bytes 65568 | tf_op jit(solution)/shard_map/ppermute | solution.py:29
  10.3 2.0 %collective-permute-start.2 = (bf16[160,256]{1,0:T(8,128)(2,1)S(1)}, bf16[160,256]{1,0:T(8,128)(2,1)S(1)}, u32[]{:S(2)}, u32[]{:S(2)}) collective-permute-start(bf16[160,256]{1,0:T(8,128)(2,1)S(1)} %pad_maximum_fusion.1), channel_id=1, source_target_pairs={{0,2},{1,3},{2,0},{3,1},{4,6},{5,7},{6,4},{7,5},{8,10},{9,11},{10,... | collective-permute-start | bytes 245768 | tf_op jit(solution)/shard_map/ppermute | solution.py:29
  13.6 0.0 copy-done.3
  13.6 0.0 copy-done.7
  13.6 0.0 copy-done.8
  13.6 0.3 %stale_rows.1 = (bf16[64,256]{1,0:T(8,128)(2,1)S(1)}, bf16[1,32,256]{2,1,0:T(8,128)(2,1)S(1)}) custom-call(s32[1]{0:T(128)S(6)} %copy.28.version_ref, s32[1]{0:T(128)S(6)} %copy.29.count_ref, bf16[2,64,256]{2,1,0:T(8,128)(2,1)S(1)} %bitcast.38, bf16[256,256]{1,0:T(8,128)(2,1)S(1)} %copy-done.1, ...), custom_call_target="tpu_custom_call", output_to_operand_aliasing={{1}: (6, {})} | custom-call | tf_op jit(solution)/shard_map/stale_rows/pallas_call | solution.py:330
  14.0 0.8 %collective-permute-done.2 = bf16[160,256]{1,0:T(8,128)(2,1)S(1)} collective-permute-done((bf16[160,256]{1,0:T(8,128)(2,1)S(1)}, bf16[160,256]{1,0:T(8,128)(2,1)S(1)}, u32[]{:S(2)}, u32[]{:S(2)}) %collective-permute-start.2) | collective-permute-done | bytes 81952 | tf_op jit(solution)/shard_map/ppermute | solution.py:29
  14.8 3.0 %collective-permute-start.3 = (bf16[160,256]{1,0:T(8,128)(2,1)S(1)}, bf16[160,256]{1,0:T(8,128)(2,1)S(1)}, u32[]{:S(2)}, u32[]{:S(2)}) collective-permute-start(bf16[160,256]{1,0:T(8,128)(2,1)S(1)} %pad_maximum_fusion.2), channel_id=1, source_target_pairs={{0,4},{1,5},{2,6},{3,7},{4,0},{5,1},{6,2},{7,3},{8,12},{9,13},{10,... | collective-permute-start | bytes 245768 | tf_op jit(solution)/shard_map/ppermute | solution.py:29
  17.9 0.0 copy-done
  17.9 0.0 copy-done.2
  17.9 0.0 copy-done.10
  17.9 0.0 copy-start.6
  17.9 0.0 copy-start.11
  17.9 2.0 %local_term.1 = (f32[12,128,256]{2,1,0:T(8,128)S(1)}, bf16[2,16,256]{2,1,0:T(8,128)(2,1)S(1)}) custom-call(s32[1,48]{1,0:T(1,128)S(1)} %copy-done.10, bf16[1536,256]{1,0:T(8,128)(2,1)S(1)} %get-tuple-element.13.grad_ref, bf16[1536,256]{1,0:T(8,128)(2,1)S(1)} %get-tuple-element.16.neigh_ref, ...), custom_call_target="tpu_custom_call", output_to_operand_aliasing={{1}: (5, {})} | custom-call | tf_op jit(solution)/shard_map/local_term/pallas_call | solution.py:351
  19.9 0.4 %collective-permute-done.3 = bf16[160,256]{1,0:T(8,128)(2,1)S(1)} collective-permute-done((bf16[160,256]{1,0:T(8,128)(2,1)S(1)}, bf16[160,256]{1,0:T(8,128)(2,1)S(1)}, u32[]{:S(2)}, u32[]{:S(2)}) %collective-permute-start.3) | collective-permute-done | bytes 81952 | tf_op jit(solution)/shard_map/ppermute | solution.py:29
  20.4 1.9 %collective-permute-start.4 = (bf16[160,256]{1,0:T(8,128)(2,1)S(1)}, bf16[160,256]{1,0:T(8,128)(2,1)S(1)}, u32[]{:S(2)}, u32[]{:S(2)}) collective-permute-start(bf16[160,256]{1,0:T(8,128)(2,1)S(1)} %pad_maximum_fusion.3), channel_id=1, source_target_pairs={{0,1},{1,0},{2,3},{3,2},{4,5},{5,4},{6,7},{7,6},{8,9},{9,8},{10,11... | collective-permute-start | bytes 245768 | tf_op jit(solution)/shard_map/ppermute | solution.py:29
  22.3 0.1 collective-permute-start.5
  22.3 2.5 %collective-permute-done.4 = bf16[160,256]{1,0:T(8,128)(2,1)S(1)} collective-permute-done((bf16[160,256]{1,0:T(8,128)(2,1)S(1)}, bf16[160,256]{1,0:T(8,128)(2,1)S(1)}, u32[]{:S(2)}, u32[]{:S(2)}) %collective-permute-start.4) | collective-permute-done | bytes 81952 | tf_op jit(solution)/shard_map/ppermute | solution.py:29
  24.9 0.0 collective-permute-start.6
  24.9 0.0 collective-permute-done.5
  25.0 0.0 copy-done.6
  25.0 0.0 copy-done.11
  25.0 1.2 %finish.1 = (bf16[1536,256]{1,0:T(8,128)(2,1)}, bf16[2,256,256]{2,1,0:T(8,128)(2,1)}) custom-call(f32[12,128,256]{2,1,0:T(8,128)S(1)} %get-tuple-element.19.base_ref, bf16[64,256]{1,0:T(8,128)(2,1)S(1)} %bitcast.37, bf16[64,256]{1,0:T(8,128)(2,1)S(1)} %slice.77.stale_ref, s32[8,8]{1,0:T(8,128)S(1)} %bitcast.42, s32[1,64]{1,0:T(1,128)S(1)} %copy-done.11, ...), custom_call_target="tpu_custom_call" | custom-call | tf_op jit(solution)/shard_map/finish/pallas_call | solution.py:370
  26.2 0.0 collective-permute-done.6.last_ref
  26.2 0.7 %weight_grads.1 = bf16[2,256,256]{2,1,0:T(8,128)(2,1)} custom-call(bf16[128,256]{1,0:T(8,128)(2,1)S(1)} %collective-permute-done.6.last_ref, bf16[2,256,256]{2,1,0:T(8,128)(2,1)} %get-tuple-element.23.sums_in), custom_call_target="tpu_custom_call", output_to_operand_aliasing={{}: (1, {})} | custom-call | tf_op jit(solution)/shard_map/weight_grads/pallas_call | solution.py:391
  (23 shorter events, 0.2 us)
Async XLA Ops:
  3.4 1.5 %collective-permute-start = (bf16[256,256]{1,0:T(8,128)(2,1)S(1)}, bf16[256,256]{1,0:T(8,128)(2,1)S(1)}, u32[]{:S(2)}, u32[]{:S(2)}) collective-permute-start(bf16[256,256]{1,0:T(8,128)(2,1)S(1)} %get-tuple-element.15.after_ref), channel_id=1, source_target_pairs={{0,8},{8,0},{1,9},{9,1},{2,10},{10,2},{3,11},{11,3},{4,12},{12,4},... | collective-permute-start | bytes 393224 | tf_op jit(solution)/shard_map/ppermute | solution.py:29
  3.9 4.0 %copy-start.1 = (bf16[256,256]{1,0:T(8,128)(2,1)S(1)}, bf16[256,256]{1,0:T(8,128)(2,1)}, u32[]{:S(2)}) copy-start(bf16[256,256]{1,0:T(8,128)(2,1)} %weight_ref.4) | copy-start | bytes 393220
  3.9 4.0 %copy-start.4 = (s32[1,8,8,4]{2,3,1,0:T(4,128)S(1)}, s32[1,8,8,4]{2,3,1,0:T(4,128)}, u32[]{:S(2)}) copy-start(s32[1,8,8,4]{2,3,1,0:T(4,128)} %param.24) | copy-start | bytes 3076
  3.9 4.0 %copy-start.5 = (f32[1,8,8,4]{2,3,1,0:T(4,128)S(1)}, f32[1,8,8,4]{2,3,1,0:T(4,128)}, u32[]{:S(2)}) copy-start(f32[1,8,8,4]{2,3,1,0:T(4,128)} %param.25) | copy-start | bytes 3076
  3.9 4.0 %copy-start.9 = (s32[1,8]{1,0:T(1,128)S(1)}, s32[1,8]{1,0:T(1,128)}, u32[]{:S(2)}) copy-start(s32[1,8]{1,0:T(1,128)} %count_ref.2) | copy-start | bytes 100
  4.3 9.3 %copy-start.3 = (bf16[1,2,64,256]{3,2,1,0:T(8,128)(2,1)S(1)}, bf16[1,2,64,256]{3,2,1,0:T(8,128)(2,1)}, u32[]{:S(2)}) copy-start(bf16[1,2,64,256]{3,2,1,0:T(8,128)(2,1)} %param.28) | copy-start | bytes 196612
  4.3 9.3 %copy-start.7 = (s32[1,64,4]{1,2,0:T(4,128)S(1)}, s32[1,64,4]{1,2,0:T(4,128)}, u32[]{:S(2)}) copy-start(s32[1,64,4]{1,2,0:T(4,128)} %param.30) | copy-start | bytes 3076
  4.3 9.3 %copy-start.8 = (f32[1,64,4]{1,2,0:T(4,128)S(1)}, f32[1,64,4]{1,2,0:T(4,128)}, u32[]{:S(2)}) copy-start(f32[1,64,4]{1,2,0:T(4,128)} %param.31) | copy-start | bytes 3076
  4.3 13.5 %copy-start = (bf16[1,48,128,128]{3,2,1,0:T(8,128)(2,1)S(1)}, bf16[1,48,128,128]{3,2,1,0:T(8,128)(2,1)}, u32[]{:S(2)}) copy-start(bf16[1,48,128,128]{3,2,1,0:T(8,128)(2,1)} %param.22) | copy-start | bytes 4718596
  4.4 13.5 %copy-start.2 = (bf16[256,256]{1,0:T(8,128)(2,1)S(1)}, bf16[256,256]{1,0:T(8,128)(2,1)}, u32[]{:S(2)}) copy-start(bf16[256,256]{1,0:T(8,128)(2,1)} %weight_ref.5) | copy-start | bytes 393220
  4.4 13.5 %copy-start.10 = (s32[1,48]{1,0:T(1,128)S(1)}, s32[1,48]{1,0:T(1,128)}, u32[]{:S(2)}) copy-start(s32[1,48]{1,0:T(1,128)} %source_ref.1) | copy-start | bytes 580
  4.9 5.3 %collective-permute-start.1 = (bf16[128,256]{1,0:T(8,128)(2,1)S(1)}, bf16[128,256]{1,0:T(8,128)(2,1)S(1)}, u32[]{:S(2)}, u32[]{:S(2)}) collective-permute-start(bf16[128,256]{1,0:T(8,128)(2,1)S(1)} %select_convert_fusion.after_ref), channel_id=1, source_target_pairs={{0,1},{1,0},{2,3},{3,2},{4,5},{5,4},{6,7},{7,6},{8,9},{9,8},{10,11... | collective-permute-start | bytes 196616 | tf_op jit(solution)/shard_map/ppermute | solution.py:29
  10.3 4.5 %collective-permute-start.2 = (bf16[160,256]{1,0:T(8,128)(2,1)S(1)}, bf16[160,256]{1,0:T(8,128)(2,1)S(1)}, u32[]{:S(2)}, u32[]{:S(2)}) collective-permute-start(bf16[160,256]{1,0:T(8,128)(2,1)S(1)} %pad_maximum_fusion.1), channel_id=1, source_target_pairs={{0,2},{1,3},{2,0},{3,1},{4,6},{5,7},{6,4},{7,5},{8,10},{9,11},{10,... | collective-permute-start | bytes 245768 | tf_op jit(solution)/shard_map/ppermute | solution.py:29
  14.8 5.4 %collective-permute-start.3 = (bf16[160,256]{1,0:T(8,128)(2,1)S(1)}, bf16[160,256]{1,0:T(8,128)(2,1)S(1)}, u32[]{:S(2)}, u32[]{:S(2)}) collective-permute-start(bf16[160,256]{1,0:T(8,128)(2,1)S(1)} %pad_maximum_fusion.2), channel_id=1, source_target_pairs={{0,4},{1,5},{2,6},{3,7},{4,0},{5,1},{6,2},{7,3},{8,12},{9,13},{10,... | collective-permute-start | bytes 245768 | tf_op jit(solution)/shard_map/ppermute | solution.py:29
  17.9 7.1 %copy-start.6 = (s32[1,8,8]{2,1,0:T(8,128)S(1)}, s32[1,8,8]{2,1,0:T(8,128)}, u32[]{:S(2)}) copy-start(s32[1,8,8]{2,1,0:T(8,128)} %param.27) | copy-start | bytes 772
  17.9 7.1 %copy-start.11 = (s32[1,64]{1,0:T(1,128)S(1)}, s32[1,64]{1,0:T(1,128)}, u32[]{:S(2)}) copy-start(s32[1,64]{1,0:T(1,128)} %cross_ref.1) | copy-start | bytes 772
  20.4 4.5 %collective-permute-start.4 = (bf16[160,256]{1,0:T(8,128)(2,1)S(1)}, bf16[160,256]{1,0:T(8,128)(2,1)S(1)}, u32[]{:S(2)}, u32[]{:S(2)}) collective-permute-start(bf16[160,256]{1,0:T(8,128)(2,1)S(1)} %pad_maximum_fusion.3), channel_id=1, source_target_pairs={{0,1},{1,0},{2,3},{3,2},{4,5},{5,4},{6,7},{7,6},{8,9},{9,8},{10,11... | collective-permute-start | bytes 245768 | tf_op jit(solution)/shard_map/ppermute | solution.py:29
  22.3 2.7 %collective-permute-start.5 = (bf16[192,256]{1,0:T(8,128)(2,1)S(1)}, bf16[192,256]{1,0:T(8,128)(2,1)S(1)}, u32[]{:S(2)}, u32[]{:S(2)}) collective-permute-start(bf16[192,256]{1,0:T(8,128)(2,1)S(1)} %pad_maximum_fusion), channel_id=1, source_target_pairs={{0,8},{8,0},{1,9},{9,1},{2,10},{10,2},{3,11},{11,3},{4,12},{12,4},... | collective-permute-start | bytes 294920 | tf_op jit(solution)/shard_map/ppermute | solution.py:29
  24.9 1.3 %collective-permute-start.6 = (bf16[128,256]{1,0:T(8,128)(2,1)S(1)}, bf16[128,256]{1,0:T(8,128)(2,1)S(1)}, u32[]{:S(2)}, u32[]{:S(2)}) collective-permute-start(bf16[128,256]{1,0:T(8,128)(2,1)S(1)} %slice.78.across_ref), channel_id=1, source_target_pairs={{0,8},{8,0},{1,9},{9,1},{2,10},{10,2},{3,11},{11,3},{4,12},{12,4},... | collective-permute-start | bytes 196616 | tf_op jit(solution)/shard_map/ppermute | solution.py:29

commit v6 on v5

--- a/solution.py
+++ b/solution.py
@@ -39,8 +39,8 @@
     return [*range(1, bits), 0]
 
 
-def hop_order(count):
-    hops = hop_bits(count)[::-1]
+def hop_order(count, first_hop_fastest=False):
+    hops = hop_bits(count) if first_hop_fastest else hop_bits(count)[::-1]
     return [sum(((i >> j) & 1) << bit for j, bit in enumerate(hops)) for i in range(count)]
 
 
@@ -207,7 +207,7 @@
     me = lax.axis_index("dom")
     blocks = base_ref.shape[0]
     peers, cap = recv_ref.shape
-    targets = [recv_ref[pl.ds(jnp.bitwise_xor(me, o), 1), :] for o in hop_order(peers)]
+    targets = [recv_ref[pl.ds(jnp.bitwise_xor(me, o), 1), :] for o in hop_order(peers, True)]
     targets = jnp.concatenate(targets + [cross_ref[...]], axis=1)
     values = jnp.concatenate([fresh_ref[...], stale_ref[...]], axis=0)
     host = lax.axis_index("hst")
@@ -362,8 +362,7 @@
             )(tile_source, pre_grad, neigh_grad, w_self, tile_values[0], stay)
         other = arrived[:quarter]
         kept = given.astype(F32) + other.astype(F32)
-        held = jnp.stack([stay, arrived[quarter:].reshape(stay.shape)], axis=1)
-        held = held.reshape(-1, middle, dim)
+        held = jnp.concatenate([stay, arrived[quarter:].reshape(stay.shape)], axis=0)
     early = swap(jnp.concatenate([given, cross_out], axis=0), "hst", 0)
     stale_in = early[quarter:]
     last = swap(other, "hst", 0)

time: 27.3 us -> 27.3 us (level)
  transfers between devices with their start and end apart: 7 -> 7, of which waited for: 5 -> 5; matrix products, arithmetic and copies ran while one was open for 0% -> 0% of each run, Pallas kernels for 20% -> 21%
where the time goes in v6:
time: 27.3 us; the launch traced here: 26.8 us
  starting transfers between devices  10.4 us (38%)
  Pallas kernels  8.89 us (33%)
  waiting for transfers between devices  5.03 us (18%)
  between operations  2.21 us (8%)
    ppermute x7, starting transfers between devices, swap(): return lax.ppermute(value, axis, pairs)  10.4 us
    ppermute x7, waiting for transfers between devices, swap(): return lax.ppermute(value, axis, pairs)  5.03 us
    pallas_call x1, Pallas kernels, body(): pl.pallas_call(gradient_kernel, out_shape=(pltpu.VMEM((2, row_count, dim)...  2.71 us
    pallas_call x1, Pallas kernels, body(): pl.pallas_call(local_kernel, out_shape=(struct((blocks, 128, dim), F32),...  2.04 us
    pallas_call x1, Pallas kernels, body(): pl.pallas_call(outgoing_kernel, out_shape=(struct((row_count, dim), BF16)...  1.52 us
    pallas_call x1, Pallas kernels, body(): pl.pallas_call(finish_kernel, out_shape=(struct((row_count, dim), BF16),...  1.2 us
    pallas_call x1, Pallas kernels, body(): pl.pallas_call(last_kernel, out_shape=struct((2, dim, dim), BF16), in_spe...  0.65 us
  transfers between devices with their start and end apart: 7, of which 5 were waited for; matrix products, arithmetic and copies ran while one was open for 0% of the time, Pallas kernels for 21%

profile of v6, /device:TPU:0, one launch (start us, length us, event | category | flops | bytes accessed | tf_op | source)
XLA Modules:
  0.0 26.8 jit_solution(6445441978658360073)
XLA Ops:
  0.6 2.7 %gradients.1 = (bf16[2,1536,256]{2,1,0:T(8,128)(2,1)S(1)}, bf16[1536,256]{1,0:T(8,128)(2,1)S(1)}, bf16[256,256]{1,0:T(8,128)(2,1)S(1)}) custom-call(bf16[1536,256]{1,0:T(8,128)(2,1)} %features_hbm.1, bf16[1536,256]{1,0:T(8,128)(2,1)} %aggregated_hbm.1, bf16[1536,256]{1,0:T(8,128)(2,1)} %cotangent_hbm.1, bf16[256,256]{1,0:T(8,128)(2,1)} %weight_ref.5, ...), custom_call_target="tpu_custom_call" | custom-call | tf_op jit(solution)/shard_map/gradients/pallas_call | solution.py:273
  3.4 0.5 %collective-permute-start = (bf16[256,256]{1,0:T(8,128)(2,1)S(1)}, bf16[256,256]{1,0:T(8,128)(2,1)S(1)}, u32[]{:S(2)}, u32[]{:S(2)}) collective-permute-start(bf16[256,256]{1,0:T(8,128)(2,1)S(1)} %get-tuple-element.15.after_ref), channel_id=1, source_target_pairs={{0,8},{8,0},{1,9},{9,1},{2,10},{10,2},{3,11},{11,3},{4,12},{12,4},... | collective-permute-start | bytes 393224 | tf_op jit(solution)/shard_map/ppermute | solution.py:29
  3.9 0.0 copy-start.1
  3.9 0.0 copy-start.4
  3.9 0.0 copy-start.5
  3.9 0.0 copy-start.9
  3.9 0.4 %kept_sum.1 = f32[256,256]{1,0:T(8,128)S(1)} custom-call(bf16[2,1536,256]{2,1,0:T(8,128)(2,1)S(1)} %get-tuple-element.14.inputs_ref, bf16[1536,256]{1,0:T(8,128)(2,1)S(1)} %get-tuple-element.13.grad_ref, bf16[256,256]{1,0:T(8,128)(2,1)S(1)} %get-tuple-element.15.after_ref), custom_call_target="tpu_custom_call" | custom-call | tf_op jit(solution)/shard_map/kept_sum/pallas_call | solution.py:292
  4.3 0.0 copy-start.3
  4.3 0.0 copy-start.7
  4.3 0.0 copy-start.8
  4.3 0.0 copy-start
  4.4 0.0 copy-start.2
  4.4 0.0 copy-start.10
  4.4 0.5 %collective-permute-done = bf16[256,256]{1,0:T(8,128)(2,1)S(1)} collective-permute-done((bf16[256,256]{1,0:T(8,128)(2,1)S(1)}, bf16[256,256]{1,0:T(8,128)(2,1)S(1)}, u32[]{:S(2)}, u32[]{:S(2)}) %collective-permute-start) | collective-permute-done | bytes 131104 | tf_op jit(solution)/shard_map/ppermute | solution.py:29
  4.9 2.9 %collective-permute-start.1 = (bf16[128,256]{1,0:T(8,128)(2,1)S(1)}, bf16[128,256]{1,0:T(8,128)(2,1)S(1)}, u32[]{:S(2)}, u32[]{:S(2)}) collective-permute-start(bf16[128,256]{1,0:T(8,128)(2,1)S(1)} %select_convert_fusion.after_ref), channel_id=1, source_target_pairs={{0,1},{1,0},{2,3},{3,2},{4,5},{5,4},{6,7},{7,6},{8,9},{9,8},{10,11... | collective-permute-start | bytes 196616 | tf_op jit(solution)/shard_map/ppermute | solution.py:29
  7.8 0.0 copy-done.1
  7.8 0.0 copy-done.4
  7.8 0.0 copy-done.5
  7.8 0.0 copy-done.9
  7.8 1.5 %outgoing.1 = (bf16[1536,256]{1,0:T(8,128)(2,1)S(1)}, bf16[64,256]{1,0:T(8,128)(2,1)S(1)}) custom-call(s32[1,8]{1,0:T(1,128)S(1)} %copy-done.9, bf16[1536,256]{1,0:T(8,128)(2,1)S(1)} %get-tuple-element.13.grad_ref, bf16[256,256]{1,0:T(8,128)(2,1)S(1)} %copy-done.1, s32[8,4,8]{2,1,0:T(4,128)S(1)} %bitcast.31, f32[8,4,8]{2,1,0:T(4,128)S(1)} %bitcast.32, ...), custom_call_target="tpu_custom_call" | custom-call | tf_op jit(solution)/shard_map/outgoing/pallas_call | solution.py:307
  9.4 0.9 %collective-permute-done.1 = bf16[128,256]{1,0:T(8,128)(2,1)S(1)} collective-permute-done((bf16[128,256]{1,0:T(8,128)(2,1)S(1)}, bf16[128,256]{1,0:T(8,128)(2,1)S(1)}, u32[]{:S(2)}, u32[]{:S(2)}) %collective-permute-start.1) | collective-permute-done | bytes 65568 | tf_op jit(solution)/shard_map/ppermute | solution.py:29
  10.3 2.0 %collective-permute-start.2 = (bf16[160,256]{1,0:T(8,128)(2,1)S(1)}, bf16[160,256]{1,0:T(8,128)(2,1)S(1)}, u32[]{:S(2)}, u32[]{:S(2)}) collective-permute-start(bf16[160,256]{1,0:T(8,128)(2,1)S(1)} %pad_maximum_fusion.1), channel_id=1, source_target_pairs={{0,2},{1,3},{2,0},{3,1},{4,6},{5,7},{6,4},{7,5},{8,10},{9,11},{10,... | collective-permute-start | bytes 245768 | tf_op jit(solution)/shard_map/ppermute | solution.py:29
  13.6 0.0 copy-done.3
  13.6 0.0 copy-done.7
  13.6 0.0 copy-done.8
  13.6 0.3 %stale_rows.1 = (bf16[64,256]{1,0:T(8,128)(2,1)S(1)}, bf16[1,32,256]{2,1,0:T(8,128)(2,1)S(1)}) custom-call(s32[1]{0:T(128)S(6)} %copy.25.version_ref, s32[1]{0:T(128)S(6)} %copy.26.count_ref, bf16[2,64,256]{2,1,0:T(8,128)(2,1)S(1)} %bitcast.29, bf16[256,256]{1,0:T(8,128)(2,1)S(1)} %copy-done.1, ...), custom_call_target="tpu_custom_call", output_to_operand_aliasing={{1}: (6, {})} | custom-call | tf_op jit(solution)/shard_map/stale_rows/pallas_call | solution.py:330
  14.0 0.8 %collective-permute-done.2 = bf16[160,256]{1,0:T(8,128)(2,1)S(1)} collective-permute-done((bf16[160,256]{1,0:T(8,128)(2,1)S(1)}, bf16[160,256]{1,0:T(8,128)(2,1)S(1)}, u32[]{:S(2)}, u32[]{:S(2)}) %collective-permute-start.2) | collective-permute-done | bytes 81952 | tf_op jit(solution)/shard_map/ppermute | solution.py:29
  14.8 3.0 %collective-permute-start.3 = (bf16[160,256]{1,0:T(8,128)(2,1)S(1)}, bf16[160,256]{1,0:T(8,128)(2,1)S(1)}, u32[]{:S(2)}, u32[]{:S(2)}) collective-permute-start(bf16[160,256]{1,0:T(8,128)(2,1)S(1)} %pad_maximum_fusion.2), channel_id=1, source_target_pairs={{0,4},{1,5},{2,6},{3,7},{4,0},{5,1},{6,2},{7,3},{8,12},{9,13},{10,... | collective-permute-start | bytes 245768 | tf_op jit(solution)/shard_map/ppermute | solution.py:29
  17.9 0.0 copy-done
  17.9 0.0 copy-done.2
  17.9 0.0 copy-done.10
  17.9 0.0 copy-start.6
  17.9 0.0 copy-start.11
  17.9 2.0 %local_term.1 = (f32[12,128,256]{2,1,0:T(8,128)S(1)}, bf16[2,16,256]{2,1,0:T(8,128)(2,1)S(1)}) custom-call(s32[1,48]{1,0:T(1,128)S(1)} %copy-done.10, bf16[1536,256]{1,0:T(8,128)(2,1)S(1)} %get-tuple-element.13.grad_ref, bf16[1536,256]{1,0:T(8,128)(2,1)S(1)} %get-tuple-element.16.neigh_ref, ...), custom_call_target="tpu_custom_call", output_to_operand_aliasing={{1}: (5, {})} | custom-call | tf_op jit(solution)/shard_map/local_term/pallas_call | solution.py:351
  19.9 0.3 %collective-permute-done.3 = bf16[160,256]{1,0:T(8,128)(2,1)S(1)} collective-permute-done((bf16[160,256]{1,0:T(8,128)(2,1)S(1)}, bf16[160,256]{1,0:T(8,128)(2,1)S(1)}, u32[]{:S(2)}, u32[]{:S(2)}) %collective-permute-start.3) | collective-permute-done | bytes 81952 | tf_op jit(solution)/shard_map/ppermute | solution.py:29
  20.3 1.9 %collective-permute-start.4 = (bf16[160,256]{1,0:T(8,128)(2,1)S(1)}, bf16[160,256]{1,0:T(8,128)(2,1)S(1)}, u32[]{:S(2)}, u32[]{:S(2)}) collective-permute-start(bf16[160,256]{1,0:T(8,128)(2,1)S(1)} %pad_maximum_fusion.3), channel_id=1, source_target_pairs={{0,1},{1,0},{2,3},{3,2},{4,5},{5,4},{6,7},{7,6},{8,9},{9,8},{10,11... | collective-permute-start | bytes 245768 | tf_op jit(solution)/shard_map/ppermute | solution.py:29
  22.2 0.1 collective-permute-start.5
  22.3 2.5 %collective-permute-done.4 = bf16[160,256]{1,0:T(8,128)(2,1)S(1)} collective-permute-done((bf16[160,256]{1,0:T(8,128)(2,1)S(1)}, bf16[160,256]{1,0:T(8,128)(2,1)S(1)}, u32[]{:S(2)}, u32[]{:S(2)}) %collective-permute-start.4) | collective-permute-done | bytes 81952 | tf_op jit(solution)/shard_map/ppermute | solution.py:29
  24.8 0.0 collective-permute-start.6
  24.9 0.0 collective-permute-done.5
  24.9 0.0 copy-done.6
  24.9 0.0 copy-done.11
  24.9 1.2 %finish.1 = (bf16[1536,256]{1,0:T(8,128)(2,1)}, bf16[2,256,256]{2,1,0:T(8,128)(2,1)}) custom-call(f32[12,128,256]{2,1,0:T(8,128)S(1)} %get-tuple-element.19.base_ref, bf16[64,256]{1,0:T(8,128)(2,1)S(1)} %maximum_bitcast_fusion.fresh_ref, bf16[64,256]{1,0:T(8,128)(2,1)S(1)} %slice.77.stale_ref, s32[8,8]{1,0:T(8,128)S(1)} %bitcast.33, s32[1,64]{1,0:T(1,128)S(1)} %copy-done.11, ...), custom_call_target="tpu_custom_call" | custom-call | tf_op jit(solution)/shard_map/finish/pallas_call | solution.py:369
  26.1 0.0 collective-permute-done.6.last_ref
  26.2 0.7 %weight_grads.1 = bf16[2,256,256]{2,1,0:T(8,128)(2,1)} custom-call(bf16[128,256]{1,0:T(8,128)(2,1)S(1)} %collective-permute-done.6.last_ref, bf16[2,256,256]{2,1,0:T(8,128)(2,1)} %get-tuple-element.23.sums_in), custom_call_target="tpu_custom_call", output_to_operand_aliasing={{}: (1, {})} | custom-call | tf_op jit(solution)/shard_map/weight_grads/pallas_call | solution.py:390
  (19 shorter events, 0.2 us)
Async XLA Ops:
  3.4 1.5 %collective-permute-start = (bf16[256,256]{1,0:T(8,128)(2,1)S(1)}, bf16[256,256]{1,0:T(8,128)(2,1)S(1)}, u32[]{:S(2)}, u32[]{:S(2)}) collective-permute-start(bf16[256,256]{1,0:T(8,128)(2,1)S(1)} %get-tuple-element.15.after_ref), channel_id=1, source_target_pairs={{0,8},{8,0},{1,9},{9,1},{2,10},{10,2},{3,11},{11,3},{4,12},{12,4},... | collective-permute-start | bytes 393224 | tf_op jit(solution)/shard_map/ppermute | solution.py:29
  3.9 4.0 %copy-start.1 = (bf16[256,256]{1,0:T(8,128)(2,1)S(1)}, bf16[256,256]{1,0:T(8,128)(2,1)}, u32[]{:S(2)}) copy-start(bf16[256,256]{1,0:T(8,128)(2,1)} %weight_ref.4) | copy-start | bytes 393220
  3.9 4.0 %copy-start.4 = (s32[1,8,8,4]{2,3,1,0:T(4,128)S(1)}, s32[1,8,8,4]{2,3,1,0:T(4,128)}, u32[]{:S(2)}) copy-start(s32[1,8,8,4]{2,3,1,0:T(4,128)} %param.24) | copy-start | bytes 3076
  3.9 4.0 %copy-start.5 = (f32[1,8,8,4]{2,3,1,0:T(4,128)S(1)}, f32[1,8,8,4]{2,3,1,0:T(4,128)}, u32[]{:S(2)}) copy-start(f32[1,8,8,4]{2,3,1,0:T(4,128)} %param.25) | copy-start | bytes 3076
  3.9 4.0 %copy-start.9 = (s32[1,8]{1,0:T(1,128)S(1)}, s32[1,8]{1,0:T(1,128)}, u32[]{:S(2)}) copy-start(s32[1,8]{1,0:T(1,128)} %count_ref.2) | copy-start | bytes 100
  4.3 9.3 %copy-start.3 = (bf16[1,2,64,256]{3,2,1,0:T(8,128)(2,1)S(1)}, bf16[1,2,64,256]{3,2,1,0:T(8,128)(2,1)}, u32[]{:S(2)}) copy-start(bf16[1,2,64,256]{3,2,1,0:T(8,128)(2,1)} %param.28) | copy-start | bytes 196612
  4.3 9.3 %copy-start.7 = (s32[1,64,4]{1,2,0:T(4,128)S(1)}, s32[1,64,4]{1,2,0:T(4,128)}, u32[]{:S(2)}) copy-start(s32[1,64,4]{1,2,0:T(4,128)} %param.30) | copy-start | bytes 3076
  4.3 9.3 %copy-start.8 = (f32[1,64,4]{1,2,0:T(4,128)S(1)}, f32[1,64,4]{1,2,0:T(4,128)}, u32[]{:S(2)}) copy-start(f32[1,64,4]{1,2,0:T(4,128)} %param.31) | copy-start | bytes 3076
  4.3 13.5 %copy-start = (bf16[1,48,128,128]{3,2,1,0:T(8,128)(2,1)S(1)}, bf16[1,48,128,128]{3,2,1,0:T(8,128)(2,1)}, u32[]{:S(2)}) copy-start(bf16[1,48,128,128]{3,2,1,0:T(8,128)(2,1)} %param.22) | copy-start | bytes 4718596
  4.4 13.5 %copy-start.2 = (bf16[256,256]{1,0:T(8,128)(2,1)S(1)}, bf16[256,256]{1,0:T(8,128)(2,1)}, u32[]{:S(2)}) copy-start(bf16[256,256]{1,0:T(8,128)(2,1)} %weight_ref.5) | copy-start | bytes 393220
  4.4 13.5 %copy-start.10 = (s32[1,48]{1,0:T(1,128)S(1)}, s32[1,48]{1,0:T(1,128)}, u32[]{:S(2)}) copy-start(s32[1,48]{1,0:T(1,128)} %source_ref.1) | copy-start | bytes 580
  4.9 5.3 %collective-permute-start.1 = (bf16[128,256]{1,0:T(8,128)(2,1)S(1)}, bf16[128,256]{1,0:T(8,128)(2,1)S(1)}, u32[]{:S(2)}, u32[]{:S(2)}) collective-permute-start(bf16[128,256]{1,0:T(8,128)(2,1)S(1)} %select_convert_fusion.after_ref), channel_id=1, source_target_pairs={{0,1},{1,0},{2,3},{3,2},{4,5},{5,4},{6,7},{7,6},{8,9},{9,8},{10,11... | collective-permute-start | bytes 196616 | tf_op jit(solution)/shard_map/ppermute | solution.py:29
  10.3 4.5 %collective-permute-start.2 = (bf16[160,256]{1,0:T(8,128)(2,1)S(1)}, bf16[160,256]{1,0:T(8,128)(2,1)S(1)}, u32[]{:S(2)}, u32[]{:S(2)}) collective-permute-start(bf16[160,256]{1,0:T(8,128)(2,1)S(1)} %pad_maximum_fusion.1), channel_id=1, source_target_pairs={{0,2},{1,3},{2,0},{3,1},{4,6},{5,7},{6,4},{7,5},{8,10},{9,11},{10,... | collective-permute-start | bytes 245768 | tf_op jit(solution)/shard_map/ppermute | solution.py:29
  14.8 5.4 %collective-permute-start.3 = (bf16[160,256]{1,0:T(8,128)(2,1)S(1)}, bf16[160,256]{1,0:T(8,128)(2,1)S(1)}, u32[]{:S(2)}, u32[]{:S(2)}) collective-permute-start(bf16[160,256]{1,0:T(8,128)(2,1)S(1)} %pad_maximum_fusion.2), channel_id=1, source_target_pairs={{0,4},{1,5},{2,6},{3,7},{4,0},{5,1},{6,2},{7,3},{8,12},{9,13},{10,... | collective-permute-start | bytes 245768 | tf_op jit(solution)/shard_map/ppermute | solution.py:29
  17.9 7.1 %copy-start.6 = (s32[1,8,8]{2,1,0:T(8,128)S(1)}, s32[1,8,8]{2,1,0:T(8,128)}, u32[]{:S(2)}) copy-start(s32[1,8,8]{2,1,0:T(8,128)} %param.27) | copy-start | bytes 772
  17.9 7.1 %copy-start.11 = (s32[1,64]{1,0:T(1,128)S(1)}, s32[1,64]{1,0:T(1,128)}, u32[]{:S(2)}) copy-start(s32[1,64]{1,0:T(1,128)} %cross_ref.1) | copy-start | bytes 772
  20.3 4.5 %collective-permute-start.4 = (bf16[160,256]{1,0:T(8,128)(2,1)S(1)}, bf16[160,256]{1,0:T(8,128)(2,1)S(1)}, u32[]{:S(2)}, u32[]{:S(2)}) collective-permute-start(bf16[160,256]{1,0:T(8,128)(2,1)S(1)} %pad_maximum_fusion.3), channel_id=1, source_target_pairs={{0,1},{1,0},{2,3},{3,2},{4,5},{5,4},{6,7},{7,6},{8,9},{9,8},{10,11... | collective-permute-start | bytes 245768 | tf_op jit(solution)/shard_map/ppermute | solution.py:29
  22.2 2.7 %collective-permute-start.5 = (bf16[192,256]{1,0:T(8,128)(2,1)S(1)}, bf16[192,256]{1,0:T(8,128)(2,1)S(1)}, u32[]{:S(2)}, u32[]{:S(2)}) collective-permute-start(bf16[192,256]{1,0:T(8,128)(2,1)S(1)} %pad_maximum_fusion), channel_id=1, source_target_pairs={{0,8},{8,0},{1,9},{9,1},{2,10},{10,2},{3,11},{11,3},{4,12},{12,4},... | collective-permute-start | bytes 294920 | tf_op jit(solution)/shard_map/ppermute | solution.py:29
  24.8 1.3 %collective-permute-start.6 = (bf16[128,256]{1,0:T(8,128)(2,1)S(1)}, bf16[128,256]{1,0:T(8,128)(2,1)S(1)}, u32[]{:S(2)}, u32[]{:S(2)}) collective-permute-start(bf16[128,256]{1,0:T(8,128)(2,1)S(1)} %slice.78.across_ref), channel_id=1, source_target_pairs={{0,8},{8,0},{1,9},{9,1},{2,10},{10,2},{3,11},{11,3},{4,12},{12,4},... | collective-permute-start | bytes 196616 | tf_op jit(solution)/shard_map/ppermute | solution.py:29

commit v7 on v5

--- a/solution.py
+++ b/solution.py
@@ -166,8 +166,11 @@
     neigh_ref,
     weight_ref,
     tile_ref,
+    recv_ref,
+    cross_ref,
     stay_ref,
     base_ref,
+    hit_ref,
     same_ref,
 ):
     blocks = base_ref.shape[0]
@@ -183,6 +186,12 @@
         for t in range(b * per_block, (b + 1) * per_block):
             product = lax.dot_general(tile_ref[t], neigh, TN, preferred_element_type=F32)
             base_ref[source_ref[0, t]] += product
+    me = lax.axis_index("dom")
+    targets = [recv_ref[pl.ds(jnp.bitwise_xor(me, o), 1), :] for o in hop_order(recv_ref.shape[0])]
+    targets = jnp.concatenate(targets + [cross_ref[...]], axis=1)
+    for b in range(blocks):
+        node = b * 128 + lax.broadcasted_iota(jnp.int32, (128, targets.shape[1]), 0)
+        hit_ref[pl.ds(b * 128, 128), :] = jnp.where(node == targets, 1.0, 0.0).astype(BF16)
 
 
 def quarters(size):
@@ -194,8 +203,7 @@
     base_ref,
     fresh_ref,
     stale_ref,
-    recv_ref,
-    cross_ref,
+    hit_ref,
     own_ref,
     across_ref,
     host_ref,
@@ -204,11 +212,7 @@
     out,
     sems,
 ):
-    me = lax.axis_index("dom")
     blocks = base_ref.shape[0]
-    peers, cap = recv_ref.shape
-    targets = [recv_ref[pl.ds(jnp.bitwise_xor(me, o), 1), :] for o in hop_order(peers)]
-    targets = jnp.concatenate(targets + [cross_ref[...]], axis=1)
     values = jnp.concatenate([fresh_ref[...], stale_ref[...]], axis=0)
     host = lax.axis_index("hst")
     here, there = quarters(own_ref.shape[0])
@@ -220,8 +224,7 @@
     for copy in copies:
         copy.start()
     for b in range(blocks):
-        node = b * 128 + lax.broadcasted_iota(jnp.int32, (128, targets.shape[1]), 0)
-        hit = jnp.where(node == targets, 1.0, 0.0).astype(BF16)
+        hit = hit_ref[pl.ds(b * 128, 128), :]
         total = base_ref[b] + jnp.dot(hit, values, preferred_element_type=F32)
         out[pl.ds(b * 128, 128), :] = total.astype(BF16)
         if (b + 1) % OUT_BLOCKS == 0 or b + 1 == blocks:
@@ -348,18 +351,28 @@
                 stay,
             )
         if step == 1:
-            base, stay = pl.pallas_call(
+            base, hit, stay = pl.pallas_call(
                 local_kernel,
                 out_shape=(
                     struct((blocks, 128, dim), F32),
+                    struct((row_count, peers * cap + cross_rows.shape[1]), BF16),
                     struct(stay.shape, stay.dtype),
                 ),
-                in_specs=[SMEM, VMEM, VMEM, VMEM, VMEM, ANY],
-                out_specs=(VMEM, ANY),
-                input_output_aliases={5: 1},
+                in_specs=[SMEM, VMEM, VMEM, VMEM, VMEM, VMEM, VMEM, ANY],
+                out_specs=(VMEM, VMEM, ANY),
+                input_output_aliases={7: 2},
                 compiler_params=PARAMS,
                 name="local_term",
-            )(tile_source, pre_grad, neigh_grad, w_self, tile_values[0], stay)
+            )(
+                tile_source,
+                pre_grad,
+                neigh_grad,
+                w_self,
+                tile_values[0],
+                recv_rows[0],
+                cross_rows,
+                stay,
+            )
         other = arrived[:quarter]
         kept = given.astype(F32) + other.astype(F32)
         held = jnp.stack([stay, arrived[quarter:].reshape(stay.shape)], axis=1)
@@ -370,7 +383,7 @@
     out_rows, sums = pl.pallas_call(
         finish_kernel,
         out_shape=(struct((row_count, dim), BF16), struct((2, dim, dim), BF16)),
-        in_specs=[VMEM] * 8,
+        in_specs=[VMEM] * 7,
         out_specs=(ANY, ANY),
         scratch_shapes=[
             pltpu.VMEM((row_count, dim), BF16),
@@ -382,8 +395,7 @@
         base,
         held.reshape(peers * cap, dim),
         stale_in,
-        recv_rows[0],
-        cross_rows,
+        hit,
         given,
         other,
         early[:quarter],

time: 27.3 us -> 27.2 us (level)
  transfers between devices with their start and end apart: 7 -> 7, of which waited for: 5 -> 5; matrix products, arithmetic and copies ran while one was open for 0% -> 0% of each run, Pallas kernels for 20% -> 21%
where the time goes in v7:
time: 27.2 us; the launch traced here: 26.8 us
  starting transfers between devices  10.4 us (38%)
  Pallas kernels  8.9 us (33%)
  waiting for transfers between devices  4.94 us (18%)
  between operations  2.24 us (8%)
    ppermute x7, starting transfers between devices, swap(): return lax.ppermute(value, axis, pairs)  10.4 us
    ppermute x7, waiting for transfers between devices, swap(): return lax.ppermute(value, axis, pairs)  4.94 us
    pallas_call x1, Pallas kernels, body(): pl.pallas_call(gradient_kernel, out_shape=(pltpu.VMEM((2, row_count, dim)...  2.71 us
    pallas_call x1, Pallas kernels, body(): pl.pallas_call(local_kernel, out_shape=(struct((blocks, 128, dim), F32),...  2.13 us
    pallas_call x1, Pallas kernels, body(): pl.pallas_call(outgoing_kernel, out_shape=(struct((row_count, dim), BF16)...  1.52 us
    pallas_call x1, Pallas kernels, body(): pl.pallas_call(finish_kernel, out_shape=(struct((row_count, dim), BF16),...  1.14 us
    pallas_call x1, Pallas kernels, body(): pl.pallas_call(last_kernel, out_shape=struct((2, dim, dim), BF16), in_spe...  0.64 us
  transfers between devices with their start and end apart: 7, of which 5 were waited for; matrix products, arithmetic and copies ran while one was open for 0% of the time, Pallas kernels for 21%

profile of v7, /device:TPU:0, one launch (start us, length us, event | category | flops | bytes accessed | tf_op | source)
XLA Modules:
  0.0 26.8 jit_solution(9879920714396172190)
XLA Ops:
  0.6 2.7 %gradients.1 = (bf16[2,1536,256]{2,1,0:T(8,128)(2,1)S(1)}, bf16[1536,256]{1,0:T(8,128)(2,1)S(1)}, bf16[256,256]{1,0:T(8,128)(2,1)S(1)}) custom-call(bf16[1536,256]{1,0:T(8,128)(2,1)} %features_hbm.1, bf16[1536,256]{1,0:T(8,128)(2,1)} %aggregated_hbm.1, bf16[1536,256]{1,0:T(8,128)(2,1)} %cotangent_hbm.1, bf16[256,256]{1,0:T(8,128)(2,1)} %weight_ref.5, ...), custom_call_target="tpu_custom_call" | custom-call | tf_op jit(solution)/shard_map/gradients/pallas_call | solution.py:276
  3.4 0.5 %collective-permute-start = (bf16[256,256]{1,0:T(8,128)(2,1)S(1)}, bf16[256,256]{1,0:T(8,128)(2,1)S(1)}, u32[]{:S(2)}, u32[]{:S(2)}) collective-permute-start(bf16[256,256]{1,0:T(8,128)(2,1)S(1)} %get-tuple-element.16.after_ref), channel_id=1, source_target_pairs={{0,8},{8,0},{1,9},{9,1},{2,10},{10,2},{3,11},{11,3},{4,12},{12,4},... | collective-permute-start | bytes 393224 | tf_op jit(solution)/shard_map/ppermute | solution.py:29
  3.9 0.0 copy-start.1
  3.9 0.0 copy-start.4
  3.9 0.0 copy-start.5
  3.9 0.0 copy-start.9
  3.9 0.4 %kept_sum.1 = f32[256,256]{1,0:T(8,128)S(1)} custom-call(bf16[2,1536,256]{2,1,0:T(8,128)(2,1)S(1)} %get-tuple-element.15.inputs_ref, bf16[1536,256]{1,0:T(8,128)(2,1)S(1)} %get-tuple-element.14.grad_ref, bf16[256,256]{1,0:T(8,128)(2,1)S(1)} %get-tuple-element.16.after_ref), custom_call_target="tpu_custom_call" | custom-call | tf_op jit(solution)/shard_map/kept_sum/pallas_call | solution.py:295
  4.3 0.0 copy-start.3
  4.3 0.0 copy-start.7
  4.3 0.0 copy-start.8
  4.3 0.0 copy-start
  4.4 0.0 copy-start.2
  4.4 0.0 copy-start.6
  4.4 0.0 copy-start.10
  4.4 0.0 copy-start.11
  4.4 0.4 %collective-permute-done = bf16[256,256]{1,0:T(8,128)(2,1)S(1)} collective-permute-done((bf16[256,256]{1,0:T(8,128)(2,1)S(1)}, bf16[256,256]{1,0:T(8,128)(2,1)S(1)}, u32[]{:S(2)}, u32[]{:S(2)}) %collective-permute-start) | collective-permute-done | bytes 131104 | tf_op jit(solution)/shard_map/ppermute | solution.py:29
  4.9 2.9 %collective-permute-start.1 = (bf16[128,256]{1,0:T(8,128)(2,1)S(1)}, bf16[128,256]{1,0:T(8,128)(2,1)S(1)}, u32[]{:S(2)}, u32[]{:S(2)}) collective-permute-start(bf16[128,256]{1,0:T(8,128)(2,1)S(1)} %select_convert_fusion.after_ref), channel_id=1, source_target_pairs={{0,1},{1,0},{2,3},{3,2},{4,5},{5,4},{6,7},{7,6},{8,9},{9,8},{10,11... | collective-permute-start | bytes 196616 | tf_op jit(solution)/shard_map/ppermute | solution.py:29
  7.8 0.0 copy-done.1
  7.8 0.0 copy-done.4
  7.8 0.0 copy-done.5
  7.8 0.0 copy-done.9
  7.8 1.5 %outgoing.1 = (bf16[1536,256]{1,0:T(8,128)(2,1)S(1)}, bf16[64,256]{1,0:T(8,128)(2,1)S(1)}) custom-call(s32[1,8]{1,0:T(1,128)S(1)} %copy-done.9, bf16[1536,256]{1,0:T(8,128)(2,1)S(1)} %get-tuple-element.14.grad_ref, bf16[256,256]{1,0:T(8,128)(2,1)S(1)} %copy-done.1, s32[8,4,8]{2,1,0:T(4,128)S(1)} %bitcast.40, f32[8,4,8]{2,1,0:T(4,128)S(1)} %bitcast.41, ...), custom_call_target="tpu_custom_call" | custom-call | tf_op jit(solution)/shard_map/outgoing/pallas_call | solution.py:310
  9.4 0.9 %collective-permute-done.1 = bf16[128,256]{1,0:T(8,128)(2,1)S(1)} collective-permute-done((bf16[128,256]{1,0:T(8,128)(2,1)S(1)}, bf16[128,256]{1,0:T(8,128)(2,1)S(1)}, u32[]{:S(2)}, u32[]{:S(2)}) %collective-permute-start.1) | collective-permute-done | bytes 65568 | tf_op jit(solution)/shard_map/ppermute | solution.py:29
  10.3 2.0 %collective-permute-start.2 = (bf16[160,256]{1,0:T(8,128)(2,1)S(1)}, bf16[160,256]{1,0:T(8,128)(2,1)S(1)}, u32[]{:S(2)}, u32[]{:S(2)}) collective-permute-start(bf16[160,256]{1,0:T(8,128)(2,1)S(1)} %pad_maximum_fusion.1), channel_id=1, source_target_pairs={{0,2},{1,3},{2,0},{3,1},{4,6},{5,7},{6,4},{7,5},{8,10},{9,11},{10,... | collective-permute-start | bytes 245768 | tf_op jit(solution)/shard_map/ppermute | solution.py:29
  13.6 0.0 copy-done.3
  13.6 0.0 copy-done.7
  13.6 0.0 copy-done.8
  13.6 0.3 %stale_rows.1 = (bf16[64,256]{1,0:T(8,128)(2,1)S(1)}, bf16[1,32,256]{2,1,0:T(8,128)(2,1)S(1)}) custom-call(s32[1]{0:T(128)S(6)} %copy.28.version_ref, s32[1]{0:T(128)S(6)} %copy.29.count_ref, bf16[2,64,256]{2,1,0:T(8,128)(2,1)S(1)} %bitcast.38, bf16[256,256]{1,0:T(8,128)(2,1)S(1)} %copy-done.1, ...), custom_call_target="tpu_custom_call", output_to_operand_aliasing={{1}: (6, {})} | custom-call | tf_op jit(solution)/shard_map/stale_rows/pallas_call | solution.py:333
  14.0 0.8 %collective-permute-done.2 = bf16[160,256]{1,0:T(8,128)(2,1)S(1)} collective-permute-done((bf16[160,256]{1,0:T(8,128)(2,1)S(1)}, bf16[160,256]{1,0:T(8,128)(2,1)S(1)}, u32[]{:S(2)}, u32[]{:S(2)}) %collective-permute-start.2) | collective-permute-done | bytes 81952 | tf_op jit(solution)/shard_map/ppermute | solution.py:29
  14.8 3.0 %collective-permute-start.3 = (bf16[160,256]{1,0:T(8,128)(2,1)S(1)}, bf16[160,256]{1,0:T(8,128)(2,1)S(1)}, u32[]{:S(2)}, u32[]{:S(2)}) collective-permute-start(bf16[160,256]{1,0:T(8,128)(2,1)S(1)} %pad_maximum_fusion.2), channel_id=1, source_target_pairs={{0,4},{1,5},{2,6},{3,7},{4,0},{5,1},{6,2},{7,3},{8,12},{9,13},{10,... | collective-permute-start | bytes 245768 | tf_op jit(solution)/shard_map/ppermute | solution.py:29
  17.9 0.0 copy-done
  17.9 0.0 copy-done.2
  17.9 0.0 copy-done.6
  17.9 0.0 copy-done.10
  17.9 0.0 copy-done.11
  17.9 2.1 %local_term.1 = (f32[12,128,256]{2,1,0:T(8,128)S(1)}, bf16[1536,128]{1,0:T(8,128)(2,1)S(1)}, bf16[2,16,256]{2,1,0:T(8,128)(2,1)S(1)}) custom-call(s32[1,48]{1,0:T(1,128)S(1)} %copy-done.10, bf16[1536,256]{1,0:T(8,128)(2,1)S(1)} %get-tuple-element.14.grad_ref, bf16[1536,256]{1,0:T(8,128)(2,1)S(1)} %get-tuple-element.17.neigh_ref, ...), custom_call_target="tpu_custom_call", output_to_operand_aliasing={{2}: (7, {})} | custom-call | tf_op jit(solution)/shard_map/local_term/pallas_call | solution.py:354
  20.0 0.3 collective-permute-done.3
  20.4 1.9 %collective-permute-start.4 = (bf16[160,256]{1,0:T(8,128)(2,1)S(1)}, bf16[160,256]{1,0:T(8,128)(2,1)S(1)}, u32[]{:S(2)}, u32[]{:S(2)}) collective-permute-start(bf16[160,256]{1,0:T(8,128)(2,1)S(1)} %pad_maximum_fusion.3), channel_id=1, source_target_pairs={{0,1},{1,0},{2,3},{3,2},{4,5},{5,4},{6,7},{7,6},{8,9},{9,8},{10,11... | collective-permute-start | bytes 245768 | tf_op jit(solution)/shard_map/ppermute | solution.py:29
  22.3 0.1 collective-permute-start.5
  22.3 2.5 %collective-permute-done.4 = bf16[160,256]{1,0:T(8,128)(2,1)S(1)} collective-permute-done((bf16[160,256]{1,0:T(8,128)(2,1)S(1)}, bf16[160,256]{1,0:T(8,128)(2,1)S(1)}, u32[]{:S(2)}, u32[]{:S(2)}) %collective-permute-start.4) | collective-permute-done | bytes 81952 | tf_op jit(solution)/shard_map/ppermute | solution.py:29
  24.9 0.0 collective-permute-start.6
  24.9 0.0 collective-permute-done.5
  25.0 1.1 %finish.1 = (bf16[1536,256]{1,0:T(8,128)(2,1)}, bf16[2,256,256]{2,1,0:T(8,128)(2,1)}) custom-call(f32[12,128,256]{2,1,0:T(8,128)S(1)} %get-tuple-element.20.base_ref, bf16[64,256]{1,0:T(8,128)(2,1)S(1)} %bitcast.37, bf16[64,256]{1,0:T(8,128)(2,1)S(1)} %slice.77.stale_ref, bf16[1536,128]{1,0:T(8,128)(2,1)S(1)} %get-tuple-element.23.hit_ref, ...), custom_call_target="tpu_custom_call" | custom-call | tf_op jit(solution)/shard_map/finish/pallas_call | solution.py:383
  26.1 0.0 collective-permute-done.6.last_ref
  26.1 0.6 %weight_grads.1 = bf16[2,256,256]{2,1,0:T(8,128)(2,1)} custom-call(bf16[128,256]{1,0:T(8,128)(2,1)S(1)} %collective-permute-done.6.last_ref, bf16[2,256,256]{2,1,0:T(8,128)(2,1)} %get-tuple-element.25.sums_in), custom_call_target="tpu_custom_call", output_to_operand_aliasing={{}: (1, {})} | custom-call | tf_op jit(solution)/shard_map/weight_grads/pallas_call | solution.py:403
  (23 shorter events, 0.2 us)
Async XLA Ops:
  3.4 1.5 %collective-permute-start = (bf16[256,256]{1,0:T(8,128)(2,1)S(1)}, bf16[256,256]{1,0:T(8,128)(2,1)S(1)}, u32[]{:S(2)}, u32[]{:S(2)}) collective-permute-start(bf16[256,256]{1,0:T(8,128)(2,1)S(1)} %get-tuple-element.16.after_ref), channel_id=1, source_target_pairs={{0,8},{8,0},{1,9},{9,1},{2,10},{10,2},{3,11},{11,3},{4,12},{12,4},... | collective-permute-start | bytes 393224 | tf_op jit(solution)/shard_map/ppermute | solution.py:29
  3.9 4.0 %copy-start.1 = (bf16[256,256]{1,0:T(8,128)(2,1)S(1)}, bf16[256,256]{1,0:T(8,128)(2,1)}, u32[]{:S(2)}) copy-start(bf16[256,256]{1,0:T(8,128)(2,1)} %weight_ref.4) | copy-start | bytes 393220
  3.9 4.0 %copy-start.4 = (s32[1,8,8,4]{2,3,1,0:T(4,128)S(1)}, s32[1,8,8,4]{2,3,1,0:T(4,128)}, u32[]{:S(2)}) copy-start(s32[1,8,8,4]{2,3,1,0:T(4,128)} %param.24) | copy-start | bytes 3076
  3.9 4.0 %copy-start.5 = (f32[1,8,8,4]{2,3,1,0:T(4,128)S(1)}, f32[1,8,8,4]{2,3,1,0:T(4,128)}, u32[]{:S(2)}) copy-start(f32[1,8,8,4]{2,3,1,0:T(4,128)} %param.25) | copy-start | bytes 3076
  3.9 4.0 %copy-start.9 = (s32[1,8]{1,0:T(1,128)S(1)}, s32[1,8]{1,0:T(1,128)}, u32[]{:S(2)}) copy-start(s32[1,8]{1,0:T(1,128)} %count_ref.2) | copy-start | bytes 100
  4.3 9.3 %copy-start.3 = (bf16[1,2,64,256]{3,2,1,0:T(8,128)(2,1)S(1)}, bf16[1,2,64,256]{3,2,1,0:T(8,128)(2,1)}, u32[]{:S(2)}) copy-start(bf16[1,2,64,256]{3,2,1,0:T(8,128)(2,1)} %param.28) | copy-start | bytes 196612
  4.3 9.3 %copy-start.7 = (s32[1,64,4]{1,2,0:T(4,128)S(1)}, s32[1,64,4]{1,2,0:T(4,128)}, u32[]{:S(2)}) copy-start(s32[1,64,4]{1,2,0:T(4,128)} %param.30) | copy-start | bytes 3076
  4.3 9.3 %copy-start.8 = (f32[1,64,4]{1,2,0:T(4,128)S(1)}, f32[1,64,4]{1,2,0:T(4,128)}, u32[]{:S(2)}) copy-start(f32[1,64,4]{1,2,0:T(4,128)} %param.31) | copy-start | bytes 3076
  4.3 13.5 %copy-start = (bf16[1,48,128,128]{3,2,1,0:T(8,128)(2,1)S(1)}, bf16[1,48,128,128]{3,2,1,0:T(8,128)(2,1)}, u32[]{:S(2)}) copy-start(bf16[1,48,128,128]{3,2,1,0:T(8,128)(2,1)} %param.22) | copy-start | bytes 4718596
  4.4 13.5 %copy-start.2 = (bf16[256,256]{1,0:T(8,128)(2,1)S(1)}, bf16[256,256]{1,0:T(8,128)(2,1)}, u32[]{:S(2)}) copy-start(bf16[256,256]{1,0:T(8,128)(2,1)} %weight_ref.5) | copy-start | bytes 393220
  4.4 13.5 %copy-start.6 = (s32[1,8,8]{2,1,0:T(8,128)S(1)}, s32[1,8,8]{2,1,0:T(8,128)}, u32[]{:S(2)}) copy-start(s32[1,8,8]{2,1,0:T(8,128)} %param.27) | copy-start | bytes 772
  4.4 13.5 %copy-start.10 = (s32[1,48]{1,0:T(1,128)S(1)}, s32[1,48]{1,0:T(1,128)}, u32[]{:S(2)}) copy-start(s32[1,48]{1,0:T(1,128)} %source_ref.1) | copy-start | bytes 580
  4.4 13.5 %copy-start.11 = (s32[1,64]{1,0:T(1,128)S(1)}, s32[1,64]{1,0:T(1,128)}, u32[]{:S(2)}) copy-start(s32[1,64]{1,0:T(1,128)} %cross_ref.1) | copy-start | bytes 772
  4.9 5.3 %collective-permute-start.1 = (bf16[128,256]{1,0:T(8,128)(2,1)S(1)}, bf16[128,256]{1,0:T(8,128)(2,1)S(1)}, u32[]{:S(2)}, u32[]{:S(2)}) collective-permute-start(bf16[128,256]{1,0:T(8,128)(2,1)S(1)} %select_convert_fusion.after_ref), channel_id=1, source_target_pairs={{0,1},{1,0},{2,3},{3,2},{4,5},{5,4},{6,7},{7,6},{8,9},{9,8},{10,11... | collective-permute-start | bytes 196616 | tf_op jit(solution)/shard_map/ppermute | solution.py:29
  10.3 4.5 %collective-permute-start.2 = (bf16[160,256]{1,0:T(8,128)(2,1)S(1)}, bf16[160,256]{1,0:T(8,128)(2,1)S(1)}, u32[]{:S(2)}, u32[]{:S(2)}) collective-permute-start(bf16[160,256]{1,0:T(8,128)(2,1)S(1)} %pad_maximum_fusion.1), channel_id=1, source_target_pairs={{0,2},{1,3},{2,0},{3,1},{4,6},{5,7},{6,4},{7,5},{8,10},{9,11},{10,... | collective-permute-start | bytes 245768 | tf_op jit(solution)/shard_map/ppermute | solution.py:29
  14.8 5.4 %collective-permute-start.3 = (bf16[160,256]{1,0:T(8,128)(2,1)S(1)}, bf16[160,256]{1,0:T(8,128)(2,1)S(1)}, u32[]{:S(2)}, u32[]{:S(2)}) collective-permute-start(bf16[160,256]{1,0:T(8,128)(2,1)S(1)} %pad_maximum_fusion.2), channel_id=1, source_target_pairs={{0,4},{1,5},{2,6},{3,7},{4,0},{5,1},{6,2},{7,3},{8,12},{9,13},{10,... | collective-permute-start | bytes 245768 | tf_op jit(solution)/shard_map/ppermute | solution.py:29
  20.4 4.5 %collective-permute-start.4 = (bf16[160,256]{1,0:T(8,128)(2,1)S(1)}, bf16[160,256]{1,0:T(8,128)(2,1)S(1)}, u32[]{:S(2)}, u32[]{:S(2)}) collective-permute-start(bf16[160,256]{1,0:T(8,128)(2,1)S(1)} %pad_maximum_fusion.3), channel_id=1, source_target_pairs={{0,1},{1,0},{2,3},{3,2},{4,5},{5,4},{6,7},{7,6},{8,9},{9,8},{10,11... | collective-permute-start | bytes 245768 | tf_op jit(solution)/shard_map/ppermute | solution.py:29
  22.3 2.7 %collective-permute-start.5 = (bf16[192,256]{1,0:T(8,128)(2,1)S(1)}, bf16[192,256]{1,0:T(8,128)(2,1)S(1)}, u32[]{:S(2)}, u32[]{:S(2)}) collective-permute-start(bf16[192,256]{1,0:T(8,128)(2,1)S(1)} %pad_maximum_fusion), channel_id=1, source_target_pairs={{0,8},{8,0},{1,9},{9,1},{2,10},{10,2},{3,11},{11,3},{4,12},{12,4},... | collective-permute-start | bytes 294920 | tf_op jit(solution)/shard_map/ppermute | solution.py:29
  24.9 1.3 %collective-permute-start.6 = (bf16[128,256]{1,0:T(8,128)(2,1)S(1)}, bf16[128,256]{1,0:T(8,128)(2,1)S(1)}, u32[]{:S(2)}, u32[]{:S(2)}) collective-permute-start(bf16[128,256]{1,0:T(8,128)(2,1)S(1)} %slice.78.across_ref), channel_id=1, source_target_pairs={{0,8},{8,0},{1,9},{9,1},{2,10},{10,2},{3,11},{11,3},{4,12},{12,4},... | collective-permute-start | bytes 196616 | tf_op jit(solution)/shard_map/ppermute | solution.py:29
